TPU v7x, 32 devices: a whole 2x2x4 slice. The times are simulated.
32 devices in a mesh: groups: 2 (over y), dp: 4 (over z), expert: 4 (over x, core).
Axes of the slice: x: 2, y: 2, z: 4, core: 2. Of those that a mesh axis runs over, the one named last changes fastest.
Arguments:
- tokens: bfloat16 [4096, 4096], P(('groups', 'dp', 'expert')), parts along dimension 0, may hold values from -6 to 6
- assign: int32 [4096, 8], P(('groups', 'dp', 'expert')), parts along dimension 0, may hold values from 0 to 127, all different within a row
- probs: float32 [4096, 8], P(('groups', 'dp', 'expert')), parts along dimension 0, may hold values from 0.1 to 1
- expert_weights: bfloat16 [4, 3, 768, 4096], P('dp', None, 'expert'), may hold values from -4 to 4
Outputs:
- mixed: bfloat16 [4096, 4096], P(('groups', 'dp', 'expert')), parts along dimension 0
There are 2 independent parts, one for each index of `groups`. A program takes and returns all parts, laid end to end along the dimension named above; an argument that names none is the same for every part. Nothing has to cross between parts.
All inputs are finite; a program needn't handle non-finite values.
Results may differ from a plain program's by a relative error of at most 0.0058.
Values may be sent and summed in bfloat16 or wider, within the bound.
No kernel may reach another device: no remote copies, remote signals or barrier semaphores. Data moves between devices by JAX's collectives and lax.ppermute only.
A program may use at most 128 MiB of HBM per device.

v0:
```python
import jax
import jax.numpy as jnp
from jax import lax
from jax.sharding import PartitionSpec as P


def from_behind(block, axis, distance):
    devices = range(lax.axis_size(axis))
    route = [((i - distance) % len(devices), i) for i in devices]
    return lax.ppermute(block, axis, route)


def routing_slots(assign_block, experts_here, capacity):
    copies = assign_block.shape[0] * assign_block.shape[1]
    flat_ids = assign_block.reshape(copies)
    labels = jnp.arange(experts_here, dtype=jnp.int32)
    onehot_table = (flat_ids[:, None] == labels[None, :]).astype(jnp.int32)
    earlier = jnp.cumsum(onehot_table, axis=0, dtype=jnp.int32) - onehot_table
    position = jnp.sum(earlier * onehot_table, axis=1, dtype=jnp.int32)
    inside = jnp.sum(onehot_table, axis=1, dtype=jnp.int32)
    kept_mask = (inside > 0) & (position < capacity)
    dump_slot = experts_here * capacity
    slot_of = jnp.where(kept_mask, flat_ids * capacity + position, dump_slot)
    owner_token = jnp.arange(copies, dtype=jnp.int32) // assign_block.shape[1]
    slot_token = jnp.zeros((dump_slot + 1,), jnp.int32).at[slot_of].set(owner_token)[:dump_slot]
    filled = (
        jnp.zeros((dump_slot + 1,), jnp.int32)
        .at[slot_of]
        .set(jnp.ones_like(owner_token))[:dump_slot]
    )
    return (
        slot_of.reshape(assign_block.shape),
        kept_mask.reshape(assign_block.shape),
        slot_token,
        filled,
    )


def dispatch_rows(tok_rows, slot_token, filled):
    picked = jnp.take(tok_rows, slot_token, axis=0)
    return jnp.where(filled[:, None] > 0, picked, jnp.zeros_like(picked))


def combine_copies(returned, slot_of, kept_mask, weights):
    limit = returned.shape[0] - 1
    total = jnp.zeros((slot_of.shape[0], returned.shape[1]), jnp.float32)
    for rank in range(slot_of.shape[1]):
        picked = jnp.take(returned, jnp.minimum(slot_of[:, rank], limit), axis=0).astype(
            jnp.float32
        )
        factor = jnp.where(kept_mask[:, rank], weights[:, rank], jnp.zeros_like(weights[:, rank]))
        total = total + factor[:, None] * picked
    return total.astype(jnp.bfloat16)


def hidden_part(rows_in, slab):
    both = jnp.einsum("rd,kfd->krf", rows_in, slab[:2], preferred_element_type=jnp.float32)
    return (jax.nn.silu(both[0]) * both[1]).astype(jnp.bfloat16)


def local(tokens, assign, probs, expert_weights):
    experts_here = lax.axis_size("dp")
    capacity = tokens.shape[0] // 8
    width = tokens.shape[1]
    slot_of, kept_mask, slot_token, filled = routing_slots(assign, experts_here, capacity)
    outgoing = dispatch_rows(tokens, slot_token, filled).reshape(experts_here, capacity, width)
    arrived = lax.all_to_all(outgoing, "dp", split_axis=0, concat_axis=0, tiled=True)
    live_rows = arrived.reshape(experts_here * capacity, width)
    own_slab = expert_weights[0]
    hops_total = lax.axis_size("expert")
    hidden_pieces = []
    down_pieces = []
    travelling = own_slab
    for rounds in range(hops_total):
        hidden_pieces.append(hidden_part(live_rows, travelling))
        down_pieces.append(travelling[2])
        if rounds + 1 < hops_total:
            travelling = from_behind(travelling, "expert", 1)
    hidden_all = jnp.concatenate(hidden_pieces, axis=1)
    down_all = jnp.concatenate(down_pieces, axis=0)
    summed = jnp.dot(hidden_all, down_all, preferred_element_type=jnp.float32)
    results = summed.astype(jnp.bfloat16).reshape(experts_here, capacity, width)
    returned = lax.all_to_all(results, "dp", split_axis=0, concat_axis=0, tiled=True)
    return combine_copies(
        returned.reshape(experts_here * capacity, width), slot_of, kept_mask, probs
    )


def solution(mesh):
    placed = (
        P(("groups", "dp", "expert"), None),
        P(("groups", "dp", "expert"), None),
        P(("groups", "dp", "expert"), None),
        P("dp", None, "expert", None),
    )
    return jax.shard_map(
        local,
        mesh=mesh,
        in_specs=placed,
        out_specs=P(("groups", "dp", "expert"), None),
        check_vma=False,
    )
```

profile of v0, /device:TPU:0, one launch (start us, length us, event | category | flops | bytes accessed | tf_op | source)
XLA Modules:
  0.0 211.0 jit_solution(18027865610384389631)
XLA Ops:
  0.0 0.5 collective-permute-start
  0.5 0.8 copy.16
  1.2 0.1 eq.29
  1.3 0.1 eq.25
  1.4 1.1 reduce-window.6
  2.6 0.2 slice_reduce_fusion
  2.8 0.2 reduce-window.9
  3.1 51.4 %collective-permute-done = bf16[3,192,4096]{2,1,0:T(8,128)(2,1)} collective-permute-done((bf16[3,192,4096]{2,1,0:T(8,128)(2,1)}, bf16[3,192,4096]{2,1,0:T(8,128)(2,1)}, u32[]{:S(2)}, u32[]{:S(2)}) %collective-permute-start) | collective-permute-done | bytes 4718624 | tf_op jit(solution)/shard_map/ppermute | solution.py:10
  54.5 0.1 gt.32
  54.7 0.1 mul.126
  54.9 4.3 %scatter_custom_fusion.1 = s32[65]{0:T(128)S(1)} fusion(s32[1024]{0:T(1024)S(1)} %bitcast.103, s32[1024]{0:T(1024)S(1)} %add_select_fusion.1, s32[]{:T(128)} %constant.37.clone.1), kind=kCustom, calls=%fused_computation.138 | custom fusion | bytes 264 | tf_op jit(solution)/shard_map/scatter | solution.py:25
  59.2 4.3 %scatter_custom_fusion = s32[65]{0:T(128)S(1)} fusion(s32[1024]{0:T(1024)S(1)} %bitcast.104, s32[1024]{0:T(1024)S(1)} %broadcast.151, s32[]{:T(128)} %constant.37.clone.1), kind=kCustom, calls=%fused_computation.140 | custom fusion | bytes 264 | tf_op jit(solution)/shard_map/scatter | solution.py:29
  63.5 0.1 gt.36
  63.7 0.9 gather_fusion
  64.6 0.9 select_select_fusion
  65.5 5.7 %all-to-all-start = ((bf16[4,16,4096]{2,1,0:T(8,128)(2,1)}), bf16[4,16,4096]{2,1,0:T(8,128)(2,1)S(1)}, u32[]{:S(2)}, u32[]{:S(2)}) async-start(bf16[4,16,4096]{2,1,0:T(8,128)(2,1)} %select_select_fusion), calls=%async_computation | async-start | bytes 1048576 | tf_op jit(solution)/shard_map/all_to_all | solution.py:67
  71.2 0.4 fusion.54
  71.8 36.6 %collective-permute-done.1 = bf16[3,192,4096]{2,1,0:T(8,128)(2,1)} collective-permute-done((bf16[3,192,4096]{2,1,0:T(8,128)(2,1)}, bf16[3,192,4096]{2,1,0:T(8,128)(2,1)}, u32[]{:S(2)}, u32[]{:S(2)}) %collective-permute-start.1) | collective-permute-done | bytes 4718624 | tf_op jit(solution)/shard_map/ppermute | solution.py:10
  108.4 0.1 copy.26
  108.5 0.1 copy.24
  108.6 0.1 copy.23
  108.7 0.1 copy.22
  108.8 0.1 copy.21
  108.9 0.1 copy.20
  109.1 0.1 copy.18
  109.2 0.1 copy.25
  109.3 0.4 select_reduce_fusion.7
  109.7 1.5 slice_bitcast_fusion.3
  111.2 3.0 %fusion.20 = f32[2,64,192]{2,1,0:T(8,128)S(1)} fusion(bf16[64,4096,1]{1,0,2:T(8,128)(2,1)S(1)} %bitcast.97, bf16[1,3,192,4096]{3,2,1,0:T(8,128)(2,1)} %param.9), kind=kOutput, calls=%fused_computation.34 | convolution fusion | flops 201326592 | bytes 3768320 | tf_op jit(solution)/shard_map/rd,kfd->krf/dot_general | solution.py:57
  114.2 3.0 %fusion.23 = f32[2,64,192]{2,1,0:T(8,128)S(1)} fusion(bf16[64,4096,1]{1,0,2:T(8,128)(2,1)S(1)} %bitcast.98, bf16[3,192,4096]{2,1,0:T(8,128)(2,1)} %collective-permute-done), kind=kOutput, calls=%fused_computation.35 | convolution fusion | flops 201326592 | bytes 3768320 | tf_op jit(solution)/shard_map/rd,kfd->krf/dot_general | solution.py:57
  117.3 1.5 slice_bitcast_fusion.2
  118.8 3.0 %fusion.26 = f32[2,64,192]{2,1,0:T(8,128)S(1)} fusion(bf16[64,4096,1]{1,0,2:T(8,128)(2,1)S(1)} %bitcast.99, bf16[3,192,4096]{2,1,0:T(8,128)(2,1)} %collective-permute-done.1), kind=kOutput, calls=%fused_computation.36 | convolution fusion | flops 201326592 | bytes 3768320 | tf_op jit(solution)/shard_map/rd,kfd->krf/dot_general | solution.py:57
  121.8 1.5 slice_bitcast_fusion.1
  123.3 38.9 %collective-permute-done.2 = bf16[3,192,4096]{2,1,0:T(8,128)(2,1)} collective-permute-done((bf16[3,192,4096]{2,1,0:T(8,128)(2,1)}, bf16[3,192,4096]{2,1,0:T(8,128)(2,1)}, u32[]{:S(2)}, u32[]{:S(2)}) %collective-permute-start.2) | collective-permute-done | bytes 4718624 | tf_op jit(solution)/shard_map/ppermute | solution.py:10
  162.2 3.0 %fusion.29 = f32[2,64,192]{2,1,0:T(8,128)S(1)} fusion(bf16[64,4096,1]{1,0,2:T(8,128)(2,1)S(1)} %bitcast.100, bf16[3,192,4096]{2,1,0:T(8,128)(2,1)} %collective-permute-done.2), kind=kOutput, calls=%fused_computation.37 | convolution fusion | flops 201326592 | bytes 3768320 | tf_op jit(solution)/shard_map/rd,kfd->krf/dot_general | solution.py:57
  165.3 1.5 slice_bitcast_fusion
  166.8 2.2 %fusion.8 = bf16[64,4096]{1,0:T(8,128)(2,1)} fusion(bf16[192,4096]{1,0:T(8,128)(2,1)S(1)} %slice_bitcast_fusion, bf16[192,4096]{1,0:T(8,128)(2,1)S(1)} %slice_bitcast_fusion.1, bf16[192,4096]{1,0:T(8,128)(2,1)S(1)} %slice_bitcast_fusion.2, bf16[192,4096]{1,0:T(8,128)(2,1)S(1)} %slice_bitcast_fusion.3, bf16[64,192]{1,0:T(8,128)(2,1)S(1)} %fusion.47, ...), kind=kOutput, calls=%fused_computation.19 | convolution fusion | flops 428474368 | bytes 6914048 | tf_op jit(solution)/shard_map/dot_general | solution.py:81
  168.9 5.7 %all-to-all-start.1 = ((bf16[4,16,4096]{2,1,0:T(8,128)(2,1)}), bf16[4,16,4096]{2,1,0:T(8,128)(2,1)S(1)}, u32[]{:S(2)}, u32[]{:S(2)}) async-start(bf16[4,16,4096]{2,1,0:T(8,128)(2,1)} %bitcast.25), calls=%async_computation.1 | async-start | bytes 1048576 | tf_op jit(solution)/shard_map/all_to_all | solution.py:83
  174.7 13.7 %all-to-all-done.1 = bf16[4,16,4096]{2,1,0:T(8,128)(2,1)S(1)} async-done(((bf16[4,16,4096]{2,1,0:T(8,128)(2,1)}), bf16[4,16,4096]{2,1,0:T(8,128)(2,1)S(1)}, u32[]{:S(2)}, u32[]{:S(2)}) %all-to-all-start.1) | async-done | bytes 524320 | tf_op jit(solution)/shard_map/all_to_all | solution.py:83
  188.4 1.2 gather_fusion.8
  189.6 2.2 %gather_fusion.7 = bf16[128,4096]{1,0:T(8,128)(2,1)} fusion(bf16[64,4096]{1,0:T(8,128)(2,1)S(1)} %bitcast.88, s32[1024]{0:T(1024)S(1)} %pad_clamp_fusion.1), kind=kCustom, calls=%fused_computation.6.clone | custom fusion | bytes 2097664 | tf_op jit(solution)/shard_map/jit(_take)/gather | solution.py:48
  191.8 2.2 %gather_fusion.6 = bf16[128,4096]{1,0:T(8,128)(2,1)} fusion(bf16[64,4096]{1,0:T(8,128)(2,1)S(1)} %bitcast.89, s32[1024]{0:T(1024)S(1)} %pad_clamp_fusion.2), kind=kCustom, calls=%fused_computation.5.clone | custom fusion | bytes 2097664 | tf_op jit(solution)/shard_map/jit(_take)/gather | solution.py:48
  194.0 2.2 %gather_fusion.5 = bf16[128,4096]{1,0:T(8,128)(2,1)} fusion(bf16[64,4096]{1,0:T(8,128)(2,1)S(1)} %bitcast.90, s32[1024]{0:T(1024)S(1)} %pad_clamp_fusion.3), kind=kCustom, calls=%fused_computation.4.clone | custom fusion | bytes 2097664 | tf_op jit(solution)/shard_map/jit(_take)/gather | solution.py:48
  196.2 2.2 %gather_fusion.4 = bf16[128,4096]{1,0:T(8,128)(2,1)} fusion(bf16[64,4096]{1,0:T(8,128)(2,1)S(1)} %bitcast.91, s32[1024]{0:T(1024)S(1)} %pad_clamp_fusion.4), kind=kCustom, calls=%fused_computation.3.clone | custom fusion | bytes 2097664 | tf_op jit(solution)/shard_map/jit(_take)/gather | solution.py:48
  198.4 2.2 %gather_fusion.3 = bf16[128,4096]{1,0:T(8,128)(2,1)} fusion(bf16[64,4096]{1,0:T(8,128)(2,1)S(1)} %bitcast.92, s32[1024]{0:T(1024)S(1)} %pad_clamp_fusion.5), kind=kCustom, calls=%fused_computation.2.clone | custom fusion | bytes 2097664 | tf_op jit(solution)/shard_map/jit(_take)/gather | solution.py:48
  200.5 2.2 %gather_fusion.2 = bf16[128,4096]{1,0:T(8,128)(2,1)} fusion(bf16[64,4096]{1,0:T(8,128)(2,1)S(1)} %bitcast.93, s32[1024]{0:T(1024)S(1)} %pad_clamp_fusion.6), kind=kCustom, calls=%fused_computation.1.clone | custom fusion | bytes 2097664 | tf_op jit(solution)/shard_map/jit(_take)/gather | solution.py:48
  202.7 2.2 %gather_fusion.1 = bf16[128,4096]{1,0:T(8,128)(2,1)} fusion(bf16[64,4096]{1,0:T(8,128)(2,1)S(1)} %bitcast.94, s32[1024]{0:T(1024)S(1)} %pad_clamp_fusion.7), kind=kCustom, calls=%fused_computation.clone | custom fusion | bytes 2097664 | tf_op jit(solution)/shard_map/jit(_take)/gather | solution.py:48
  204.9 6.1 %add_convert_fusion = bf16[128,4096]{1,0:T(8,128)(2,1)} fusion(bf16[128,4096]{1,0:T(8,128)(2,1)S(1)} %gather_fusion.8, bf16[128,4096]{1,0:T(8,128)(2,1)} %gather_fusion.7, bf16[128,4096]{1,0:T(8,128)(2,1)} %gather_fusion.6, bf16[128,4096]{1,0:T(8,128)(2,1)} %gather_fusion.5, bf16[128,4096]{1,0:T(8,128)(2,1)} %gather_fusion.4, ...), kind=kLoop, calls=%fused_computation.29 | loop fusion | flops 16777216 | bytes 9442304 | tf_op jit(solution)/shard_map/convert_element_type | solution.py:53
  (43 shorter events, 0.6 us)
Async XLA Ops:
  0.0 63.7 %copy-start = (bf16[128,4096]{1,0:T(8,128)(2,1)S(1)}, bf16[128,4096]{1,0:T(8,128)(2,1)}, u32[]{:S(2)}) copy-start(bf16[128,4096]{1,0:T(8,128)(2,1)} %param.6) | copy-start | bytes 3145732
  0.0 54.5 %collective-permute-start = (bf16[3,192,4096]{2,1,0:T(8,128)(2,1)}, bf16[3,192,4096]{2,1,0:T(8,128)(2,1)}, u32[]{:S(2)}, u32[]{:S(2)}) collective-permute-start(bf16[3,192,4096]{2,1,0:T(8,128)(2,1)} %bitcast.96), channel_id=1, source_target_pairs={{3,0},{0,1},{1,2},{2,3},{7,4},{4,5},{5,6},{6,7},{11,8},{8,9},{9,10... | collective-permute-start | bytes 14155784 | tf_op jit(solution)/shard_map/ppermute | solution.py:10
  54.5 53.9 %collective-permute-start.1 = (bf16[3,192,4096]{2,1,0:T(8,128)(2,1)}, bf16[3,192,4096]{2,1,0:T(8,128)(2,1)}, u32[]{:S(2)}, u32[]{:S(2)}) collective-permute-start(bf16[3,192,4096]{2,1,0:T(8,128)(2,1)} %collective-permute-done), channel_id=1, source_target_pairs={{3,0},{0,1},{1,2},{2,3},{7,4},{4,5},{5,6},{6,7},{11,8},{8,9},{9,10... | collective-permute-start | bytes 14155784 | tf_op jit(solution)/shard_map/ppermute | solution.py:10
  64.6 7.2 %copy-start.1 = (f32[128,8]{0,1:T(8,128)S(1)}, f32[128,8]{0,1:T(8,128)}, u32[]{:S(2)}) copy-start(f32[128,8]{0,1:T(8,128)} %param.8) | copy-start | bytes 12292
  65.5 45.6 %all-to-all-start = ((bf16[4,16,4096]{2,1,0:T(8,128)(2,1)}), bf16[4,16,4096]{2,1,0:T(8,128)(2,1)S(1)}, u32[]{:S(2)}, u32[]{:S(2)}) async-start(bf16[4,16,4096]{2,1,0:T(8,128)(2,1)} %select_select_fusion), calls=%async_computation | async-start | bytes 1048576 | tf_op jit(solution)/shard_map/all_to_all | solution.py:67
  108.4 53.9 %collective-permute-start.2 = (bf16[3,192,4096]{2,1,0:T(8,128)(2,1)}, bf16[3,192,4096]{2,1,0:T(8,128)(2,1)}, u32[]{:S(2)}, u32[]{:S(2)}) collective-permute-start(bf16[3,192,4096]{2,1,0:T(8,128)(2,1)} %collective-permute-done.1), channel_id=1, source_target_pairs={{3,0},{0,1},{1,2},{2,3},{7,4},{4,5},{5,6},{6,7},{11,8},{8,9},{9,10... | collective-permute-start | bytes 14155784 | tf_op jit(solution)/shard_map/ppermute | solution.py:10
  168.9 19.5 %all-to-all-start.1 = ((bf16[4,16,4096]{2,1,0:T(8,128)(2,1)}), bf16[4,16,4096]{2,1,0:T(8,128)(2,1)S(1)}, u32[]{:S(2)}, u32[]{:S(2)}) async-start(bf16[4,16,4096]{2,1,0:T(8,128)(2,1)} %bitcast.25), calls=%async_computation.1 | async-start | bytes 1048576 | tf_op jit(solution)/shard_map/all_to_all | solution.py:83
where the time goes:
time: 212 us; the launch traced here: 211 us
  waiting for transfers between devices  141 us (67%)
  local copies, waits for them, and re-layouts  34.6 us (16%)
  matrix products  14.2 us (7%)
  starting transfers between devices  11.8 us (6%)
  other arithmetic  9.55 us (5%)
    ppermute x3, waiting for transfers between devices, from_behind(): return lax.ppermute(block, axis, route)  127 us
    gather x8, local copies, waits for them, and re-layouts, combine_copies(): jnp.take(returned, jnp.minimum(slot_of[:, rank], limit), axis=0)  16.5 us
    all_to_all x1, waiting for transfers between devices, local(): lax.all_to_all(results, 'dp', split_axis=0, concat_axis=0, tiled=True)  13.7 us
    dot_general x4, matrix products, hidden_part(): jnp.einsum('rd,kfd->krf', rows_in, slab[:2], preferred_element_type=jnp.f...  12 us
    convert_element_type x1, other arithmetic, combine_copies(): return total.astype(jnp.bfloat16)  6.12 us
    squeeze x4, local copies, waits for them, and re-layouts, local(): down_pieces.append(travelling[2])  6.05 us
    all_to_all x1, starting transfers between devices, local(): lax.all_to_all(results, 'dp', split_axis=0, concat_axis=0, tiled=True)  5.68 us
    all_to_all x1, starting transfers between devices, local(): lax.all_to_all(outgoing, 'dp', split_axis=0, concat_axis=0, tiled=True)  5.68 us
  transfers between devices with their start and end apart: 5, of which 4 were waited for; matrix products, arithmetic and copies ran while one was open for 14% of the time, Pallas kernels for 0%

commit v1 on v0

v1 whole, which is shorter than its diff:
```python
import functools
import jax
import jax.numpy as jnp
from jax import lax
from jax.experimental import pallas as pl
from jax.experimental.pallas import tpu as pltpu
from jax.sharding import PartitionSpec as P

NT = (((1,), (1,)), ((), ()))
WHOLE = pl.BlockSpec(memory_space=pltpu.VMEM)
ANYWHERE = pl.BlockSpec(memory_space=pl.ANY)


def swap(block, axis, mask):
    route = [(i ^ mask, i) for i in range(lax.axis_size(axis))]
    return lax.ppermute(block, axis, route)


def dispatch_kernel(experts, cap, assign_ref, probs_ref, tok_ref, *outs):
    rows_out, mix_out = outs[:-1], outs[-1]
    top, toks = assign_ref.shape
    slots = experts * cap
    me = lax.axis_index("dp")
    place = lax.broadcasted_iota(jnp.int32, (slots, toks), 0)
    label = (place // cap) ^ me
    hit = jnp.zeros((slots, toks), jnp.float32)
    weight = jnp.zeros((slots, toks), jnp.float32)
    for k in range(top):
        same = assign_ref[k : k + 1, :] == label
        hit = hit + same.astype(jnp.float32)
        weight = weight + jnp.where(same, probs_ref[k : k + 1, :], 0.0)
    first = lax.broadcasted_iota(jnp.int32, (toks, toks), 0)
    second = lax.broadcasted_iota(jnp.int32, (toks, toks), 1)
    earlier = (first < second).astype(jnp.bfloat16)
    position = jnp.dot(
        hit.astype(jnp.bfloat16), earlier, preferred_element_type=jnp.float32
    )
    here = (hit > 0.0) & (position == (place % cap).astype(jnp.float32))
    pick = here.astype(jnp.bfloat16)
    for m in range(experts):
        rows_out[m][...] = jnp.dot(
            pick[m * cap : (m + 1) * cap],
            tok_ref[...],
            preferred_element_type=jnp.float32,
        ).astype(jnp.bfloat16)
    factor = jnp.where(here, weight, 0.0).T
    high = factor.astype(jnp.bfloat16)
    rest = factor - high.astype(jnp.float32)
    middle = rest.astype(jnp.bfloat16)
    low = (rest - middle.astype(jnp.float32)).astype(jnp.bfloat16)
    mix_out[...] = jnp.concatenate([high, middle, low], axis=1)


def dispatch(assign, probs, tokens, experts, cap):
    toks, width = tokens.shape
    return pl.pallas_call(
        functools.partial(dispatch_kernel, experts, cap),
        out_shape=[jax.ShapeDtypeStruct((cap, width), jnp.bfloat16)] * experts
        + [jax.ShapeDtypeStruct((toks, 3 * experts * cap), jnp.bfloat16)],
        in_specs=[WHOLE] * 3,
        out_specs=[WHOLE] * (experts + 1),
        name="dispatch",
    )(assign.T, probs.T, tokens)


def expert_kernel(count, steps, *refs):
    slabs, blocks, outs = refs[:2], refs[2 : 2 + count], refs[2 + count : 2 + 2 * count]
    rows, enter, leave, sems = refs[2 + 2 * count :]
    units, width = slabs[0].shape[1:]
    cap = blocks[0].shape[0]
    span = width // steps

    def fetch(phase, step, j):
        cols = pl.ds(step * span, span)
        if phase == 0:
            return pltpu.make_async_copy(
                slabs[j].at[0:2, :, cols], enter.at[2 * j : 2 * j + 2, :, cols], sems.at[phase, step, j]
            )
        return pltpu.make_async_copy(
            slabs[j].at[2, :, cols], leave.at[j, :, cols], sems.at[phase, step, j]
        )

    for phase in range(2):
        for step in range(steps):
            for j in range(2):
                fetch(phase, step, j).start()
    for b in range(count):
        rows[b * cap : (b + 1) * cap, :] = blocks[b][...]
    both = jnp.zeros((count * cap, 4 * units), jnp.float32)
    for step in range(steps):
        for j in range(2):
            fetch(0, step, j).wait()
        cols = slice(step * span, (step + 1) * span)
        both = both + lax.dot_general(
            rows[:, cols],
            enter[:, :, cols].reshape(4 * units, span),
            NT,
            preferred_element_type=jnp.float32,
        )
    hidden = []
    for j in range(2):
        gate = both[:, 2 * j * units : (2 * j + 1) * units]
        up = both[:, (2 * j + 1) * units : (2 * j + 2) * units]
        hidden.append((jax.nn.silu(gate) * up).astype(jnp.bfloat16))
    hidden = jnp.concatenate(hidden, axis=1)
    for step in range(steps):
        for j in range(2):
            fetch(1, step, j).wait()
        cols = slice(step * span, (step + 1) * span)
        part = jnp.dot(
            hidden,
            leave[:, :, cols].reshape(2 * units, span),
            preferred_element_type=jnp.float32,
        )
        for b in range(count):
            outs[b][:, cols] = part[b * cap : (b + 1) * cap].astype(outs[b].dtype)


def expert_part(own, sibling, blocks, kinds, steps=4):
    count = len(blocks)
    cap, width = blocks[0].shape
    units = own.shape[1]
    return pl.pallas_call(
        functools.partial(expert_kernel, count, steps),
        out_shape=[jax.ShapeDtypeStruct((cap, width), kind) for kind in kinds],
        in_specs=[ANYWHERE] * 2 + [WHOLE] * count,
        out_specs=[WHOLE] * count,
        scratch_shapes=[
            pltpu.VMEM((count * cap, width), jnp.bfloat16),
            pltpu.VMEM((4, units, width), jnp.bfloat16),
            pltpu.VMEM((2, units, width), jnp.bfloat16),
            pltpu.SemaphoreType.DMA((2, steps, 2)),
        ],
        compiler_params=pltpu.CompilerParams(vmem_limit_bytes=48 * 1024 * 1024),
        name="experts",
    )(own, sibling, *blocks)


def combine_kernel(count, mix_ref, *refs):
    rows = jnp.concatenate([ref[...] for ref in refs[:count]], axis=0)
    refs[count][...] = jnp.dot(
        mix_ref[...],
        jnp.concatenate([rows] * 3, axis=0),
        preferred_element_type=jnp.float32,
    ).astype(jnp.bfloat16)


def combine(mix, returned, steps=4):
    count = len(returned)
    cap, width = returned[0].shape
    toks = mix.shape[0]
    span = width // steps
    return pl.pallas_call(
        functools.partial(combine_kernel, count),
        grid=(steps,),
        out_shape=jax.ShapeDtypeStruct((toks, width), jnp.bfloat16),
        in_specs=[pl.BlockSpec(mix.shape, lambda i: (0, 0))]
        + [pl.BlockSpec((cap, span), lambda i: (0, i))] * count,
        out_specs=pl.BlockSpec((toks, span), lambda i: (0, i)),
        name="combine",
    )(mix, *returned)


def local(tokens, assign, probs, expert_weights):
    experts = lax.axis_size("dp")
    chips = lax.axis_size("expert") // 2
    cap = tokens.shape[0] // 8
    own = expert_weights[0]
    sibling = swap(own, "expert", 1)
    *outgoing, mix = dispatch(assign, probs, tokens, experts, cap)
    arrived = [swap(p, "dp", m) if m else p for m, p in enumerate(outgoing)]
    blocks = [
        swap(p, "expert", 2 * c) if c else p for p in arrived for c in range(chips)
    ]
    kinds = [jnp.bfloat16 if c else jnp.float32 for _ in arrived for c in range(chips)]
    parts = expert_part(own, sibling, blocks, kinds)
    returned = []
    for m in range(experts):
        total = parts[m * chips]
        for c in range(1, chips):
            total = total + swap(parts[m * chips + c], "expert", 2 * c).astype(jnp.float32)
        total = total.astype(jnp.bfloat16)
        returned.append(swap(total, "dp", m) if m else total)
    return combine(mix, returned)


def solution(mesh):
    placed = (
        P(("groups", "dp", "expert"), None),
        P(("groups", "dp", "expert"), None),
        P(("groups", "dp", "expert"), None),
        P("dp", None, "expert", None),
    )
    return jax.shard_map(
        local,
        mesh=mesh,
        in_specs=placed,
        out_specs=P(("groups", "dp", "expert"), None),
        check_vma=False,
    )
```

time: 212 us -> 57.4 us (0.27)
  waiting for transfers between devices: 141 us -> 18.8 us
  local copies, waits for them, and re-layouts: 34.6 us -> 1.56 us
  matrix products: 14.2 us -> 0 us
  Pallas kernels: 0 us -> 12.8 us
  starting transfers between devices: 11.8 us -> 23 us
  other arithmetic: 9.55 us -> 0.75 us
    ppermute x3 -> x15, waiting for transfers between devices: 127 us -> 18.8 us  [swap(): return lax.ppermute(block, axis, route)]
    ppermute x3 -> x15, starting transfers between devices: 0.46 us -> 23 us  [swap(): return lax.ppermute(block, axis, route)]
    gather x9 -> x0, local copies, waits for them, and re-layouts: 17.4 us -> none  [the longest x8 16.5 us: combine_copies(): jnp.take(returned, jnp.minimum(slot_of[:, rank], limit), axis=0)]
    dot_general x5 -> x0, matrix products: 14.2 us -> none  [the longest x4 12 us: hidden_part(): jnp.einsum('rd,kfd->krf', rows_in, slab[:2], preferred_element_type=jnp.f...]
    all_to_all x2 -> x0, waiting for transfers between devices: 13.7 us -> none  [the longest x1 13.7 us: local(): lax.all_to_all(results, 'dp', split_axis=0, concat_axis=0, tiled=True)]
    pallas_call x0 -> x3, Pallas kernels: none -> 12.8 us  [the longest x1 6.5 us: expert_part(): pl.pallas_call(functools.partial(expert_kernel, count, steps), out_shape=...]
    all_to_all x2 -> x0, starting transfers between devices: 11.4 us -> none  [the longest x1 5.68 us: local(): lax.all_to_all(results, 'dp', split_axis=0, concat_axis=0, tiled=True)]
    scatter x2 -> x0, local copies, waits for them, and re-layouts: 8.61 us -> none  [the longest x1 4.3 us: routing_slots(): jnp.zeros((dump_slot + 1,), jnp.int32).at[slot_of].set(owner_token)]
  transfers between devices with their start and end apart: 5 -> 15, of which waited for: 4 -> 8; matrix products, arithmetic and copies ran while one was open for 14% -> 1% of each run, Pallas kernels for 0% -> 5%
where the time goes in v1:
time: 57.4 us; the launch traced here: 57 us
  starting transfers between devices  23 us (40%)
  waiting for transfers between devices  18.8 us (33%)
  Pallas kernels  12.8 us (22%)
  local copies, waits for them, and re-layouts  1.56 us (3%)
  other arithmetic  0.75 us (1%)
    ppermute x15, starting transfers between devices, swap(): return lax.ppermute(block, axis, route)  23 us
    ppermute x15, waiting for transfers between devices, swap(): return lax.ppermute(block, axis, route)  18.8 us
    pallas_call x1, Pallas kernels, expert_part(): pl.pallas_call(functools.partial(expert_kernel, count, steps), out_shape=...  6.5 us
    pallas_call x1, Pallas kernels, combine(): pl.pallas_call(functools.partial(combine_kernel, count), grid=(steps,), o...  3.61 us
    pallas_call x1, Pallas kernels, dispatch(): pl.pallas_call(functools.partial(dispatch_kernel, experts, cap), out_shap...  2.72 us
    unnamed x8, local copies, waits for them, and re-layouts  1.56 us
  transfers between devices with their start and end apart: 15, of which 8 were waited for; matrix products, arithmetic and copies ran while one was open for 1% of the time, Pallas kernels for 5%

profile of v1, /device:TPU:0, one launch (start us, length us, event | category | flops | bytes accessed | tf_op | source)
XLA Modules:
  0.0 57.0 jit_solution(457950319690438482)
XLA Ops:
  0.0 0.5 collective-permute-start
  0.5 2.7 %dispatch.1 = (bf16[16,4096]{1,0:T(8,128)(2,1)}, bf16[16,4096]{1,0:T(8,128)(2,1)}, bf16[16,4096]{1,0:T(8,128)(2,1)}, bf16[16,4096]{1,0:T(8,128)(2,1)}, bf16[128,192]{1,0:T(8,128)(2,1)}) custom-call(s32[8,128]{1,0:T(8,128)} %bitcast.5, f32[8,128]{1,0:T(8,128)} %bitcast.6, bf16[128,4096]{1,0:T(8,128)(2,1)} %tok_ref.1), custom_call_target="tpu_custom_call" | custom-call | tf_op jit(solution)/shard_map/dispatch/pallas_call | solution.py:56
  3.2 2.6 %collective-permute-start.2 = (bf16[16,4096]{1,0:T(8,128)(2,1)}, bf16[16,4096]{1,0:T(8,128)(2,1)S(1)}, u32[]{:S(2)}, u32[]{:S(2)}) collective-permute-start(bf16[16,4096]{1,0:T(8,128)(2,1)} %get-tuple-element.20), channel_id=1, source_target_pairs={{4,0},{0,4},{12,8},{8,12},{5,1},{1,5},{13,9},{9,13},{6,2},{2,6},{1... | collective-permute-start | bytes 393224 | tf_op jit(solution)/shard_map/ppermute | solution.py:16
  5.7 2.6 %collective-permute-start.4 = (bf16[16,4096]{1,0:T(8,128)(2,1)}, bf16[16,4096]{1,0:T(8,128)(2,1)S(1)}, u32[]{:S(2)}, u32[]{:S(2)}) collective-permute-start(bf16[16,4096]{1,0:T(8,128)(2,1)} %get-tuple-element.21), channel_id=1, source_target_pairs={{8,0},{12,4},{0,8},{4,12},{9,1},{13,5},{1,9},{5,13},{10,2},{14,6},... | collective-permute-start | bytes 393224 | tf_op jit(solution)/shard_map/ppermute | solution.py:16
  8.3 0.0 collective-permute-start.6
  8.3 1.7 %collective-permute-start.1 = (bf16[16,4096]{1,0:T(8,128)(2,1)}, bf16[16,4096]{1,0:T(8,128)(2,1)S(1)}, u32[]{:S(2)}, u32[]{:S(2)}) collective-permute-start(bf16[16,4096]{1,0:T(8,128)(2,1)} %get-tuple-element.19.refs_2_), channel_id=1, source_target_pairs={{2,0},{3,1},{0,2},{1,3},{6,4},{7,5},{4,6},{5,7},{10,8},{11,9},{8,1... | collective-permute-start | bytes 393224 | tf_op jit(solution)/shard_map/ppermute | solution.py:16
  10.1 2.3 %collective-permute-done.2.refs_4_ = bf16[16,4096]{1,0:T(8,128)(2,1)S(1)} collective-permute-done((bf16[16,4096]{1,0:T(8,128)(2,1)}, bf16[16,4096]{1,0:T(8,128)(2,1)S(1)}, u32[]{:S(2)}, u32[]{:S(2)}) %collective-permute-start.2) | collective-permute-done | bytes 131104 | tf_op jit(solution)/shard_map/ppermute | solution.py:16
  12.4 1.7 %collective-permute-start.3 = (bf16[16,4096]{1,0:T(8,128)(2,1)S(1)}, bf16[16,4096]{1,0:T(8,128)(2,1)S(1)}, u32[]{:S(2)}, u32[]{:S(2)}) collective-permute-start(bf16[16,4096]{1,0:T(8,128)(2,1)S(1)} %collective-permute-done.2.refs_4_), channel_id=1, source_target_pairs={{2,0},{3,1},{0,2},{1,3},{6,4},{7,5},{4,6},{5,7},{10,8},{11,9},{8,1... | collective-permute-start | bytes 393224 | tf_op jit(solution)/shard_map/ppermute | solution.py:16
  14.1 4.7 %collective-permute-done.4.refs_6_ = bf16[16,4096]{1,0:T(8,128)(2,1)S(1)} collective-permute-done((bf16[16,4096]{1,0:T(8,128)(2,1)}, bf16[16,4096]{1,0:T(8,128)(2,1)S(1)}, u32[]{:S(2)}, u32[]{:S(2)}) %collective-permute-start.4) | collective-permute-done | bytes 131104 | tf_op jit(solution)/shard_map/ppermute | solution.py:16
  18.9 1.5 %collective-permute-start.5 = (bf16[16,4096]{1,0:T(8,128)(2,1)S(1)}, bf16[16,4096]{1,0:T(8,128)(2,1)S(1)}, u32[]{:S(2)}, u32[]{:S(2)}) collective-permute-start(bf16[16,4096]{1,0:T(8,128)(2,1)S(1)} %collective-permute-done.4.refs_6_), channel_id=1, source_target_pairs={{2,0},{3,1},{0,2},{1,3},{6,4},{7,5},{4,6},{5,7},{10,8},{11,9},{8,1... | collective-permute-start | bytes 393224 | tf_op jit(solution)/shard_map/ppermute | solution.py:16
  20.3 0.0 collective-permute-done.6.refs_8_
  20.3 0.5 collective-permute-start.7
  20.9 0.0 collective-permute-done.1.refs_3_
  20.9 0.0 collective-permute-done.3.refs_5_
  20.9 2.9 %collective-permute-done.5.refs_7_ = bf16[16,4096]{1,0:T(8,128)(2,1)S(1)} collective-permute-done((bf16[16,4096]{1,0:T(8,128)(2,1)S(1)}, bf16[16,4096]{1,0:T(8,128)(2,1)S(1)}, u32[]{:S(2)}, u32[]{:S(2)}) %collective-permute-start.5) | collective-permute-done | bytes 131104 | tf_op jit(solution)/shard_map/ppermute | solution.py:16
  23.8 1.5 %collective-permute-done.7.refs_9_ = bf16[16,4096]{1,0:T(8,128)(2,1)S(1)} collective-permute-done((bf16[16,4096]{1,0:T(8,128)(2,1)S(1)}, bf16[16,4096]{1,0:T(8,128)(2,1)S(1)}, u32[]{:S(2)}, u32[]{:S(2)}) %collective-permute-start.7) | collective-permute-done | bytes 131104 | tf_op jit(solution)/shard_map/ppermute | solution.py:16
  25.3 0.0 collective-permute-done.refs_1_
  25.3 0.0 copy-start
  25.3 0.9 %copy-done = bf16[16,4096]{1,0:T(8,128)(2,1)S(1)} copy-done((bf16[16,4096]{1,0:T(8,128)(2,1)S(1)}, bf16[16,4096]{1,0:T(8,128)(2,1)}, u32[]{:S(2)}) %copy-start) | copy-done | bytes 131096
  26.2 6.5 %experts.1 = (f32[16,4096]{1,0:T(8,128)S(1)}, bf16[16,4096]{1,0:T(8,128)(2,1)S(1)}, f32[16,4096]{1,0:T(8,128)S(1)}, bf16[16,4096]{1,0:T(8,128)(2,1)S(1)}, f32[16...) custom-call(bf16[3,192,4096]{2,1,0:T(8,128)(2,1)} %bitcast.4, ...), custom_call_target="tpu_custom_call" | custom-call | tf_op jit(solution)/shard_map/experts/pallas_call | solution.py:123
  32.7 1.5 %collective-permute-start.9 = (bf16[16,4096]{1,0:T(8,128)(2,1)S(1)}, bf16[16,4096]{1,0:T(8,128)(2,1)S(1)}, u32[]{:S(2)}, u32[]{:S(2)}) collective-permute-start(bf16[16,4096]{1,0:T(8,128)(2,1)S(1)} %get-tuple-element.26), channel_id=1, source_target_pairs={{2,0},{3,1},{0,2},{1,3},{6,4},{7,5},{4,6},{5,7},{10,8},{11,9},{8,1... | collective-permute-start | bytes 393224 | tf_op jit(solution)/shard_map/ppermute | solution.py:16
  34.2 0.6 %collective-permute-start.8 = (bf16[16,4096]{1,0:T(8,128)(2,1)S(1)}, bf16[16,4096]{1,0:T(8,128)(2,1)S(1)}, u32[]{:S(2)}, u32[]{:S(2)}) collective-permute-start(bf16[16,4096]{1,0:T(8,128)(2,1)S(1)} %get-tuple-element.24), channel_id=1, source_target_pairs={{2,0},{3,1},{0,2},{1,3},{6,4},{7,5},{4,6},{5,7},{10,8},{11,9},{8,1... | collective-permute-start | bytes 393224 | tf_op jit(solution)/shard_map/ppermute | solution.py:16
  34.8 1.4 %collective-permute-start.11 = (bf16[16,4096]{1,0:T(8,128)(2,1)S(1)}, bf16[16,4096]{1,0:T(8,128)(2,1)S(1)}, u32[]{:S(2)}, u32[]{:S(2)}) collective-permute-start(bf16[16,4096]{1,0:T(8,128)(2,1)S(1)} %get-tuple-element.28), channel_id=1, source_target_pairs={{2,0},{3,1},{0,2},{1,3},{6,4},{7,5},{4,6},{5,7},{10,8},{11,9},{8,1... | collective-permute-start | bytes 393224 | tf_op jit(solution)/shard_map/ppermute | solution.py:16
  36.2 0.6 %collective-permute-start.13 = (bf16[16,4096]{1,0:T(8,128)(2,1)S(1)}, bf16[16,4096]{1,0:T(8,128)(2,1)S(1)}, u32[]{:S(2)}, u32[]{:S(2)}) collective-permute-start(bf16[16,4096]{1,0:T(8,128)(2,1)S(1)} %get-tuple-element.30), channel_id=1, source_target_pairs={{2,0},{3,1},{0,2},{1,3},{6,4},{7,5},{4,6},{5,7},{10,8},{11,9},{8,1... | collective-permute-start | bytes 393224 | tf_op jit(solution)/shard_map/ppermute | solution.py:16
  36.9 1.8 %collective-permute-done.9 = bf16[16,4096]{1,0:T(8,128)(2,1)S(1)} collective-permute-done((bf16[16,4096]{1,0:T(8,128)(2,1)S(1)}, bf16[16,4096]{1,0:T(8,128)(2,1)S(1)}, u32[]{:S(2)}, u32[]{:S(2)}) %collective-permute-start.9) | collective-permute-done | bytes 131104 | tf_op jit(solution)/shard_map/ppermute | solution.py:16
  38.6 1.9 %collective-permute-start.10 = (bf16[16,4096]{1,0:T(8,128)(2,1)S(1)}, bf16[16,4096]{1,0:T(8,128)(2,1)S(1)}, u32[]{:S(2)}, u32[]{:S(2)}) collective-permute-start(bf16[16,4096]{1,0:T(8,128)(2,1)S(1)} %add_convert_fusion.2), channel_id=1, source_target_pairs={{4,0},{0,4},{12,8},{8,12},{5,1},{1,5},{13,9},{9,13},{6,2},{2,6},{1... | collective-permute-start | bytes 393224 | tf_op jit(solution)/shard_map/ppermute | solution.py:16
  40.5 0.9 %collective-permute-done.11 = bf16[16,4096]{1,0:T(8,128)(2,1)S(1)} collective-permute-done((bf16[16,4096]{1,0:T(8,128)(2,1)S(1)}, bf16[16,4096]{1,0:T(8,128)(2,1)S(1)}, u32[]{:S(2)}, u32[]{:S(2)}) %collective-permute-start.11) | collective-permute-done | bytes 131104 | tf_op jit(solution)/shard_map/ppermute | solution.py:16
  41.5 4.3 %collective-permute-start.12 = (bf16[16,4096]{1,0:T(8,128)(2,1)S(1)}, bf16[16,4096]{1,0:T(8,128)(2,1)S(1)}, u32[]{:S(2)}, u32[]{:S(2)}) collective-permute-start(bf16[16,4096]{1,0:T(8,128)(2,1)S(1)} %add_convert_fusion.1), channel_id=1, source_target_pairs={{8,0},{12,4},{0,8},{4,12},{9,1},{13,5},{1,9},{5,13},{10,2},{14,6},... | collective-permute-start | bytes 393224 | tf_op jit(solution)/shard_map/ppermute | solution.py:16
  45.8 0.0 collective-permute-done.13
  45.8 1.6 %collective-permute-start.14 = (bf16[16,4096]{1,0:T(8,128)(2,1)S(1)}, bf16[16,4096]{1,0:T(8,128)(2,1)S(1)}, u32[]{:S(2)}, u32[]{:S(2)}) collective-permute-start(bf16[16,4096]{1,0:T(8,128)(2,1)S(1)} %add_convert_fusion), channel_id=1, source_target_pairs={{12,0},{8,4},{4,8},{0,12},{13,1},{9,5},{5,9},{1,13},{14,2},{10,6},... | collective-permute-start | bytes 393224 | tf_op jit(solution)/shard_map/ppermute | solution.py:16
  47.4 0.0 collective-permute-done.8
  47.4 0.7 %add_convert_fusion.3.refs_0_ = bf16[16,4096]{1,0:T(8,128)(2,1)} fusion(f32[16,4096]{1,0:T(8,128)S(1)} %get-tuple-element.23, bf16[16,4096]{1,0:T(8,128)(2,1)S(1)} %collective-permute-done.8), kind=kLoop, calls=%fused_computation.3 | loop fusion | flops 196608 | bytes 524288 | tf_op jit(solution)/shard_map/convert_element_type | solution.py:182
  48.1 0.0 collective-permute-done.10.refs_1_
  48.1 0.0 copy-start.1
  48.1 3.2 %collective-permute-done.12.refs_2_ = bf16[16,4096]{1,0:T(8,128)(2,1)S(1)} collective-permute-done((bf16[16,4096]{1,0:T(8,128)(2,1)S(1)}, bf16[16,4096]{1,0:T(8,128)(2,1)S(1)}, u32[]{:S(2)}, u32[]{:S(2)}) %collective-permute-start.12) | collective-permute-done | bytes 131104 | tf_op jit(solution)/shard_map/ppermute | solution.py:16
  51.3 0.0 copy-start.2
  51.3 1.4 %collective-permute-done.14.refs_3_ = bf16[16,4096]{1,0:T(8,128)(2,1)S(1)} collective-permute-done((bf16[16,4096]{1,0:T(8,128)(2,1)S(1)}, bf16[16,4096]{1,0:T(8,128)(2,1)S(1)}, u32[]{:S(2)}, u32[]{:S(2)}) %collective-permute-start.14) | collective-permute-done | bytes 131104 | tf_op jit(solution)/shard_map/ppermute | solution.py:16
  52.7 0.0 copy-start.3
  52.7 0.0 copy-done.1
  52.7 0.0 copy-done.2
  52.7 0.6 %copy-done.3 = bf16[16,4096]{1,0:T(8,128)(2,1)} copy-done((bf16[16,4096]{1,0:T(8,128)(2,1)}, bf16[16,4096]{1,0:T(8,128)(2,1)S(1)}, u32[]{:S(2)}) %copy-start.3) | copy-done | bytes 131096
  53.4 3.6 %combine.1 = bf16[128,4096]{1,0:T(8,128)(2,1)} custom-call(bf16[128,192]{1,0:T(8,128)(2,1)} %get-tuple-element.18.mix_ref, bf16[16,4096]{1,0:T(8,128)(2,1)} %add_convert_fusion.3.refs_0_, bf16[16,4096]{1,0:T(8,128)(2,1)} %copy-done.1, bf16[16,4096]{1,0:T(8,128)(2,1)} %copy-done.2, bf16[16,4096]{1,0:T(8,128)(2,1)} %copy-done.3), custom_call_target="tpu_custom_call" | custom-call | tf_op jit(solution)/shard_map/combine/pallas_call | solution.py:153
  (3 shorter events, 0.1 us)
Async XLA Ops:
  0.0 25.3 %collective-permute-start = (bf16[3,192,4096]{2,1,0:T(8,128)(2,1)}, bf16[3,192,4096]{2,1,0:T(8,128)(2,1)}, u32[]{:S(2)}, u32[]{:S(2)}) collective-permute-start(bf16[3,192,4096]{2,1,0:T(8,128)(2,1)} %bitcast.3), channel_id=1, source_target_pairs={{1,0},{0,1},{3,2},{2,3},{5,4},{4,5},{7,6},{6,7},{9,8},{8,9},{11,10... | collective-permute-start | bytes 14155784 | tf_op jit(solution)/shard_map/ppermute | solution.py:16
  3.2 9.2 %collective-permute-start.2 = (bf16[16,4096]{1,0:T(8,128)(2,1)}, bf16[16,4096]{1,0:T(8,128)(2,1)S(1)}, u32[]{:S(2)}, u32[]{:S(2)}) collective-permute-start(bf16[16,4096]{1,0:T(8,128)(2,1)} %get-tuple-element.20), channel_id=1, source_target_pairs={{4,0},{0,4},{12,8},{8,12},{5,1},{1,5},{13,9},{9,13},{6,2},{2,6},{1... | collective-permute-start | bytes 393224 | tf_op jit(solution)/shard_map/ppermute | solution.py:16
  5.7 13.1 %collective-permute-start.4 = (bf16[16,4096]{1,0:T(8,128)(2,1)}, bf16[16,4096]{1,0:T(8,128)(2,1)S(1)}, u32[]{:S(2)}, u32[]{:S(2)}) collective-permute-start(bf16[16,4096]{1,0:T(8,128)(2,1)} %get-tuple-element.21), channel_id=1, source_target_pairs={{8,0},{12,4},{0,8},{4,12},{9,1},{13,5},{1,9},{5,13},{10,2},{14,6},... | collective-permute-start | bytes 393224 | tf_op jit(solution)/shard_map/ppermute | solution.py:16
  8.3 12.0 %collective-permute-start.6 = (bf16[16,4096]{1,0:T(8,128)(2,1)}, bf16[16,4096]{1,0:T(8,128)(2,1)S(1)}, u32[]{:S(2)}, u32[]{:S(2)}) collective-permute-start(bf16[16,4096]{1,0:T(8,128)(2,1)} %get-tuple-element.22), channel_id=1, source_target_pairs={{12,0},{8,4},{4,8},{0,12},{13,1},{9,5},{5,9},{1,13},{14,2},{10,6},... | collective-permute-start | bytes 393224 | tf_op jit(solution)/shard_map/ppermute | solution.py:16
  8.3 12.5 %collective-permute-start.1 = (bf16[16,4096]{1,0:T(8,128)(2,1)}, bf16[16,4096]{1,0:T(8,128)(2,1)S(1)}, u32[]{:S(2)}, u32[]{:S(2)}) collective-permute-start(bf16[16,4096]{1,0:T(8,128)(2,1)} %get-tuple-element.19.refs_2_), channel_id=1, source_target_pairs={{2,0},{3,1},{0,2},{1,3},{6,4},{7,5},{4,6},{5,7},{10,8},{11,9},{8,1... | collective-permute-start | bytes 393224 | tf_op jit(solution)/shard_map/ppermute | solution.py:16
  12.4 8.5 %collective-permute-start.3 = (bf16[16,4096]{1,0:T(8,128)(2,1)S(1)}, bf16[16,4096]{1,0:T(8,128)(2,1)S(1)}, u32[]{:S(2)}, u32[]{:S(2)}) collective-permute-start(bf16[16,4096]{1,0:T(8,128)(2,1)S(1)} %collective-permute-done.2.refs_4_), channel_id=1, source_target_pairs={{2,0},{3,1},{0,2},{1,3},{6,4},{7,5},{4,6},{5,7},{10,8},{11,9},{8,1... | collective-permute-start | bytes 393224 | tf_op jit(solution)/shard_map/ppermute | solution.py:16
  18.9 5.0 %collective-permute-start.5 = (bf16[16,4096]{1,0:T(8,128)(2,1)S(1)}, bf16[16,4096]{1,0:T(8,128)(2,1)S(1)}, u32[]{:S(2)}, u32[]{:S(2)}) collective-permute-start(bf16[16,4096]{1,0:T(8,128)(2,1)S(1)} %collective-permute-done.4.refs_6_), channel_id=1, source_target_pairs={{2,0},{3,1},{0,2},{1,3},{6,4},{7,5},{4,6},{5,7},{10,8},{11,9},{8,1... | collective-permute-start | bytes 393224 | tf_op jit(solution)/shard_map/ppermute | solution.py:16
  20.3 5.0 %collective-permute-start.7 = (bf16[16,4096]{1,0:T(8,128)(2,1)S(1)}, bf16[16,4096]{1,0:T(8,128)(2,1)S(1)}, u32[]{:S(2)}, u32[]{:S(2)}) collective-permute-start(bf16[16,4096]{1,0:T(8,128)(2,1)S(1)} %collective-permute-done.6.refs_8_), channel_id=1, source_target_pairs={{2,0},{3,1},{0,2},{1,3},{6,4},{7,5},{4,6},{5,7},{10,8},{11,9},{8,1... | collective-permute-start | bytes 393224 | tf_op jit(solution)/shard_map/ppermute | solution.py:16
  25.3 0.9 %copy-start = (bf16[16,4096]{1,0:T(8,128)(2,1)S(1)}, bf16[16,4096]{1,0:T(8,128)(2,1)}, u32[]{:S(2)}) copy-start(bf16[16,4096]{1,0:T(8,128)(2,1)} %get-tuple-element.19.refs_2_) | copy-start | bytes 393220
  32.7 5.9 %collective-permute-start.9 = (bf16[16,4096]{1,0:T(8,128)(2,1)S(1)}, bf16[16,4096]{1,0:T(8,128)(2,1)S(1)}, u32[]{:S(2)}, u32[]{:S(2)}) collective-permute-start(bf16[16,4096]{1,0:T(8,128)(2,1)S(1)} %get-tuple-element.26), channel_id=1, source_target_pairs={{2,0},{3,1},{0,2},{1,3},{6,4},{7,5},{4,6},{5,7},{10,8},{11,9},{8,1... | collective-permute-start | bytes 393224 | tf_op jit(solution)/shard_map/ppermute | solution.py:16
  34.2 13.2 %collective-permute-start.8 = (bf16[16,4096]{1,0:T(8,128)(2,1)S(1)}, bf16[16,4096]{1,0:T(8,128)(2,1)S(1)}, u32[]{:S(2)}, u32[]{:S(2)}) collective-permute-start(bf16[16,4096]{1,0:T(8,128)(2,1)S(1)} %get-tuple-element.24), channel_id=1, source_target_pairs={{2,0},{3,1},{0,2},{1,3},{6,4},{7,5},{4,6},{5,7},{10,8},{11,9},{8,1... | collective-permute-start | bytes 393224 | tf_op jit(solution)/shard_map/ppermute | solution.py:16
  34.8 6.6 %collective-permute-start.11 = (bf16[16,4096]{1,0:T(8,128)(2,1)S(1)}, bf16[16,4096]{1,0:T(8,128)(2,1)S(1)}, u32[]{:S(2)}, u32[]{:S(2)}) collective-permute-start(bf16[16,4096]{1,0:T(8,128)(2,1)S(1)} %get-tuple-element.28), channel_id=1, source_target_pairs={{2,0},{3,1},{0,2},{1,3},{6,4},{7,5},{4,6},{5,7},{10,8},{11,9},{8,1... | collective-permute-start | bytes 393224 | tf_op jit(solution)/shard_map/ppermute | solution.py:16
  36.2 9.5 %collective-permute-start.13 = (bf16[16,4096]{1,0:T(8,128)(2,1)S(1)}, bf16[16,4096]{1,0:T(8,128)(2,1)S(1)}, u32[]{:S(2)}, u32[]{:S(2)}) collective-permute-start(bf16[16,4096]{1,0:T(8,128)(2,1)S(1)} %get-tuple-element.30), channel_id=1, source_target_pairs={{2,0},{3,1},{0,2},{1,3},{6,4},{7,5},{4,6},{5,7},{10,8},{11,9},{8,1... | collective-permute-start | bytes 393224 | tf_op jit(solution)/shard_map/ppermute | solution.py:16
  38.6 9.5 %collective-permute-start.10 = (bf16[16,4096]{1,0:T(8,128)(2,1)S(1)}, bf16[16,4096]{1,0:T(8,128)(2,1)S(1)}, u32[]{:S(2)}, u32[]{:S(2)}) collective-permute-start(bf16[16,4096]{1,0:T(8,128)(2,1)S(1)} %add_convert_fusion.2), channel_id=1, source_target_pairs={{4,0},{0,4},{12,8},{8,12},{5,1},{1,5},{13,9},{9,13},{6,2},{2,6},{1... | collective-permute-start | bytes 393224 | tf_op jit(solution)/shard_map/ppermute | solution.py:16
  41.5 9.9 %collective-permute-start.12 = (bf16[16,4096]{1,0:T(8,128)(2,1)S(1)}, bf16[16,4096]{1,0:T(8,128)(2,1)S(1)}, u32[]{:S(2)}, u32[]{:S(2)}) collective-permute-start(bf16[16,4096]{1,0:T(8,128)(2,1)S(1)} %add_convert_fusion.1), channel_id=1, source_target_pairs={{8,0},{12,4},{0,8},{4,12},{9,1},{13,5},{1,9},{5,13},{10,2},{14,6},... | collective-permute-start | bytes 393224 | tf_op jit(solution)/shard_map/ppermute | solution.py:16
  45.8 6.9 %collective-permute-start.14 = (bf16[16,4096]{1,0:T(8,128)(2,1)S(1)}, bf16[16,4096]{1,0:T(8,128)(2,1)S(1)}, u32[]{:S(2)}, u32[]{:S(2)}) collective-permute-start(bf16[16,4096]{1,0:T(8,128)(2,1)S(1)} %add_convert_fusion), channel_id=1, source_target_pairs={{12,0},{8,4},{4,8},{0,12},{13,1},{9,5},{5,9},{1,13},{14,2},{10,6},... | collective-permute-start | bytes 393224 | tf_op jit(solution)/shard_map/ppermute | solution.py:16
  48.1 4.6 %copy-start.1 = (bf16[16,4096]{1,0:T(8,128)(2,1)}, bf16[16,4096]{1,0:T(8,128)(2,1)S(1)}, u32[]{:S(2)}) copy-start(bf16[16,4096]{1,0:T(8,128)(2,1)S(1)} %collective-permute-done.10.refs_1_) | copy-start | bytes 393220
  51.3 1.4 %copy-start.2 = (bf16[16,4096]{1,0:T(8,128)(2,1)}, bf16[16,4096]{1,0:T(8,128)(2,1)S(1)}, u32[]{:S(2)}) copy-start(bf16[16,4096]{1,0:T(8,128)(2,1)S(1)} %collective-permute-done.12.refs_2_) | copy-start | bytes 393220
  52.7 0.7 %copy-start.3 = (bf16[16,4096]{1,0:T(8,128)(2,1)}, bf16[16,4096]{1,0:T(8,128)(2,1)S(1)}, u32[]{:S(2)}) copy-start(bf16[16,4096]{1,0:T(8,128)(2,1)S(1)} %collective-permute-done.14.refs_3_) | copy-start | bytes 393220

commit v2 on v0

v2 whole, which is shorter than its diff:
```python
import functools
import jax
import jax.numpy as jnp
from jax import lax
from jax.experimental import pallas as pl
from jax.experimental.pallas import tpu as pltpu
from jax.sharding import PartitionSpec as P

NT = (((1,), (1,)), ((), ()))
WHOLE = pl.BlockSpec(memory_space=pltpu.VMEM)
ANYWHERE = pl.BlockSpec(memory_space=pl.ANY)
MAIN = pl.BlockSpec(memory_space=pltpu.HBM)


def swap(block, axis, mask):
    route = [(i ^ mask, i) for i in range(lax.axis_size(axis))]
    return lax.ppermute(block, axis, route)


def cost(micros):
    return pl.CostEstimate(flops=0, bytes_accessed=int(micros * 3690e3 * 1), transcendentals=0)


def in_main(x):
    return pltpu.with_memory_space_constraint(x, pltpu.HBM)


def slot_table(labels, cap, assign, probs):
    top, toks = assign.shape
    slots = len(labels) * cap
    place = lax.broadcasted_iota(jnp.int32, (slots, toks), 0)
    label = jnp.zeros((slots, toks), jnp.int32)
    for n, expert in enumerate(labels):
        label = jnp.where(place // cap == n, expert, label)
    hit = jnp.zeros((slots, toks), jnp.float32)
    weight = jnp.zeros((slots, toks), jnp.float32)
    for k in range(top):
        same = assign[k : k + 1, :] == label
        hit = jnp.where(same, 1.0, hit)
        if probs is not None:
            weight = jnp.where(same, probs[k : k + 1, :], weight)
    first = lax.broadcasted_iota(jnp.int32, (toks, toks), 0)
    second = lax.broadcasted_iota(jnp.int32, (toks, toks), 1)
    position = jnp.dot(
        hit.astype(jnp.bfloat16),
        (first < second).astype(jnp.bfloat16),
        preferred_element_type=jnp.float32,
    )
    here = (hit > 0.0) & (position == (place % cap).astype(jnp.float32))
    return here, weight


def dispatch_kernel(masks, cap, steps, assign_ref, tok_ref, after_ref, *refs):
    outs, (table, held, sems) = refs[: len(masks)], refs[len(masks) :]
    span = held.shape[1] // steps
    columns = [slice(s * span, (s + 1) * span) for s in range(steps)]
    small = pltpu.make_async_copy(assign_ref, table, sems.at[steps])
    small.start()
    copies = [
        pltpu.make_async_copy(tok_ref.at[:, c], held.at[:, c], sems.at[s])
        for s, c in enumerate(columns)
    ]
    for copy in copies:
        copy.start()
    small.wait()
    me = lax.axis_index("dp")
    here, _ = slot_table([me ^ m for m in masks], cap, table[...], None)
    pick = here.astype(jnp.bfloat16)
    for copy, c in zip(copies, columns):
        copy.wait()
        rows = jnp.dot(pick, held[:, c], preferred_element_type=jnp.float32)
        rows = rows.astype(jnp.bfloat16)
        for n in range(len(masks)):
            outs[n][:, c] = rows[n * cap : (n + 1) * cap]


def dispatch(assign, tokens, masks, cap, after, steps=4):
    toks, width = tokens.shape
    return pl.pallas_call(
        functools.partial(dispatch_kernel, masks, cap, steps),
        out_shape=[jax.ShapeDtypeStruct((cap, width), jnp.bfloat16)] * len(masks),
        in_specs=[MAIN, MAIN, ANYWHERE],
        out_specs=[WHOLE] * len(masks),
        scratch_shapes=[
            pltpu.VMEM(assign.shape[::-1], assign.dtype),
            pltpu.VMEM((toks, width), jnp.bfloat16),
            pltpu.SemaphoreType.DMA((steps + 1,)),
        ],
        compiler_params=pltpu.CompilerParams(vmem_limit_bytes=12 * 1024 * 1024),
        cost_estimate=cost(1.0),
        name="dispatch",
    )(in_main(assign.T), in_main(tokens), after)


def prepare_kernel(
    masks, cap, assign_ref, probs_ref, slab_ref, after_ref, mix_ref, held_ref, ids, gains, sems
):
    copies = [
        pltpu.make_async_copy(assign_ref, ids, sems.at[0]),
        pltpu.make_async_copy(probs_ref, gains, sems.at[1]),
        pltpu.make_async_copy(slab_ref, held_ref, sems.at[2]),
    ]
    for copy in copies:
        copy.start()
    copies[0].wait()
    copies[1].wait()
    me = lax.axis_index("dp")
    here, weight = slot_table([me ^ m for m in masks], cap, ids[...], gains[...])
    factor = jnp.where(here, weight, 0.0).T
    high = factor.astype(jnp.bfloat16)
    rest = factor - high.astype(jnp.float32)
    middle = rest.astype(jnp.bfloat16)
    low = (rest - middle.astype(jnp.float32)).astype(jnp.bfloat16)
    mix_ref[...] = jnp.concatenate([high, middle, low], axis=1)
    copies[2].wait()


def prepare(assign, probs, slab, masks, cap, after):
    toks = assign.shape[0]
    return pl.pallas_call(
        functools.partial(prepare_kernel, masks, cap),
        out_shape=[
            jax.ShapeDtypeStruct((toks, 3 * len(masks) * cap), jnp.bfloat16),
            jax.ShapeDtypeStruct(slab.shape, slab.dtype),
        ],
        in_specs=[MAIN] * 3 + [ANYWHERE],
        out_specs=[WHOLE] * 2,
        scratch_shapes=[
            pltpu.VMEM(assign.shape[::-1], assign.dtype),
            pltpu.VMEM(probs.shape[::-1], probs.dtype),
            pltpu.SemaphoreType.DMA((3,)),
        ],
        compiler_params=pltpu.CompilerParams(vmem_limit_bytes=16 * 1024 * 1024),
        cost_estimate=cost(2.5),
        name="prepare",
    )(in_main(assign.T), in_main(probs.T), in_main(slab), after)


def expert_kernel(count, steps, *refs):
    slabs, blocks, outs, rows = refs[:2], refs[2 : 2 + count], refs[2 + count : -1], refs[-1]
    units, width = slabs[0].shape[1:]
    cap = blocks[0].shape[0]
    span = width // steps
    columns = [slice(s * span, (s + 1) * span) for s in range(steps)]
    for b in range(count):
        rows[b * cap : (b + 1) * cap, :] = blocks[b][...]
    hidden = []
    for slab in slabs:
        both = jnp.zeros((2 * units, count * cap), jnp.float32)
        for c in columns:
            both = both + lax.dot_general(
                slab[0:2, :, c].reshape(2 * units, span),
                rows[:, c],
                NT,
                preferred_element_type=jnp.float32,
            )
        hidden.append((jax.nn.silu(both[:units]) * both[units:]).astype(jnp.bfloat16))
    hidden = jnp.concatenate(hidden, axis=0).T
    for c in columns:
        down = jnp.concatenate([slab[2, :, c] for slab in slabs], axis=0)
        part = jnp.dot(hidden, down, preferred_element_type=jnp.float32)
        start = 0
        for out in outs:
            stop = start + out.shape[0]
            out[:, c] = part[start:stop].astype(out.dtype)
            start = stop


def expert_part(own, sibling, groups, chips, blocks, steps=8):
    keys = [(m, c) for group in groups for c in range(chips) for m in group]
    cap, width = blocks[keys[0]].shape
    shapes = [
        jax.ShapeDtypeStruct((len(group) * cap, width), jnp.bfloat16 if c else jnp.float32)
        for group in groups
        for c in range(chips)
    ]
    parts = pl.pallas_call(
        functools.partial(expert_kernel, len(keys), steps),
        out_shape=shapes,
        in_specs=[WHOLE] * (2 + len(keys)),
        out_specs=[WHOLE] * len(shapes),
        scratch_shapes=[pltpu.VMEM((len(keys) * cap, width), jnp.bfloat16)],
        compiler_params=pltpu.CompilerParams(
            vmem_limit_bytes=(12 + len(keys)) * 1024 * 1024
        ),
        cost_estimate=cost(2.5),
        name="experts",
    )(own, sibling, *[blocks[k] for k in keys])
    return [parts[i * chips : (i + 1) * chips] for i in range(len(groups))]


def combine_kernel(count, steps, mix_ref, *refs):
    blocks, (out_ref, held, sems) = refs[:count], refs[count:]
    span = held.shape[1] // steps
    copies = []
    for s in range(steps):
        c = slice(s * span, (s + 1) * span)
        rows = jnp.concatenate([ref[:, c] for ref in blocks] * 3, axis=0)
        held[:, c] = jnp.dot(
            mix_ref[...], rows, preferred_element_type=jnp.float32
        ).astype(jnp.bfloat16)
        copies.append(pltpu.make_async_copy(held.at[:, c], out_ref.at[:, c], sems.at[s]))
        copies[-1].start()
    for copy in copies:
        copy.wait()


def combine(mix, returned, steps=4):
    count = len(returned)
    cap, width = returned[0].shape
    toks = mix.shape[0]
    return pl.pallas_call(
        functools.partial(combine_kernel, count, steps),
        out_shape=jax.ShapeDtypeStruct((toks, width), jnp.bfloat16),
        in_specs=[WHOLE] * (1 + count),
        out_specs=ANYWHERE,
        scratch_shapes=[
            pltpu.VMEM((toks, width), jnp.bfloat16),
            pltpu.SemaphoreType.DMA((steps,)),
        ],
        compiler_params=pltpu.CompilerParams(vmem_limit_bytes=12 * 1024 * 1024),
        cost_estimate=cost(1.2),
        name="combine",
    )(mix, *returned)


def after(x, *others):
    return lax.optimization_barrier((x, *others))[0]


def total(parts, *others):
    result = parts[0]
    for c in range(1, len(parts)):
        part = after(parts[c], *others) if others else parts[c]
        result = result + swap(part, "expert", 2 * c).astype(jnp.float32)
    return result.astype(jnp.bfloat16)


def local(tokens, assign, probs, expert_weights):
    experts = lax.axis_size("dp")
    chips = lax.axis_size("expert") // 2
    cap = tokens.shape[0] // 8
    own = expert_weights[0]
    near, far = list(range(1, experts // 2)), list(range(experts // 2, experts))
    soon, late = far[: len(far) // 2], far[len(far) // 2 :]
    order = [*soon, *late, *near, 0]
    blocks = {}

    def across(m, *others):
        for c in range(1, chips):
            blocks[m, c] = swap(after(blocks[m, 0], *others), "expert", 2 * c)

    outgoing = dict(zip(order, dispatch(assign, tokens, order, cap, tokens)))
    blocks[0, 0] = outgoing[0]
    across(0)
    for m in soon + near:
        blocks[m, 0] = swap(outgoing[m], "dp", m)
    for m in late:
        blocks[m, 0] = swap(outgoing[m], "dp", m)
    sibling = swap(after(own, outgoing[0]), "expert", 1)
    mix, own = prepare(assign, probs, own, order, cap, outgoing[0])
    for m in soon:
        across(m, mix)
    for m in near:
        across(m)
    for m in late:
        across(m)
    first, second, rest, home = expert_part(own, sibling, [soon, late, near, [0]], chips, blocks)
    results = [(soon, first, ()), (late, second, ()), (near, rest, ()), ([0], home, ())]
    returned, came = {}, {}
    for group, parts, others in results:
        rows = total(parts, *(came.get(o, o) if isinstance(o, int) else o for o in others))
        came[group[-1]] = rows
        for n, m in enumerate(group):
            row = rows[n * cap : (n + 1) * cap]
            returned[m] = swap(row, "dp", m) if m else row
    return combine(mix, [returned[m] for m in order])


def solution(mesh):
    placed = (
        P(("groups", "dp", "expert"), None),
        P(("groups", "dp", "expert"), None),
        P(("groups", "dp", "expert"), None),
        P("dp", None, "expert", None),
    )
    return jax.shard_map(
        local,
        mesh=mesh,
        in_specs=placed,
        out_specs=P(("groups", "dp", "expert"), None),
        check_vma=False,
    )
```

time: 212 us -> 45.3 us (0.21)
  waiting for transfers between devices: 141 us -> 16.4 us
  local copies, waits for them, and re-layouts: 34.6 us -> 0 us
  matrix products: 14.2 us -> 0 us
  other arithmetic: 9.55 us -> 0.11 us
  starting transfers between devices: 11.8 us -> 20.7 us
  Pallas kernels: 0 us -> 7.85 us
    ppermute x3 -> x15, waiting for transfers between devices: 127 us -> 16.4 us  [swap(): return lax.ppermute(block, axis, route)]
    ppermute x3 -> x15, starting transfers between devices: 0.46 us -> 20.7 us  [swap(): return lax.ppermute(block, axis, route)]
    gather x9 -> x0, local copies, waits for them, and re-layouts: 17.4 us -> none  [the longest x8 16.5 us: combine_copies(): jnp.take(returned, jnp.minimum(slot_of[:, rank], limit), axis=0)]
    dot_general x5 -> x0, matrix products: 14.2 us -> none  [the longest x4 12 us: hidden_part(): jnp.einsum('rd,kfd->krf', rows_in, slab[:2], preferred_element_type=jnp.f...]
    all_to_all x2 -> x0, waiting for transfers between devices: 13.7 us -> none  [the longest x1 13.7 us: local(): lax.all_to_all(results, 'dp', split_axis=0, concat_axis=0, tiled=True)]
    all_to_all x2 -> x0, starting transfers between devices: 11.4 us -> none  [the longest x1 5.68 us: local(): lax.all_to_all(results, 'dp', split_axis=0, concat_axis=0, tiled=True)]
    scatter x2 -> x0, local copies, waits for them, and re-layouts: 8.61 us -> none  [the longest x1 4.3 us: routing_slots(): jnp.zeros((dump_slot + 1,), jnp.int32).at[slot_of].set(owner_token)]
    pallas_call x0 -> x4, Pallas kernels: none -> 7.85 us  [the longest x1 2.5 us: expert_part(): pl.pallas_call(functools.partial(expert_kernel, len(keys), steps), out_sh...]
  transfers between devices with their start and end apart: 5 -> 15, of which waited for: 4 -> 10; matrix products, arithmetic and copies ran while one was open for 14% -> 0% of each run, Pallas kernels for 0% -> 5%
where the time goes in v2:
time: 45.3 us; the launch traced here: 45.1 us
  starting transfers between devices  20.7 us (46%)
  waiting for transfers between devices  16.4 us (36%)
  Pallas kernels  7.85 us (17%)
    ppermute x15, starting transfers between devices, swap(): return lax.ppermute(block, axis, route)  20.7 us
    ppermute x15, waiting for transfers between devices, swap(): return lax.ppermute(block, axis, route)  16.4 us
    pallas_call x1, Pallas kernels, expert_part(): pl.pallas_call(functools.partial(expert_kernel, len(keys), steps), out_sh...  2.5 us
    pallas_call x1, Pallas kernels, prepare(): pl.pallas_call(functools.partial(prepare_kernel, masks, cap), out_shape=[...  2.39 us
    pallas_call x1, Pallas kernels, dispatch(): pl.pallas_call(functools.partial(dispatch_kernel, masks, cap, steps), out...  1.73 us
    pallas_call x1, Pallas kernels, combine(): pl.pallas_call(functools.partial(combine_kernel, count, steps), out_shape...  1.22 us
  transfers between devices with their start and end apart: 15, of which 10 were waited for; matrix products, arithmetic and copies ran while one was open for 0% of the time, Pallas kernels for 5%

profile of v2, /device:TPU:0, one launch (start us, length us, event | category | flops | bytes accessed | tf_op | source)
XLA Modules:
  0.0 45.1 jit_solution(473442202998899063)
XLA Ops:
  0.0 1.7 %dispatch.1 = (bf16[16,4096]{1,0:T(8,128)(2,1)S(1)}, bf16[16,4096]{1,0:T(8,128)(2,1)S(1)}, bf16[16,4096]{1,0:T(8,128)(2,1)S(1)}, bf16[16,4096]{1,0:T(8,128)(2,1)S(1)}) custom-call(s32[8,128]{1,0:T(8,128)} %bitcast.5, bf16[128,4096]{1,0:T(8,128)(2,1)} %after_ref.1, bf16[128,4096]{1,0:T(8,128)(2,1)} %after_ref.1), custom_call_target="tpu_custom_call" | custom-call | bytes 3690000 | tf_op jit(solution)/shard_map/dispatch/pallas_call | solution.py:79
  1.7 0.5 %collective-permute-start = (bf16[3,192,4096]{2,1,0:T(8,128)(2,1)}, bf16[3,192,4096]{2,1,0:T(8,128)(2,1)S(1)}, u32[]{:S(2)}, u32[]{:S(2)}) collective-permute-start(bf16[3,192,4096]{2,1,0:T(8,128)(2,1)} %bitcast.3), channel_id=1, source_target_pairs={{1,0},{0,1},{3,2},{2,3},{5,4},{4,5},{7,6},{6,7},{9,8},{8,9},{11,10... | collective-permute-start | bytes 14155784 | tf_op jit(solution)/shard_map/ppermute | solution.py:17
  2.3 4.7 %collective-permute-start.3 = (bf16[16,4096]{1,0:T(8,128)(2,1)S(1)}, bf16[16,4096]{1,0:T(8,128)(2,1)S(1)}, u32[]{:S(2)}, u32[]{:S(2)}) collective-permute-start(bf16[16,4096]{1,0:T(8,128)(2,1)S(1)} %get-tuple-element.27), channel_id=1, source_target_pairs={{12,0},{8,4},{4,8},{0,12},{13,1},{9,5},{5,9},{1,13},{14,2},{10,6},... | collective-permute-start | bytes 393224 | tf_op jit(solution)/shard_map/ppermute | solution.py:17
  6.9 0.0 collective-permute-start.5
  6.9 0.6 %collective-permute-start.1 = (bf16[16,4096]{1,0:T(8,128)(2,1)S(1)}, bf16[16,4096]{1,0:T(8,128)(2,1)S(1)}, u32[]{:S(2)}, u32[]{:S(2)}) collective-permute-start(bf16[16,4096]{1,0:T(8,128)(2,1)S(1)} %get-tuple-element.25), channel_id=1, source_target_pairs={{8,0},{12,4},{0,8},{4,12},{9,1},{13,5},{1,9},{5,13},{10,2},{14,6},... | collective-permute-start | bytes 393224 | tf_op jit(solution)/shard_map/ppermute | solution.py:17
  7.6 1.6 %collective-permute-start.7 = (bf16[16,4096]{1,0:T(8,128)(2,1)S(1)}, bf16[16,4096]{1,0:T(8,128)(2,1)S(1)}, u32[]{:S(2)}, u32[]{:S(2)}) collective-permute-start(bf16[16,4096]{1,0:T(8,128)(2,1)S(1)} %get-tuple-element.21.after_ref.refs_8_), channel_id=1, source_target_pairs={{2,0},{3,1},{0,2},{1,3},{6,4},{7,5},{4,6},{5,7},{10,8},{11,9},{8,1... | collective-permute-start | bytes 393224 | tf_op jit(solution)/shard_map/ppermute | solution.py:17
  9.2 2.4 %prepare.1 = (bf16[128,192]{1,0:T(8,128)(2,1)S(1)}, bf16[3,192,4096]{2,1,0:T(8,128)(2,1)S(1)}) custom-call(s32[8,128]{1,0:T(8,128)} %bitcast.6, f32[8,128]{1,0:T(8,128)} %bitcast.7, bf16[3,192,4096]{2,1,0:T(8,128)(2,1)} %bitcast.4, bf16[16,4096]{1,0:T(8,128)(2,1)S(1)} %get-tuple-element.21.after_ref.refs_8_), custom_call_target="tpu_custom_call" | custom-call | bytes 9225000 | tf_op jit(solution)/shard_map/prepare/pallas_call | solution.py:120
  11.6 0.0 collective-permute-done.3.refs_4_
  11.6 1.3 %collective-permute-start.4 = (bf16[16,4096]{1,0:T(8,128)(2,1)S(1)}, bf16[16,4096]{1,0:T(8,128)(2,1)S(1)}, u32[]{:S(2)}, u32[]{:S(2)}) collective-permute-start(bf16[16,4096]{1,0:T(8,128)(2,1)S(1)} %collective-permute-done.3.refs_4_), channel_id=1, source_target_pairs={{2,0},{3,1},{0,2},{1,3},{6,4},{7,5},{4,6},{5,7},{10,8},{11,9},{8,1... | collective-permute-start | bytes 393224 | tf_op jit(solution)/shard_map/ppermute | solution.py:17
  13.0 1.9 %collective-permute-done.5.refs_6_ = bf16[16,4096]{1,0:T(8,128)(2,1)S(1)} collective-permute-done((bf16[16,4096]{1,0:T(8,128)(2,1)S(1)}, bf16[16,4096]{1,0:T(8,128)(2,1)S(1)}, u32[]{:S(2)}, u32[]{:S(2)}) %collective-permute-start.5) | collective-permute-done | bytes 131104 | tf_op jit(solution)/shard_map/ppermute | solution.py:17
  14.9 1.5 %collective-permute-start.6 = (bf16[16,4096]{1,0:T(8,128)(2,1)S(1)}, bf16[16,4096]{1,0:T(8,128)(2,1)S(1)}, u32[]{:S(2)}, u32[]{:S(2)}) collective-permute-start(bf16[16,4096]{1,0:T(8,128)(2,1)S(1)} %collective-permute-done.5.refs_6_), channel_id=1, source_target_pairs={{2,0},{3,1},{0,2},{1,3},{6,4},{7,5},{4,6},{5,7},{10,8},{11,9},{8,1... | collective-permute-start | bytes 393224 | tf_op jit(solution)/shard_map/ppermute | solution.py:17
  16.4 2.2 %collective-permute-done.1.refs_2_ = bf16[16,4096]{1,0:T(8,128)(2,1)S(1)} collective-permute-done((bf16[16,4096]{1,0:T(8,128)(2,1)S(1)}, bf16[16,4096]{1,0:T(8,128)(2,1)S(1)}, u32[]{:S(2)}, u32[]{:S(2)}) %collective-permute-start.1) | collective-permute-done | bytes 131104 | tf_op jit(solution)/shard_map/ppermute | solution.py:17
  18.6 1.5 %collective-permute-start.2 = (bf16[16,4096]{1,0:T(8,128)(2,1)S(1)}, bf16[16,4096]{1,0:T(8,128)(2,1)S(1)}, u32[]{:S(2)}, u32[]{:S(2)}) collective-permute-start(bf16[16,4096]{1,0:T(8,128)(2,1)S(1)} %collective-permute-done.1.refs_2_), channel_id=1, source_target_pairs={{2,0},{3,1},{0,2},{1,3},{6,4},{7,5},{4,6},{5,7},{10,8},{11,9},{8,1... | collective-permute-start | bytes 393224 | tf_op jit(solution)/shard_map/ppermute | solution.py:17
  20.1 0.0 collective-permute-done.7.refs_9_
  20.1 0.0 collective-permute-done.4.refs_5_
  20.1 0.2 collective-permute-done.6.refs_7_
  20.3 3.3 %collective-permute-done.2.refs_3_ = bf16[16,4096]{1,0:T(8,128)(2,1)S(1)} collective-permute-done((bf16[16,4096]{1,0:T(8,128)(2,1)S(1)}, bf16[16,4096]{1,0:T(8,128)(2,1)S(1)}, u32[]{:S(2)}, u32[]{:S(2)}) %collective-permute-start.2) | collective-permute-done | bytes 131104 | tf_op jit(solution)/shard_map/ppermute | solution.py:17
  23.7 0.0 collective-permute-done.refs_1_
  23.7 2.5 %experts.1 = (f32[16,4096]{1,0:T(8,128)S(1)}, bf16[16,4096]{1,0:T(8,128)(2,1)S(1)}, f32[16,4096]{1,0:T(8,128)S(1)}, bf16[16,4096]{1,0:T(8,128)(2,1)S(1)}, f32[16...) custom-call(bf16[3,192,4096]{2,1,0:T(8,128)(2,1)S(1)} %get-tuple-element, ...), custom_call_target="tpu_custom_call" | custom-call | bytes 9225000 | tf_op jit(solution)/shard_map/experts/pallas_call | solution.py:177
  26.2 1.6 %collective-permute-start.8 = (bf16[16,4096]{1,0:T(8,128)(2,1)S(1)}, bf16[16,4096]{1,0:T(8,128)(2,1)S(1)}, u32[]{:S(2)}, u32[]{:S(2)}) collective-permute-start(bf16[16,4096]{1,0:T(8,128)(2,1)S(1)} %get-tuple-element.30), channel_id=1, source_target_pairs={{2,0},{3,1},{0,2},{1,3},{6,4},{7,5},{4,6},{5,7},{10,8},{11,9},{8,1... | collective-permute-start | bytes 393224 | tf_op jit(solution)/shard_map/ppermute | solution.py:17
  27.8 0.5 %collective-permute-start.10 = (bf16[16,4096]{1,0:T(8,128)(2,1)S(1)}, bf16[16,4096]{1,0:T(8,128)(2,1)S(1)}, u32[]{:S(2)}, u32[]{:S(2)}) collective-permute-start(bf16[16,4096]{1,0:T(8,128)(2,1)S(1)} %get-tuple-element.32), channel_id=1, source_target_pairs={{2,0},{3,1},{0,2},{1,3},{6,4},{7,5},{4,6},{5,7},{10,8},{11,9},{8,1... | collective-permute-start | bytes 393224 | tf_op jit(solution)/shard_map/ppermute | solution.py:17
  28.3 1.5 %collective-permute-start.12 = (bf16[16,4096]{1,0:T(8,128)(2,1)S(1)}, bf16[16,4096]{1,0:T(8,128)(2,1)S(1)}, u32[]{:S(2)}, u32[]{:S(2)}) collective-permute-start(bf16[16,4096]{1,0:T(8,128)(2,1)S(1)} %get-tuple-element.34), channel_id=1, source_target_pairs={{2,0},{3,1},{0,2},{1,3},{6,4},{7,5},{4,6},{5,7},{10,8},{11,9},{8,1... | collective-permute-start | bytes 393224 | tf_op jit(solution)/shard_map/ppermute | solution.py:17
  29.8 0.5 %collective-permute-start.14 = (bf16[16,4096]{1,0:T(8,128)(2,1)S(1)}, bf16[16,4096]{1,0:T(8,128)(2,1)S(1)}, u32[]{:S(2)}, u32[]{:S(2)}) collective-permute-start(bf16[16,4096]{1,0:T(8,128)(2,1)S(1)} %get-tuple-element.36), channel_id=1, source_target_pairs={{2,0},{3,1},{0,2},{1,3},{6,4},{7,5},{4,6},{5,7},{10,8},{11,9},{8,1... | collective-permute-start | bytes 393224 | tf_op jit(solution)/shard_map/ppermute | solution.py:17
  30.3 2.4 %collective-permute-done.8 = bf16[16,4096]{1,0:T(8,128)(2,1)S(1)} collective-permute-done((bf16[16,4096]{1,0:T(8,128)(2,1)S(1)}, bf16[16,4096]{1,0:T(8,128)(2,1)S(1)}, u32[]{:S(2)}, u32[]{:S(2)}) %collective-permute-start.8) | collective-permute-done | bytes 131104 | tf_op jit(solution)/shard_map/ppermute | solution.py:17
  32.7 1.6 %collective-permute-start.9 = (bf16[16,4096]{1,0:T(8,128)(2,1)S(1)}, bf16[16,4096]{1,0:T(8,128)(2,1)S(1)}, u32[]{:S(2)}, u32[]{:S(2)}) collective-permute-start(bf16[16,4096]{1,0:T(8,128)(2,1)S(1)} %add_convert_fusion.3), channel_id=1, source_target_pairs={{8,0},{12,4},{0,8},{4,12},{9,1},{13,5},{1,9},{5,13},{10,2},{14,6},... | collective-permute-start | bytes 393224 | tf_op jit(solution)/shard_map/ppermute | solution.py:17
  34.3 1.2 %collective-permute-done.10 = bf16[16,4096]{1,0:T(8,128)(2,1)S(1)} collective-permute-done((bf16[16,4096]{1,0:T(8,128)(2,1)S(1)}, bf16[16,4096]{1,0:T(8,128)(2,1)S(1)}, u32[]{:S(2)}, u32[]{:S(2)}) %collective-permute-start.10) | collective-permute-done | bytes 131104 | tf_op jit(solution)/shard_map/ppermute | solution.py:17
  35.5 2.5 %collective-permute-start.11 = (bf16[16,4096]{1,0:T(8,128)(2,1)S(1)}, bf16[16,4096]{1,0:T(8,128)(2,1)S(1)}, u32[]{:S(2)}, u32[]{:S(2)}) collective-permute-start(bf16[16,4096]{1,0:T(8,128)(2,1)S(1)} %add_convert_fusion.2), channel_id=1, source_target_pairs={{12,0},{8,4},{4,8},{0,12},{13,1},{9,5},{5,9},{1,13},{14,2},{10,6},... | collective-permute-start | bytes 393224 | tf_op jit(solution)/shard_map/ppermute | solution.py:17
  38.1 0.0 collective-permute-done.12
  38.1 0.6 %collective-permute-start.13 = (bf16[16,4096]{1,0:T(8,128)(2,1)S(1)}, bf16[16,4096]{1,0:T(8,128)(2,1)S(1)}, u32[]{:S(2)}, u32[]{:S(2)}) collective-permute-start(bf16[16,4096]{1,0:T(8,128)(2,1)S(1)} %add_convert_fusion.1), channel_id=1, source_target_pairs={{4,0},{0,4},{12,8},{8,12},{5,1},{1,5},{13,9},{9,13},{6,2},{2,6},{1... | collective-permute-start | bytes 393224 | tf_op jit(solution)/shard_map/ppermute | solution.py:17
  38.7 0.1 collective-permute-done.14
  38.9 2.0 %collective-permute-done.9.refs_0_ = bf16[16,4096]{1,0:T(8,128)(2,1)S(1)} collective-permute-done((bf16[16,4096]{1,0:T(8,128)(2,1)S(1)}, bf16[16,4096]{1,0:T(8,128)(2,1)S(1)}, u32[]{:S(2)}, u32[]{:S(2)}) %collective-permute-start.9) | collective-permute-done | bytes 131104 | tf_op jit(solution)/shard_map/ppermute | solution.py:17
  40.9 1.7 %collective-permute-done.11.refs_1_ = bf16[16,4096]{1,0:T(8,128)(2,1)S(1)} collective-permute-done((bf16[16,4096]{1,0:T(8,128)(2,1)S(1)}, bf16[16,4096]{1,0:T(8,128)(2,1)S(1)}, u32[]{:S(2)}, u32[]{:S(2)}) %collective-permute-start.11) | collective-permute-done | bytes 131104 | tf_op jit(solution)/shard_map/ppermute | solution.py:17
  42.5 1.3 %collective-permute-done.13.refs_2_ = bf16[16,4096]{1,0:T(8,128)(2,1)S(1)} collective-permute-done((bf16[16,4096]{1,0:T(8,128)(2,1)S(1)}, bf16[16,4096]{1,0:T(8,128)(2,1)S(1)}, u32[]{:S(2)}, u32[]{:S(2)}) %collective-permute-start.13) | collective-permute-done | bytes 131104 | tf_op jit(solution)/shard_map/ppermute | solution.py:17
  43.9 1.2 %combine.1 = bf16[128,4096]{1,0:T(8,128)(2,1)} custom-call(bf16[128,192]{1,0:T(8,128)(2,1)S(1)} %get-tuple-element.22.mix_ref, bf16[16,4096]{1,0:T(8,128)(2,1)S(1)} %collective-permute-done.9.refs_0_, bf16[16,4096]{1,0:T(8,128)(2,1)S(1)} %collective-permute-done.11.refs_1_, bf16[16,4096]{1,0:T(8,128)(2,1)S(1)} %collective-permute-done.13.refs_2_, ...), custom_call_target="tpu_custom_call" | custom-call | bytes 4428000 | tf_op jit(solution)/shard_map/combine/pallas_call | solution.py:212
  (4 shorter events, 0.1 us)
Async XLA Ops:
  1.7 21.9 %collective-permute-start = (bf16[3,192,4096]{2,1,0:T(8,128)(2,1)}, bf16[3,192,4096]{2,1,0:T(8,128)(2,1)S(1)}, u32[]{:S(2)}, u32[]{:S(2)}) collective-permute-start(bf16[3,192,4096]{2,1,0:T(8,128)(2,1)} %bitcast.3), channel_id=1, source_target_pairs={{1,0},{0,1},{3,2},{2,3},{5,4},{4,5},{7,6},{6,7},{9,8},{8,9},{11,10... | collective-permute-start | bytes 14155784 | tf_op jit(solution)/shard_map/ppermute | solution.py:17
  2.3 9.4 %collective-permute-start.3 = (bf16[16,4096]{1,0:T(8,128)(2,1)S(1)}, bf16[16,4096]{1,0:T(8,128)(2,1)S(1)}, u32[]{:S(2)}, u32[]{:S(2)}) collective-permute-start(bf16[16,4096]{1,0:T(8,128)(2,1)S(1)} %get-tuple-element.27), channel_id=1, source_target_pairs={{12,0},{8,4},{4,8},{0,12},{13,1},{9,5},{5,9},{1,13},{14,2},{10,6},... | collective-permute-start | bytes 393224 | tf_op jit(solution)/shard_map/ppermute | solution.py:17
  6.9 8.0 %collective-permute-start.5 = (bf16[16,4096]{1,0:T(8,128)(2,1)S(1)}, bf16[16,4096]{1,0:T(8,128)(2,1)S(1)}, u32[]{:S(2)}, u32[]{:S(2)}) collective-permute-start(bf16[16,4096]{1,0:T(8,128)(2,1)S(1)} %get-tuple-element.28), channel_id=1, source_target_pairs={{4,0},{0,4},{12,8},{8,12},{5,1},{1,5},{13,9},{9,13},{6,2},{2,6},{1... | collective-permute-start | bytes 393224 | tf_op jit(solution)/shard_map/ppermute | solution.py:17
  6.9 11.7 %collective-permute-start.1 = (bf16[16,4096]{1,0:T(8,128)(2,1)S(1)}, bf16[16,4096]{1,0:T(8,128)(2,1)S(1)}, u32[]{:S(2)}, u32[]{:S(2)}) collective-permute-start(bf16[16,4096]{1,0:T(8,128)(2,1)S(1)} %get-tuple-element.25), channel_id=1, source_target_pairs={{8,0},{12,4},{0,8},{4,12},{9,1},{13,5},{1,9},{5,13},{10,2},{14,6},... | collective-permute-start | bytes 393224 | tf_op jit(solution)/shard_map/ppermute | solution.py:17
  7.6 12.5 %collective-permute-start.7 = (bf16[16,4096]{1,0:T(8,128)(2,1)S(1)}, bf16[16,4096]{1,0:T(8,128)(2,1)S(1)}, u32[]{:S(2)}, u32[]{:S(2)}) collective-permute-start(bf16[16,4096]{1,0:T(8,128)(2,1)S(1)} %get-tuple-element.21.after_ref.refs_8_), channel_id=1, source_target_pairs={{2,0},{3,1},{0,2},{1,3},{6,4},{7,5},{4,6},{5,7},{10,8},{11,9},{8,1... | collective-permute-start | bytes 393224 | tf_op jit(solution)/shard_map/ppermute | solution.py:17
  11.6 8.5 %collective-permute-start.4 = (bf16[16,4096]{1,0:T(8,128)(2,1)S(1)}, bf16[16,4096]{1,0:T(8,128)(2,1)S(1)}, u32[]{:S(2)}, u32[]{:S(2)}) collective-permute-start(bf16[16,4096]{1,0:T(8,128)(2,1)S(1)} %collective-permute-done.3.refs_4_), channel_id=1, source_target_pairs={{2,0},{3,1},{0,2},{1,3},{6,4},{7,5},{4,6},{5,7},{10,8},{11,9},{8,1... | collective-permute-start | bytes 393224 | tf_op jit(solution)/shard_map/ppermute | solution.py:17
  14.9 5.4 %collective-permute-start.6 = (bf16[16,4096]{1,0:T(8,128)(2,1)S(1)}, bf16[16,4096]{1,0:T(8,128)(2,1)S(1)}, u32[]{:S(2)}, u32[]{:S(2)}) collective-permute-start(bf16[16,4096]{1,0:T(8,128)(2,1)S(1)} %collective-permute-done.5.refs_6_), channel_id=1, source_target_pairs={{2,0},{3,1},{0,2},{1,3},{6,4},{7,5},{4,6},{5,7},{10,8},{11,9},{8,1... | collective-permute-start | bytes 393224 | tf_op jit(solution)/shard_map/ppermute | solution.py:17
  18.6 5.1 %collective-permute-start.2 = (bf16[16,4096]{1,0:T(8,128)(2,1)S(1)}, bf16[16,4096]{1,0:T(8,128)(2,1)S(1)}, u32[]{:S(2)}, u32[]{:S(2)}) collective-permute-start(bf16[16,4096]{1,0:T(8,128)(2,1)S(1)} %collective-permute-done.1.refs_2_), channel_id=1, source_target_pairs={{2,0},{3,1},{0,2},{1,3},{6,4},{7,5},{4,6},{5,7},{10,8},{11,9},{8,1... | collective-permute-start | bytes 393224 | tf_op jit(solution)/shard_map/ppermute | solution.py:17
  26.2 6.5 %collective-permute-start.8 = (bf16[16,4096]{1,0:T(8,128)(2,1)S(1)}, bf16[16,4096]{1,0:T(8,128)(2,1)S(1)}, u32[]{:S(2)}, u32[]{:S(2)}) collective-permute-start(bf16[16,4096]{1,0:T(8,128)(2,1)S(1)} %get-tuple-element.30), channel_id=1, source_target_pairs={{2,0},{3,1},{0,2},{1,3},{6,4},{7,5},{4,6},{5,7},{10,8},{11,9},{8,1... | collective-permute-start | bytes 393224 | tf_op jit(solution)/shard_map/ppermute | solution.py:17
  27.8 7.7 %collective-permute-start.10 = (bf16[16,4096]{1,0:T(8,128)(2,1)S(1)}, bf16[16,4096]{1,0:T(8,128)(2,1)S(1)}, u32[]{:S(2)}, u32[]{:S(2)}) collective-permute-start(bf16[16,4096]{1,0:T(8,128)(2,1)S(1)} %get-tuple-element.32), channel_id=1, source_target_pairs={{2,0},{3,1},{0,2},{1,3},{6,4},{7,5},{4,6},{5,7},{10,8},{11,9},{8,1... | collective-permute-start | bytes 393224 | tf_op jit(solution)/shard_map/ppermute | solution.py:17
  28.3 9.8 %collective-permute-start.12 = (bf16[16,4096]{1,0:T(8,128)(2,1)S(1)}, bf16[16,4096]{1,0:T(8,128)(2,1)S(1)}, u32[]{:S(2)}, u32[]{:S(2)}) collective-permute-start(bf16[16,4096]{1,0:T(8,128)(2,1)S(1)} %get-tuple-element.34), channel_id=1, source_target_pairs={{2,0},{3,1},{0,2},{1,3},{6,4},{7,5},{4,6},{5,7},{10,8},{11,9},{8,1... | collective-permute-start | bytes 393224 | tf_op jit(solution)/shard_map/ppermute | solution.py:17
  29.8 9.1 %collective-permute-start.14 = (bf16[16,4096]{1,0:T(8,128)(2,1)S(1)}, bf16[16,4096]{1,0:T(8,128)(2,1)S(1)}, u32[]{:S(2)}, u32[]{:S(2)}) collective-permute-start(bf16[16,4096]{1,0:T(8,128)(2,1)S(1)} %get-tuple-element.36), channel_id=1, source_target_pairs={{2,0},{3,1},{0,2},{1,3},{6,4},{7,5},{4,6},{5,7},{10,8},{11,9},{8,1... | collective-permute-start | bytes 393224 | tf_op jit(solution)/shard_map/ppermute | solution.py:17
  32.7 8.2 %collective-permute-start.9 = (bf16[16,4096]{1,0:T(8,128)(2,1)S(1)}, bf16[16,4096]{1,0:T(8,128)(2,1)S(1)}, u32[]{:S(2)}, u32[]{:S(2)}) collective-permute-start(bf16[16,4096]{1,0:T(8,128)(2,1)S(1)} %add_convert_fusion.3), channel_id=1, source_target_pairs={{8,0},{12,4},{0,8},{4,12},{9,1},{13,5},{1,9},{5,13},{10,2},{14,6},... | collective-permute-start | bytes 393224 | tf_op jit(solution)/shard_map/ppermute | solution.py:17
  35.5 7.0 %collective-permute-start.11 = (bf16[16,4096]{1,0:T(8,128)(2,1)S(1)}, bf16[16,4096]{1,0:T(8,128)(2,1)S(1)}, u32[]{:S(2)}, u32[]{:S(2)}) collective-permute-start(bf16[16,4096]{1,0:T(8,128)(2,1)S(1)} %add_convert_fusion.2), channel_id=1, source_target_pairs={{12,0},{8,4},{4,8},{0,12},{13,1},{9,5},{5,9},{1,13},{14,2},{10,6},... | collective-permute-start | bytes 393224 | tf_op jit(solution)/shard_map/ppermute | solution.py:17
  38.1 5.8 %collective-permute-start.13 = (bf16[16,4096]{1,0:T(8,128)(2,1)S(1)}, bf16[16,4096]{1,0:T(8,128)(2,1)S(1)}, u32[]{:S(2)}, u32[]{:S(2)}) collective-permute-start(bf16[16,4096]{1,0:T(8,128)(2,1)S(1)} %add_convert_fusion.1), channel_id=1, source_target_pairs={{4,0},{0,4},{12,8},{8,12},{5,1},{1,5},{13,9},{9,13},{6,2},{2,6},{1... | collective-permute-start | bytes 393224 | tf_op jit(solution)/shard_map/ppermute | solution.py:17

commit v3 on v2

--- a/solution.py
+++ b/solution.py
@@ -18,7 +18,7 @@
 
 
 def cost(micros):
-    return pl.CostEstimate(flops=0, bytes_accessed=int(micros * 3690e3 * 1), transcendentals=0)
+    return pl.CostEstimate(flops=0, bytes_accessed=int(micros * 3690e3), transcendentals=0)
 
 
 def in_main(x):
@@ -50,7 +50,7 @@
     return here, weight
 
 
-def dispatch_kernel(masks, cap, steps, assign_ref, tok_ref, after_ref, *refs):
+def dispatch_kernel(masks, cap, steps, assign_ref, tok_ref, *refs):
     outs, (table, held, sems) = refs[: len(masks)], refs[len(masks) :]
     span = held.shape[1] // steps
     columns = [slice(s * span, (s + 1) * span) for s in range(steps)]
@@ -74,12 +74,12 @@
             outs[n][:, c] = rows[n * cap : (n + 1) * cap]
 
 
-def dispatch(assign, tokens, masks, cap, after, steps=4):
+def dispatch(assign, tokens, masks, cap, steps=2):
     toks, width = tokens.shape
     return pl.pallas_call(
         functools.partial(dispatch_kernel, masks, cap, steps),
         out_shape=[jax.ShapeDtypeStruct((cap, width), jnp.bfloat16)] * len(masks),
-        in_specs=[MAIN, MAIN, ANYWHERE],
+        in_specs=[MAIN, MAIN],
         out_specs=[WHOLE] * len(masks),
         scratch_shapes=[
             pltpu.VMEM(assign.shape[::-1], assign.dtype),
@@ -89,7 +89,7 @@
         compiler_params=pltpu.CompilerParams(vmem_limit_bytes=12 * 1024 * 1024),
         cost_estimate=cost(1.0),
         name="dispatch",
-    )(in_main(assign.T), in_main(tokens), after)
+    )(in_main(assign.T), in_main(tokens))
 
 
 def prepare_kernel(
@@ -166,15 +166,11 @@
             start = stop
 
 
-def expert_part(own, sibling, groups, chips, blocks, steps=8):
-    keys = [(m, c) for group in groups for c in range(chips) for m in group]
+def expert_part(own, sibling, blocks, wanted, steps=8):
+    keys = [key for some, _ in wanted for key in some]
     cap, width = blocks[keys[0]].shape
-    shapes = [
-        jax.ShapeDtypeStruct((len(group) * cap, width), jnp.bfloat16 if c else jnp.float32)
-        for group in groups
-        for c in range(chips)
-    ]
-    parts = pl.pallas_call(
+    shapes = [jax.ShapeDtypeStruct((len(some) * cap, width), kind) for some, kind in wanted]
+    return pl.pallas_call(
         functools.partial(expert_kernel, len(keys), steps),
         out_shape=shapes,
         in_specs=[WHOLE] * (2 + len(keys)),
@@ -186,18 +182,23 @@
         cost_estimate=cost(2.5),
         name="experts",
     )(own, sibling, *[blocks[k] for k in keys])
-    return [parts[i * chips : (i + 1) * chips] for i in range(len(groups))]
-
-
-def combine_kernel(count, steps, mix_ref, *refs):
-    blocks, (out_ref, held, sems) = refs[:count], refs[count:]
+
+
+def combine_kernel(count, near, chips, steps, mix_ref, *refs):
+    blocks, home, pairs = refs[:count], refs[count], refs[count + 1 : count + 1 + near]
+    gots, (out_ref, held, sems) = refs[count + 1 + near : -3], refs[-3:]
     span = held.shape[1] // steps
     copies = []
     for s in range(steps):
         c = slice(s * span, (s + 1) * span)
-        rows = jnp.concatenate([ref[:, c] for ref in blocks] * 3, axis=0)
+        homes = [home[:, c]] + [pair[:, c].astype(jnp.float32) for pair in pairs]
+        homes = jnp.concatenate(homes, axis=0)
+        for n in range(chips - 1):
+            group = gots[n * (near + 1) : (n + 1) * (near + 1)]
+            homes = homes + jnp.concatenate([got[:, c] for got in group], axis=0).astype(jnp.float32)
+        rows = jnp.concatenate([ref[:, c] for ref in blocks] + [homes.astype(jnp.bfloat16)], axis=0)
         held[:, c] = jnp.dot(
-            mix_ref[...], rows, preferred_element_type=jnp.float32
+            mix_ref[...], jnp.concatenate([rows] * 3, axis=0), preferred_element_type=jnp.float32
         ).astype(jnp.bfloat16)
         copies.append(pltpu.make_async_copy(held.at[:, c], out_ref.at[:, c], sems.at[s]))
         copies[-1].start()
@@ -205,14 +206,15 @@
         copy.wait()
 
 
-def combine(mix, returned, steps=4):
-    count = len(returned)
-    cap, width = returned[0].shape
+def combine(mix, returned, home, pairs, gots, steps=4):
+    count, near, chips = len(returned), len(pairs), lax.axis_size("expert") // 2
+    width = home.shape[1]
     toks = mix.shape[0]
+    arrays = [mix, *returned, home, *pairs, *gots]
     return pl.pallas_call(
-        functools.partial(combine_kernel, count, steps),
+        functools.partial(combine_kernel, count, near, chips, steps),
         out_shape=jax.ShapeDtypeStruct((toks, width), jnp.bfloat16),
-        in_specs=[WHOLE] * (1 + count),
+        in_specs=[WHOLE] * len(arrays),
         out_specs=ANYWHERE,
         scratch_shapes=[
             pltpu.VMEM((toks, width), jnp.bfloat16),
@@ -221,19 +223,11 @@
         compiler_params=pltpu.CompilerParams(vmem_limit_bytes=12 * 1024 * 1024),
         cost_estimate=cost(1.2),
         name="combine",
-    )(mix, *returned)
+    )(*arrays)
 
 
 def after(x, *others):
     return lax.optimization_barrier((x, *others))[0]
-
-
-def total(parts, *others):
-    result = parts[0]
-    for c in range(1, len(parts)):
-        part = after(parts[c], *others) if others else parts[c]
-        result = result + swap(part, "expert", 2 * c).astype(jnp.float32)
-    return result.astype(jnp.bfloat16)
 
 
 def local(tokens, assign, probs, expert_weights):
@@ -243,38 +237,65 @@
     own = expert_weights[0]
     near, far = list(range(1, experts // 2)), list(range(experts // 2, experts))
     soon, late = far[: len(far) // 2], far[len(far) // 2 :]
-    order = [*soon, *late, *near, 0]
-    blocks = {}
-
-    def across(m, *others):
-        for c in range(1, chips):
-            blocks[m, c] = swap(after(blocks[m, 0], *others), "expert", 2 * c)
-
-    outgoing = dict(zip(order, dispatch(assign, tokens, order, cap, tokens)))
-    blocks[0, 0] = outgoing[0]
+    others = range(1, chips)
+
+    leave = [*soon, *late, *near, 0]
+    outgoing = dict(zip(leave, dispatch(assign, tokens, leave, cap)))
+    blocks = {(0, 0): outgoing[0]}
+
+    def across(m, *before):
+        for c in others:
+            blocks[m, c] = swap(after(blocks[m, 0], *before), "expert", 2 * c)
+
     across(0)
-    for m in soon + near:
-        blocks[m, 0] = swap(outgoing[m], "dp", m)
-    for m in late:
+    for m in [*soon, *near, *late]:
         blocks[m, 0] = swap(outgoing[m], "dp", m)
     sibling = swap(after(own, outgoing[0]), "expert", 1)
-    mix, own = prepare(assign, probs, own, order, cap, outgoing[0])
+    order = [*soon, *late, 0, *near]
+    mix, own = prepare(assign, probs, own, order, cap, blocks[0, chips - 1])
     for m in soon:
         across(m, mix)
+    for m in [*near, *late]:
+        across(m)
+
+    def share(m, home=jnp.float32):
+        return {(m, c): jnp.bfloat16 if c else home for c in range(chips)}
+
+    def compute(wanted):
+        kinds = [([key], kind) for key, kind in wanted.items()]
+        return dict(zip(wanted, expert_part(own, sibling, blocks, kinds)))
+
+    wanted = {}
+    for m in late:
+        wanted |= share(m)
+    parts = compute(wanted)
+    came = {(m, c): swap(parts[m, c], "expert", 2 * c) for m in late for c in others}
+    blocks[soon[0], 0] = after(blocks[soon[0], 0], parts[late[0], 0])
+    wanted = {}
+    for m in soon:
+        wanted |= share(m)
     for m in near:
-        across(m)
-    for m in late:
-        across(m)
-    first, second, rest, home = expert_part(own, sibling, [soon, late, near, [0]], chips, blocks)
-    results = [(soon, first, ()), (late, second, ()), (near, rest, ()), ([0], home, ())]
-    returned, came = {}, {}
-    for group, parts, others in results:
-        rows = total(parts, *(came.get(o, o) if isinstance(o, int) else o for o in others))
-        came[group[-1]] = rows
-        for n, m in enumerate(group):
-            row = rows[n * cap : (n + 1) * cap]
-            returned[m] = swap(row, "dp", m) if m else row
-    return combine(mix, [returned[m] for m in order])
+        wanted |= share(m, jnp.bfloat16)
+    parts |= compute(wanted | share(0))
+    first = came[late[-1], chips - 1]
+    for m in soon:
+        for c in others:
+            came[m, c] = swap(after(parts[m, c], came[late[0], c]), "expert", 2 * c)
+
+    pairs = [[swap(after(parts[m, c], first), "dp", m) for c in range(chips)] for m in near]
+    returned = {}
+    for m in [*late, *soon]:
+        row = parts[m, 0]
+        for c in others:
+            row = row + came[m, c].astype(jnp.float32)
+        returned[m] = swap(row.astype(jnp.bfloat16), "dp", m)
+    homes = {c: swap(after(parts[0, c], first), "expert", 2 * c) for c in others}
+    gots = []
+    for c in others:
+        gots += [homes[c]] + [swap(pair[c], "expert", 2 * c) for pair in pairs]
+    return combine(
+        mix, [returned[m] for m in [*soon, *late]], parts[0, 0], [pair[0] for pair in pairs], gots
+    )
 
 
 def solution(mesh):

time: 45.3 us -> 42.6 us (0.940)
  waiting for transfers between devices: 16.4 us -> 10.9 us
  Pallas kernels: 7.85 us -> 10.1 us
  starting transfers between devices: 20.7 us -> 21.3 us
    ppermute x15 -> x16, waiting for transfers between devices: 16.4 us -> 10.9 us  [swap(): return lax.ppermute(block, axis, route)]
    pallas_call x1 -> x2, Pallas kernels: 2.5 us -> 4.94 us  [expert_part(): pl.pallas_call(functools.partial(expert_kernel, len(keys), steps), out_sh...]
    ppermute x15 -> x16, starting transfers between devices: 20.7 us -> 21.3 us  [swap(): return lax.ppermute(block, axis, route)]
  transfers between devices with their start and end apart: 15 -> 16, of which waited for: 10 -> 9; matrix products, arithmetic and copies ran while one was open for 0% -> 0% of each run, Pallas kernels for 5% -> 17%
where the time goes in v3:
time: 42.6 us; the launch traced here: 42.4 us
  starting transfers between devices  21.3 us (50%)
  waiting for transfers between devices  10.9 us (26%)
  Pallas kernels  10.1 us (24%)
    ppermute x16, starting transfers between devices, swap(): return lax.ppermute(block, axis, route)  21.3 us
    ppermute x16, waiting for transfers between devices, swap(): return lax.ppermute(block, axis, route)  10.9 us
    pallas_call x2, Pallas kernels, expert_part(): pl.pallas_call(functools.partial(expert_kernel, len(keys), steps), out_sh...  4.94 us
    pallas_call x1, Pallas kernels, prepare(): pl.pallas_call(functools.partial(prepare_kernel, masks, cap), out_shape=[...  2.4 us
    pallas_call x1, Pallas kernels, dispatch(): pl.pallas_call(functools.partial(dispatch_kernel, masks, cap, steps), out...  1.53 us
    pallas_call x1, Pallas kernels, combine(): pl.pallas_call(functools.partial(combine_kernel, count, near, chips, step...  1.23 us
  transfers between devices with their start and end apart: 16, of which 9 were waited for; matrix products, arithmetic and copies ran while one was open for 0% of the time, Pallas kernels for 17%

profile of v3, /device:TPU:0, one launch (start us, length us, event | category | flops | bytes accessed | tf_op | source)
XLA Modules:
  0.0 42.4 jit_solution(15252397336380025734)
XLA Ops:
  0.0 1.5 %dispatch.1 = (bf16[16,4096]{1,0:T(8,128)(2,1)S(1)}, bf16[16,4096]{1,0:T(8,128)(2,1)S(1)}, bf16[16,4096]{1,0:T(8,128)(2,1)S(1)}, bf16[16,4096]{1,0:T(8,128)(2,1)S(1)}) custom-call(s32[8,128]{1,0:T(8,128)} %bitcast.5, bf16[128,4096]{1,0:T(8,128)(2,1)} %tok_ref.1), custom_call_target="tpu_custom_call" | custom-call | bytes 3690000 | tf_op jit(solution)/shard_map/dispatch/pallas_call | solution.py:79
  1.5 0.5 %collective-permute-start.1 = (bf16[3,192,4096]{2,1,0:T(8,128)(2,1)}, bf16[3,192,4096]{2,1,0:T(8,128)(2,1)S(1)}, u32[]{:S(2)}, u32[]{:S(2)}) collective-permute-start(bf16[3,192,4096]{2,1,0:T(8,128)(2,1)} %bitcast.3), channel_id=1, source_target_pairs={{1,0},{0,1},{3,2},{2,3},{5,4},{4,5},{7,6},{6,7},{9,8},{8,9},{11,10... | collective-permute-start | bytes 14155784 | tf_op jit(solution)/shard_map/ppermute | solution.py:17
  2.1 4.7 %collective-permute-start.3 = (bf16[16,4096]{1,0:T(8,128)(2,1)S(1)}, bf16[16,4096]{1,0:T(8,128)(2,1)S(1)}, u32[]{:S(2)}, u32[]{:S(2)}) collective-permute-start(bf16[16,4096]{1,0:T(8,128)(2,1)S(1)} %get-tuple-element.31), channel_id=1, source_target_pairs={{12,0},{8,4},{4,8},{0,12},{13,1},{9,5},{5,9},{1,13},{14,2},{10,6},... | collective-permute-start | bytes 393224 | tf_op jit(solution)/shard_map/ppermute | solution.py:17
  6.7 0.0 collective-permute-start.6
  6.7 1.5 %collective-permute-start = (bf16[16,4096]{1,0:T(8,128)(2,1)S(1)}, bf16[16,4096]{1,0:T(8,128)(2,1)S(1)}, u32[]{:S(2)}, u32[]{:S(2)}) collective-permute-start(bf16[16,4096]{1,0:T(8,128)(2,1)S(1)} %get-tuple-element.26.refs_6_), channel_id=1, source_target_pairs={{2,0},{3,1},{0,2},{1,3},{6,4},{7,5},{4,6},{5,7},{10,8},{11,9},{8,1... | collective-permute-start | bytes 393224 | tf_op jit(solution)/shard_map/ppermute | solution.py:17
  8.2 0.8 %collective-permute-start.2 = (bf16[16,4096]{1,0:T(8,128)(2,1)S(1)}, bf16[16,4096]{1,0:T(8,128)(2,1)S(1)}, u32[]{:S(2)}, u32[]{:S(2)}) collective-permute-start(bf16[16,4096]{1,0:T(8,128)(2,1)S(1)} %get-tuple-element.30), channel_id=1, source_target_pairs={{8,0},{12,4},{0,8},{4,12},{9,1},{13,5},{1,9},{5,13},{10,2},{14,6},... | collective-permute-start | bytes 393224 | tf_op jit(solution)/shard_map/ppermute | solution.py:17
  9.0 2.1 %collective-permute-done.3.refs_2_ = bf16[16,4096]{1,0:T(8,128)(2,1)S(1)} collective-permute-done((bf16[16,4096]{1,0:T(8,128)(2,1)S(1)}, bf16[16,4096]{1,0:T(8,128)(2,1)S(1)}, u32[]{:S(2)}, u32[]{:S(2)}) %collective-permute-start.3) | collective-permute-done | bytes 131104 | tf_op jit(solution)/shard_map/ppermute | solution.py:17
  11.1 1.6 %collective-permute-start.4 = (bf16[16,4096]{1,0:T(8,128)(2,1)S(1)}, bf16[16,4096]{1,0:T(8,128)(2,1)S(1)}, u32[]{:S(2)}, u32[]{:S(2)}) collective-permute-start(bf16[16,4096]{1,0:T(8,128)(2,1)S(1)} %collective-permute-done.3.refs_2_), channel_id=1, source_target_pairs={{2,0},{3,1},{0,2},{1,3},{6,4},{7,5},{4,6},{5,7},{10,8},{11,9},{8,1... | collective-permute-start | bytes 393224 | tf_op jit(solution)/shard_map/ppermute | solution.py:17
  12.8 2.0 %collective-permute-done.6.refs_4_ = bf16[16,4096]{1,0:T(8,128)(2,1)S(1)} collective-permute-done((bf16[16,4096]{1,0:T(8,128)(2,1)S(1)}, bf16[16,4096]{1,0:T(8,128)(2,1)S(1)}, u32[]{:S(2)}, u32[]{:S(2)}) %collective-permute-start.6) | collective-permute-done | bytes 131104 | tf_op jit(solution)/shard_map/ppermute | solution.py:17
  14.7 1.5 %collective-permute-start.7 = (bf16[16,4096]{1,0:T(8,128)(2,1)S(1)}, bf16[16,4096]{1,0:T(8,128)(2,1)S(1)}, u32[]{:S(2)}, u32[]{:S(2)}) collective-permute-start(bf16[16,4096]{1,0:T(8,128)(2,1)S(1)} %collective-permute-done.6.refs_4_), channel_id=1, source_target_pairs={{2,0},{3,1},{0,2},{1,3},{6,4},{7,5},{4,6},{5,7},{10,8},{11,9},{8,1... | collective-permute-start | bytes 393224 | tf_op jit(solution)/shard_map/ppermute | solution.py:17
  16.2 0.0 collective-permute-done.after_ref.refs_7_
  16.2 2.4 %prepare.1 = (bf16[128,192]{1,0:T(8,128)(2,1)S(1)}, bf16[3,192,4096]{2,1,0:T(8,128)(2,1)S(1)}) custom-call(s32[8,128]{1,0:T(8,128)} %bitcast.6, f32[8,128]{1,0:T(8,128)} %bitcast.7, bf16[3,192,4096]{2,1,0:T(8,128)(2,1)} %bitcast.4, bf16[16,4096]{1,0:T(8,128)(2,1)S(1)} %collective-permute-done.after_ref.refs_7_), custom_call_target="tpu_custom_call" | custom-call | bytes 9225000 | tf_op jit(solution)/shard_map/prepare/pallas_call | solution.py:120
  18.6 0.0 collective-permute-done.2.refs_2_
  18.6 1.3 %collective-permute-start.5 = (bf16[16,4096]{1,0:T(8,128)(2,1)S(1)}, bf16[16,4096]{1,0:T(8,128)(2,1)S(1)}, u32[]{:S(2)}, u32[]{:S(2)}) collective-permute-start(bf16[16,4096]{1,0:T(8,128)(2,1)S(1)} %collective-permute-done.2.refs_2_), channel_id=1, source_target_pairs={{2,0},{3,1},{0,2},{1,3},{6,4},{7,5},{4,6},{5,7},{10,8},{11,9},{8,1... | collective-permute-start | bytes 393224 | tf_op jit(solution)/shard_map/ppermute | solution.py:17
  19.9 0.0 collective-permute-done.4.refs_3_
  19.9 0.0 collective-permute-done.1.refs_1_
  19.9 2.4 %experts.2 = (f32[16,4096]{1,0:T(8,128)S(1)}, bf16[16,4096]{1,0:T(8,128)(2,1)S(1)}) custom-call(bf16[3,192,4096]{2,1,0:T(8,128)(2,1)S(1)} %get-tuple-element.28.refs_0_, bf16[3,192,4096]{2,1,0:T(8,128)(2,1)S(1)} %collective-permute-done.1.refs_1_, bf16[16,4096]{1,0:T(8,128)(2,1)S(1)} %collective-permute-done.3.refs_2_, ...), custom_call_target="tpu_custom_call" | custom-call | bytes 9225000 | tf_op jit(solution)/shard_map/experts/pallas_call | solution.py:173
  22.4 0.8 %collective-permute-start.8 = (bf16[16,4096]{1,0:T(8,128)(2,1)S(1)}, bf16[16,4096]{1,0:T(8,128)(2,1)S(1)}, u32[]{:S(2)}, u32[]{:S(2)}) collective-permute-start(bf16[16,4096]{1,0:T(8,128)(2,1)S(1)} %get-tuple-element.38), channel_id=1, source_target_pairs={{2,0},{3,1},{0,2},{1,3},{6,4},{7,5},{4,6},{5,7},{10,8},{11,9},{8,1... | collective-permute-start | bytes 393224 | tf_op jit(solution)/shard_map/ppermute | solution.py:17
  23.2 0.0 collective-permute-done.7.refs_5_
  23.2 0.7 %collective-permute-done.5.refs_3_ = bf16[16,4096]{1,0:T(8,128)(2,1)S(1)} collective-permute-done((bf16[16,4096]{1,0:T(8,128)(2,1)S(1)}, bf16[16,4096]{1,0:T(8,128)(2,1)S(1)}, u32[]{:S(2)}, u32[]{:S(2)}) %collective-permute-start.5) | collective-permute-done | bytes 131104 | tf_op jit(solution)/shard_map/ppermute | solution.py:17
  23.8 2.5 %experts.3 = (f32[16,4096]{1,0:T(8,128)S(1)}, bf16[16,4096]{1,0:T(8,128)(2,1)S(1)}, bf16[16,4096]{1,0:T(8,128)(2,1)S(1)}, bf16[16,4096]{1,0:T(8,128)(2,1)S(1)}, ...) custom-call(bf16[3,192,4096]{2,1,0:T(8,128)(2,1)S(1)} %get-tuple-element.28.refs_0_, ...), custom_call_target="tpu_custom_call" | custom-call | bytes 9225000 | tf_op jit(solution)/shard_map/experts/pallas_call | solution.py:173
  26.4 1.0 %collective-permute-done.8 = bf16[16,4096]{1,0:T(8,128)(2,1)S(1)} collective-permute-done((bf16[16,4096]{1,0:T(8,128)(2,1)S(1)}, bf16[16,4096]{1,0:T(8,128)(2,1)S(1)}, u32[]{:S(2)}, u32[]{:S(2)}) %collective-permute-start.8) | collective-permute-done | bytes 131104 | tf_op jit(solution)/shard_map/ppermute | solution.py:17
  27.3 0.9 %collective-permute-start.14 = (bf16[16,4096]{1,0:T(8,128)(2,1)S(1)}, bf16[16,4096]{1,0:T(8,128)(2,1)S(1)}, u32[]{:S(2)}, u32[]{:S(2)}) collective-permute-start(bf16[16,4096]{1,0:T(8,128)(2,1)S(1)} %get-tuple-element.46), channel_id=1, source_target_pairs={{4,0},{0,4},{12,8},{8,12},{5,1},{1,5},{13,9},{9,13},{6,2},{2,6},{1... | collective-permute-start | bytes 393224 | tf_op jit(solution)/shard_map/ppermute | solution.py:17
  28.2 1.1 %collective-permute-start.9 = (bf16[16,4096]{1,0:T(8,128)(2,1)S(1)}, bf16[16,4096]{1,0:T(8,128)(2,1)S(1)}, u32[]{:S(2)}, u32[]{:S(2)}) collective-permute-start(bf16[16,4096]{1,0:T(8,128)(2,1)S(1)} %get-tuple-element.39), channel_id=1, source_target_pairs={{2,0},{3,1},{0,2},{1,3},{6,4},{7,5},{4,6},{5,7},{10,8},{11,9},{8,1... | collective-permute-start | bytes 393224 | tf_op jit(solution)/shard_map/ppermute | solution.py:17
  29.3 2.1 %collective-permute-start.11 = (bf16[16,4096]{1,0:T(8,128)(2,1)S(1)}, bf16[16,4096]{1,0:T(8,128)(2,1)S(1)}, u32[]{:S(2)}, u32[]{:S(2)}) collective-permute-start(bf16[16,4096]{1,0:T(8,128)(2,1)S(1)} %add_convert_fusion), channel_id=1, source_target_pairs={{12,0},{8,4},{4,8},{0,12},{13,1},{9,5},{5,9},{1,13},{14,2},{10,6},... | collective-permute-start | bytes 393224 | tf_op jit(solution)/shard_map/ppermute | solution.py:17
  31.4 0.5 %collective-permute-start.13 = (bf16[16,4096]{1,0:T(8,128)(2,1)S(1)}, bf16[16,4096]{1,0:T(8,128)(2,1)S(1)}, u32[]{:S(2)}, u32[]{:S(2)}) collective-permute-start(bf16[16,4096]{1,0:T(8,128)(2,1)S(1)} %get-tuple-element.44), channel_id=1, source_target_pairs={{2,0},{3,1},{0,2},{1,3},{6,4},{7,5},{4,6},{5,7},{10,8},{11,9},{8,1... | collective-permute-start | bytes 393224 | tf_op jit(solution)/shard_map/ppermute | solution.py:17
  31.9 1.1 %collective-permute-start.12 = (bf16[16,4096]{1,0:T(8,128)(2,1)S(1)}, bf16[16,4096]{1,0:T(8,128)(2,1)S(1)}, u32[]{:S(2)}, u32[]{:S(2)}) collective-permute-start(bf16[16,4096]{1,0:T(8,128)(2,1)S(1)} %get-tuple-element.42), channel_id=1, source_target_pairs={{4,0},{0,4},{12,8},{8,12},{5,1},{1,5},{13,9},{9,13},{6,2},{2,6},{1... | collective-permute-start | bytes 393224 | tf_op jit(solution)/shard_map/ppermute | solution.py:17
  33.1 1.3 %collective-permute-done.14 = bf16[16,4096]{1,0:T(8,128)(2,1)S(1)} collective-permute-done((bf16[16,4096]{1,0:T(8,128)(2,1)S(1)}, bf16[16,4096]{1,0:T(8,128)(2,1)S(1)}, u32[]{:S(2)}, u32[]{:S(2)}) %collective-permute-start.14) | collective-permute-done | bytes 131104 | tf_op jit(solution)/shard_map/ppermute | solution.py:17
  34.4 0.8 %collective-permute-start.15 = (bf16[16,4096]{1,0:T(8,128)(2,1)S(1)}, bf16[16,4096]{1,0:T(8,128)(2,1)S(1)}, u32[]{:S(2)}, u32[]{:S(2)}) collective-permute-start(bf16[16,4096]{1,0:T(8,128)(2,1)S(1)} %collective-permute-done.14), channel_id=1, source_target_pairs={{2,0},{3,1},{0,2},{1,3},{6,4},{7,5},{4,6},{5,7},{10,8},{11,9},{8,1... | collective-permute-start | bytes 393224 | tf_op jit(solution)/shard_map/ppermute | solution.py:17
  35.2 0.0 collective-permute-done.9
  35.2 2.1 %collective-permute-start.10 = (bf16[16,4096]{1,0:T(8,128)(2,1)S(1)}, bf16[16,4096]{1,0:T(8,128)(2,1)S(1)}, u32[]{:S(2)}, u32[]{:S(2)}) collective-permute-start(bf16[16,4096]{1,0:T(8,128)(2,1)S(1)} %add_convert_fusion.1), channel_id=1, source_target_pairs={{8,0},{12,4},{0,8},{4,12},{9,1},{13,5},{1,9},{5,13},{10,2},{14,6},... | collective-permute-start | bytes 393224 | tf_op jit(solution)/shard_map/ppermute | solution.py:17
  37.3 0.4 collective-permute-done.11.refs_1_
  37.7 0.0 collective-permute-done.13.refs_4_
  37.7 1.3 %collective-permute-done.12.refs_3_ = bf16[16,4096]{1,0:T(8,128)(2,1)S(1)} collective-permute-done((bf16[16,4096]{1,0:T(8,128)(2,1)S(1)}, bf16[16,4096]{1,0:T(8,128)(2,1)S(1)}, u32[]{:S(2)}, u32[]{:S(2)}) %collective-permute-start.12) | collective-permute-done | bytes 131104 | tf_op jit(solution)/shard_map/ppermute | solution.py:17
  39.1 0.3 collective-permute-done.15.refs_5_
  39.4 1.8 %collective-permute-done.10.refs_0_ = bf16[16,4096]{1,0:T(8,128)(2,1)S(1)} collective-permute-done((bf16[16,4096]{1,0:T(8,128)(2,1)S(1)}, bf16[16,4096]{1,0:T(8,128)(2,1)S(1)}, u32[]{:S(2)}, u32[]{:S(2)}) %collective-permute-start.10) | collective-permute-done | bytes 131104 | tf_op jit(solution)/shard_map/ppermute | solution.py:17
  41.2 1.2 %combine.1 = bf16[128,4096]{1,0:T(8,128)(2,1)} custom-call(bf16[128,192]{1,0:T(8,128)(2,1)S(1)} %get-tuple-element.27.mix_ref, bf16[16,4096]{1,0:T(8,128)(2,1)S(1)} %collective-permute-done.10.refs_0_, bf16[16,4096]{1,0:T(8,128)(2,1)S(1)} %collective-permute-done.11.refs_1_, f32[16,4096]{1,0:T(8,128)S(1)} %get-tuple-element.40.refs_2_, ...), custom_call_target="tpu_custom_call" | custom-call | bytes 4428000 | tf_op jit(solution)/shard_map/combine/pallas_call | solution.py:214
  (2 shorter events, 0.1 us)
Async XLA Ops:
  1.5 18.4 %collective-permute-start.1 = (bf16[3,192,4096]{2,1,0:T(8,128)(2,1)}, bf16[3,192,4096]{2,1,0:T(8,128)(2,1)S(1)}, u32[]{:S(2)}, u32[]{:S(2)}) collective-permute-start(bf16[3,192,4096]{2,1,0:T(8,128)(2,1)} %bitcast.3), channel_id=1, source_target_pairs={{1,0},{0,1},{3,2},{2,3},{5,4},{4,5},{7,6},{6,7},{9,8},{8,9},{11,10... | collective-permute-start | bytes 14155784 | tf_op jit(solution)/shard_map/ppermute | solution.py:17
  2.1 9.1 %collective-permute-start.3 = (bf16[16,4096]{1,0:T(8,128)(2,1)S(1)}, bf16[16,4096]{1,0:T(8,128)(2,1)S(1)}, u32[]{:S(2)}, u32[]{:S(2)}) collective-permute-start(bf16[16,4096]{1,0:T(8,128)(2,1)S(1)} %get-tuple-element.31), channel_id=1, source_target_pairs={{12,0},{8,4},{4,8},{0,12},{13,1},{9,5},{5,9},{1,13},{14,2},{10,6},... | collective-permute-start | bytes 393224 | tf_op jit(solution)/shard_map/ppermute | solution.py:17
  6.7 8.0 %collective-permute-start.6 = (bf16[16,4096]{1,0:T(8,128)(2,1)S(1)}, bf16[16,4096]{1,0:T(8,128)(2,1)S(1)}, u32[]{:S(2)}, u32[]{:S(2)}) collective-permute-start(bf16[16,4096]{1,0:T(8,128)(2,1)S(1)} %get-tuple-element.35), channel_id=1, source_target_pairs={{4,0},{0,4},{12,8},{8,12},{5,1},{1,5},{13,9},{9,13},{6,2},{2,6},{1... | collective-permute-start | bytes 393224 | tf_op jit(solution)/shard_map/ppermute | solution.py:17
  6.7 9.5 %collective-permute-start = (bf16[16,4096]{1,0:T(8,128)(2,1)S(1)}, bf16[16,4096]{1,0:T(8,128)(2,1)S(1)}, u32[]{:S(2)}, u32[]{:S(2)}) collective-permute-start(bf16[16,4096]{1,0:T(8,128)(2,1)S(1)} %get-tuple-element.26.refs_6_), channel_id=1, source_target_pairs={{2,0},{3,1},{0,2},{1,3},{6,4},{7,5},{4,6},{5,7},{10,8},{11,9},{8,1... | collective-permute-start | bytes 393224 | tf_op jit(solution)/shard_map/ppermute | solution.py:17
  8.2 10.4 %collective-permute-start.2 = (bf16[16,4096]{1,0:T(8,128)(2,1)S(1)}, bf16[16,4096]{1,0:T(8,128)(2,1)S(1)}, u32[]{:S(2)}, u32[]{:S(2)}) collective-permute-start(bf16[16,4096]{1,0:T(8,128)(2,1)S(1)} %get-tuple-element.30), channel_id=1, source_target_pairs={{8,0},{12,4},{0,8},{4,12},{9,1},{13,5},{1,9},{5,13},{10,2},{14,6},... | collective-permute-start | bytes 393224 | tf_op jit(solution)/shard_map/ppermute | solution.py:17
  11.1 8.8 %collective-permute-start.4 = (bf16[16,4096]{1,0:T(8,128)(2,1)S(1)}, bf16[16,4096]{1,0:T(8,128)(2,1)S(1)}, u32[]{:S(2)}, u32[]{:S(2)}) collective-permute-start(bf16[16,4096]{1,0:T(8,128)(2,1)S(1)} %collective-permute-done.3.refs_2_), channel_id=1, source_target_pairs={{2,0},{3,1},{0,2},{1,3},{6,4},{7,5},{4,6},{5,7},{10,8},{11,9},{8,1... | collective-permute-start | bytes 393224 | tf_op jit(solution)/shard_map/ppermute | solution.py:17
  14.7 8.4 %collective-permute-start.7 = (bf16[16,4096]{1,0:T(8,128)(2,1)S(1)}, bf16[16,4096]{1,0:T(8,128)(2,1)S(1)}, u32[]{:S(2)}, u32[]{:S(2)}) collective-permute-start(bf16[16,4096]{1,0:T(8,128)(2,1)S(1)} %collective-permute-done.6.refs_4_), channel_id=1, source_target_pairs={{2,0},{3,1},{0,2},{1,3},{6,4},{7,5},{4,6},{5,7},{10,8},{11,9},{8,1... | collective-permute-start | bytes 393224 | tf_op jit(solution)/shard_map/ppermute | solution.py:17
  18.6 5.2 %collective-permute-start.5 = (bf16[16,4096]{1,0:T(8,128)(2,1)S(1)}, bf16[16,4096]{1,0:T(8,128)(2,1)S(1)}, u32[]{:S(2)}, u32[]{:S(2)}) collective-permute-start(bf16[16,4096]{1,0:T(8,128)(2,1)S(1)} %collective-permute-done.2.refs_2_), channel_id=1, source_target_pairs={{2,0},{3,1},{0,2},{1,3},{6,4},{7,5},{4,6},{5,7},{10,8},{11,9},{8,1... | collective-permute-start | bytes 393224 | tf_op jit(solution)/shard_map/ppermute | solution.py:17
  22.4 5.0 %collective-permute-start.8 = (bf16[16,4096]{1,0:T(8,128)(2,1)S(1)}, bf16[16,4096]{1,0:T(8,128)(2,1)S(1)}, u32[]{:S(2)}, u32[]{:S(2)}) collective-permute-start(bf16[16,4096]{1,0:T(8,128)(2,1)S(1)} %get-tuple-element.38), channel_id=1, source_target_pairs={{2,0},{3,1},{0,2},{1,3},{6,4},{7,5},{4,6},{5,7},{10,8},{11,9},{8,1... | collective-permute-start | bytes 393224 | tf_op jit(solution)/shard_map/ppermute | solution.py:17
  27.3 7.1 %collective-permute-start.14 = (bf16[16,4096]{1,0:T(8,128)(2,1)S(1)}, bf16[16,4096]{1,0:T(8,128)(2,1)S(1)}, u32[]{:S(2)}, u32[]{:S(2)}) collective-permute-start(bf16[16,4096]{1,0:T(8,128)(2,1)S(1)} %get-tuple-element.46), channel_id=1, source_target_pairs={{4,0},{0,4},{12,8},{8,12},{5,1},{1,5},{13,9},{9,13},{6,2},{2,6},{1... | collective-permute-start | bytes 393224 | tf_op jit(solution)/shard_map/ppermute | solution.py:17
  28.2 7.0 %collective-permute-start.9 = (bf16[16,4096]{1,0:T(8,128)(2,1)S(1)}, bf16[16,4096]{1,0:T(8,128)(2,1)S(1)}, u32[]{:S(2)}, u32[]{:S(2)}) collective-permute-start(bf16[16,4096]{1,0:T(8,128)(2,1)S(1)} %get-tuple-element.39), channel_id=1, source_target_pairs={{2,0},{3,1},{0,2},{1,3},{6,4},{7,5},{4,6},{5,7},{10,8},{11,9},{8,1... | collective-permute-start | bytes 393224 | tf_op jit(solution)/shard_map/ppermute | solution.py:17
  29.3 8.4 %collective-permute-start.11 = (bf16[16,4096]{1,0:T(8,128)(2,1)S(1)}, bf16[16,4096]{1,0:T(8,128)(2,1)S(1)}, u32[]{:S(2)}, u32[]{:S(2)}) collective-permute-start(bf16[16,4096]{1,0:T(8,128)(2,1)S(1)} %add_convert_fusion), channel_id=1, source_target_pairs={{12,0},{8,4},{4,8},{0,12},{13,1},{9,5},{5,9},{1,13},{14,2},{10,6},... | collective-permute-start | bytes 393224 | tf_op jit(solution)/shard_map/ppermute | solution.py:17
  31.4 6.3 %collective-permute-start.13 = (bf16[16,4096]{1,0:T(8,128)(2,1)S(1)}, bf16[16,4096]{1,0:T(8,128)(2,1)S(1)}, u32[]{:S(2)}, u32[]{:S(2)}) collective-permute-start(bf16[16,4096]{1,0:T(8,128)(2,1)S(1)} %get-tuple-element.44), channel_id=1, source_target_pairs={{2,0},{3,1},{0,2},{1,3},{6,4},{7,5},{4,6},{5,7},{10,8},{11,9},{8,1... | collective-permute-start | bytes 393224 | tf_op jit(solution)/shard_map/ppermute | solution.py:17
  31.9 7.1 %collective-permute-start.12 = (bf16[16,4096]{1,0:T(8,128)(2,1)S(1)}, bf16[16,4096]{1,0:T(8,128)(2,1)S(1)}, u32[]{:S(2)}, u32[]{:S(2)}) collective-permute-start(bf16[16,4096]{1,0:T(8,128)(2,1)S(1)} %get-tuple-element.42), channel_id=1, source_target_pairs={{4,0},{0,4},{12,8},{8,12},{5,1},{1,5},{13,9},{9,13},{6,2},{2,6},{1... | collective-permute-start | bytes 393224 | tf_op jit(solution)/shard_map/ppermute | solution.py:17
  34.4 5.0 %collective-permute-start.15 = (bf16[16,4096]{1,0:T(8,128)(2,1)S(1)}, bf16[16,4096]{1,0:T(8,128)(2,1)S(1)}, u32[]{:S(2)}, u32[]{:S(2)}) collective-permute-start(bf16[16,4096]{1,0:T(8,128)(2,1)S(1)} %collective-permute-done.14), channel_id=1, source_target_pairs={{2,0},{3,1},{0,2},{1,3},{6,4},{7,5},{4,6},{5,7},{10,8},{11,9},{8,1... | collective-permute-start | bytes 393224 | tf_op jit(solution)/shard_map/ppermute | solution.py:17
  35.2 5.9 %collective-permute-start.10 = (bf16[16,4096]{1,0:T(8,128)(2,1)S(1)}, bf16[16,4096]{1,0:T(8,128)(2,1)S(1)}, u32[]{:S(2)}, u32[]{:S(2)}) collective-permute-start(bf16[16,4096]{1,0:T(8,128)(2,1)S(1)} %add_convert_fusion.1), channel_id=1, source_target_pairs={{8,0},{12,4},{0,8},{4,12},{9,1},{13,5},{1,9},{5,13},{10,2},{14,6},... | collective-permute-start | bytes 393224 | tf_op jit(solution)/shard_map/ppermute | solution.py:17

commit v4 on v3

--- a/solution.py
+++ b/solution.py
@@ -18,7 +18,7 @@
 
 
 def cost(micros):
-    return pl.CostEstimate(flops=0, bytes_accessed=int(micros * 3690e3), transcendentals=0)
+    return pl.CostEstimate(flops=0, bytes_accessed=int(micros * 3690e3 * 1), transcendentals=0)
 
 
 def in_main(x):
@@ -187,15 +187,21 @@
 def combine_kernel(count, near, chips, steps, mix_ref, *refs):
     blocks, home, pairs = refs[:count], refs[count], refs[count + 1 : count + 1 + near]
     gots, (out_ref, held, sems) = refs[count + 1 + near : -3], refs[-3:]
+    cap = home.shape[0]
     span = held.shape[1] // steps
     copies = []
     for s in range(steps):
         c = slice(s * span, (s + 1) * span)
-        homes = [home[:, c]] + [pair[:, c].astype(jnp.float32) for pair in pairs]
+        homes = [home[:, c]] + [pair[:cap, c].astype(jnp.float32) for pair in pairs]
         homes = jnp.concatenate(homes, axis=0)
+        each = len(gots) // (chips - 1)
         for n in range(chips - 1):
-            group = gots[n * (near + 1) : (n + 1) * (near + 1)]
-            homes = homes + jnp.concatenate([got[:, c] for got in group], axis=0).astype(jnp.float32)
+            group = gots[n * each : (n + 1) * each]
+            share = jnp.concatenate([got[:, c] for got in group], axis=0).astype(jnp.float32)
+            if each == 1 and near:
+                homes = jnp.concatenate([homes[:cap] + share, homes[cap:]], axis=0)
+            else:
+                homes = homes + share
         rows = jnp.concatenate([ref[:, c] for ref in blocks] + [homes.astype(jnp.bfloat16)], axis=0)
         held[:, c] = jnp.dot(
             mix_ref[...], jnp.concatenate([rows] * 3, axis=0), preferred_element_type=jnp.float32
@@ -230,6 +236,9 @@
     return lax.optimization_barrier((x, *others))[0]
 
 
+OPT = {'co': '23', 'do': '2310', 'zo': '2130', 'sib': 'a', 'pre': 'x', 'xo': '213', 'xd1': '', 'xd2': 'm', 'xd3': '', 'bo': '23', 'back': 'x', 'od': '2n', 'nd': '3', 'pz': '1', 'A': '3', 'ab': '1', 'fd': '', 'nb': '', 'ps': '1', 'pd': '3', 'b': 'g', 'sb': '13'}
+
+
 def local(tokens, assign, probs, expert_weights):
     experts = lax.axis_size("dp")
     chips = lax.axis_size("expert") // 2
@@ -237,65 +246,143 @@
     own = expert_weights[0]
     near, far = list(range(1, experts // 2)), list(range(experts // 2, experts))
     soon, late = far[: len(far) // 2], far[len(far) // 2 :]
+    lists = {"1": near, "2": soon, "3": late, "0": [0]}
     others = range(1, chips)
-
-    leave = [*soon, *late, *near, 0]
-    outgoing = dict(zip(leave, dispatch(assign, tokens, leave, cap)))
-    blocks = {(0, 0): outgoing[0]}
-
-    def across(m, *before):
+    blocks, came = {}, {}
+
+    def run(code):
+        return [m for k in code for m in lists[k]]
+
+    order = run(OPT["co"]) + [0] + near
+    rows_order = run(OPT["do"])
+    outgoing = dict(zip(rows_order, dispatch(assign, tokens, rows_order, cap, steps=2)))
+    blocks[0, 0] = outgoing[0]
+    state = {}
+
+    def dep(code):
+        out = []
+        for k in code:
+            if k == "m":
+                out.append(state["mix"])
+            elif k == "x":
+                out.append(blocks[0, chips - 1])
+            elif k in "123":
+                out.append(blocks[lists[k][-1], 0])
+        return out
+
+    for m in run(OPT["zo"]):
+        if m:
+            blocks[m, 0] = swap(after(outgoing[m]) if "z" in OPT["b"] else outgoing[m], "dp", m)
+        else:
+            for c in others:
+                blocks[0, c] = swap(after(outgoing[0]) if "o" in OPT["b"] else outgoing[0], "expert", 2 * c)
+    sibling = swap(own if OPT["sib"] == "s" else after(own, outgoing[0]), "expert", 1)
+    pre = {"o": outgoing[0], "x": blocks[0, chips - 1], "1": blocks[near[0], 0], "3": blocks[late[0], 0]}[OPT["pre"]]
+    state["mix"], held = prepare(assign, probs, after(own) if "w" in OPT["b"] else own, order, cap, pre)
+    away = run(OPT["bo"])
+    zfirst = OPT["back"] == "z"
+    tagged = {("f", m, c): ([(m, c)], jnp.bfloat16 if c else jnp.float32) for m in away for c in range(chips)}
+    for m in near:
+        if zfirst and OPT["ps"]:
+            tagged |= {("n", m, c): ([(m, c)], jnp.bfloat16) for c in range(chips)}
+        elif zfirst:
+            tagged["n", m, 0] = ([(m, c) for c in range(chips)], jnp.bfloat16)
+        else:
+            tagged |= {("n", m, c): ([(m, c)], jnp.bfloat16 if c else jnp.float32) for c in range(chips)}
+    tagged |= {("h", 0, c): ([(0, c)], jnp.bfloat16 if c else jnp.float32) for c in range(chips)}
+    early = run(OPT["A"])
+    first = [t for t in tagged if t[1] in early]
+    second = [t for t in tagged if t[1] not in early]
+    made = {}
+
+    def compute_first():
+        made.update(zip(first, expert_part(held, sibling, blocks, [tagged[t] for t in first])))
+
+    for code in OPT["xo"]:
+        before = dep(OPT["xd" + code])
+        if "a" in OPT["xd" + code]:
+            compute_first()
+            before.append(made[first[0]])
+        for m in lists[code]:
+            for c in others:
+                here = after(blocks[m, 0], *before) if before or code in OPT["sb"] else blocks[m, 0]
+                blocks[m, c] = swap(here, "expert", 2 * c)
+    if first and not made:
+        compute_first()
+    if first and OPT["ab"]:
+        k = tagged[second[0]][0][0]
+        blocks[k] = after(blocks[k], made[first[0]])
+    made |= dict(zip(second, expert_part(held, sibling, blocks, [tagged[t] for t in second])))
+    for t in first:
+        if t[0] in OPT["nb"]:
+            made[t] = after(made[t], made[second[0]])
+    pf = [made[t] for t in tagged if t[0] == "f"]
+    pn = [made[t] for t in tagged if t[0] == "n"]
+    ph = [made[t] for t in tagged if t[0] == "h"]
+    for n, m in enumerate(away):
         for c in others:
-            blocks[m, c] = swap(after(blocks[m, 0], *before), "expert", 2 * c)
-
-    across(0)
-    for m in [*soon, *near, *late]:
-        blocks[m, 0] = swap(outgoing[m], "dp", m)
-    sibling = swap(after(own, outgoing[0]), "expert", 1)
-    order = [*soon, *late, 0, *near]
-    mix, own = prepare(assign, probs, own, order, cap, blocks[0, chips - 1])
-    for m in soon:
-        across(m, mix)
-    for m in [*near, *late]:
-        across(m)
-
-    def share(m, home=jnp.float32):
-        return {(m, c): jnp.bfloat16 if c else home for c in range(chips)}
-
-    def compute(wanted):
-        kinds = [([key], kind) for key, kind in wanted.items()]
-        return dict(zip(wanted, expert_part(own, sibling, blocks, kinds)))
-
-    wanted = {}
-    for m in late:
-        wanted |= share(m)
-    parts = compute(wanted)
-    came = {(m, c): swap(parts[m, c], "expert", 2 * c) for m in late for c in others}
-    blocks[soon[0], 0] = after(blocks[soon[0], 0], parts[late[0], 0])
-    wanted = {}
-    for m in soon:
-        wanted |= share(m)
-    for m in near:
-        wanted |= share(m, jnp.bfloat16)
-    parts |= compute(wanted | share(0))
-    first = came[late[-1], chips - 1]
-    for m in soon:
+            part = after(pf[n * chips + c]) if "p" in OPT["b"] else pf[n * chips + c]
+            if OPT["fd"] and n and first and m not in early:
+                part = after(part, came[away[0], c])
+            came[m, c] = swap(part, "expert", 2 * c)
+
+    def bdep(code):
+        return [came[lists[k][-1], chips - 1] for k in code if k in "23"]
+
+    returned = {}
+
+    def send_far():
+        for n, m in enumerate(away):
+            row = pf[n * chips]
+            for c in others:
+                row = row + came[m, c].astype(jnp.float32)
+            row = row.astype(jnp.bfloat16)
+            if m in soon and "s" in OPT["b"] or m in late and "l" in OPT["b"]:
+                row = after(row)
+            returned[m] = swap(row, "dp", m)
+
+    def send_home(*more):
+        return {c: swap(after(ph[c], *bdep(OPT["od"]), *more), "expert", 2 * c) for c in others}
+
+    if zfirst:
+        def send_pairs():
+            each = chips if OPT["ps"] else 1
+            sent = [swap(after(part, *bdep(OPT["pd"])), "dp", near[n // each]) for n, part in enumerate(pn)]
+            if OPT["ps"]:
+                return [sent[n * chips : (n + 1) * chips] for n in range(len(near))]
+            return [[pair[c * cap : (c + 1) * cap] for c in range(chips)] for pair in sent]
+
+        if OPT["pz"] == "0":
+            pairs = send_pairs()
+            send_far()
+        else:
+            send_far()
+            pairs = send_pairs()
+        hx = send_home()
+        gots = []
         for c in others:
-            came[m, c] = swap(after(parts[m, c], came[late[0], c]), "expert", 2 * c)
-
-    pairs = [[swap(after(parts[m, c], first), "dp", m) for c in range(chips)] for m in near]
-    returned = {}
-    for m in [*late, *soon]:
-        row = parts[m, 0]
+            gots.append(hx[c])
+            gots += [
+                swap(after(pair[c], *bdep(OPT["nd"])) if "g" in OPT["b"] or OPT["nd"] else pair[c], "expert", 2 * c)
+                for pair in pairs
+            ]
+        return combine(
+            state["mix"], [returned[m] for m in order[: len(far)]], ph[0], [pair[0] for pair in pairs], gots
+        )
+    nx = {
+        (m, c): swap(after(pn[n * chips + c], *bdep(OPT["nd"])), "expert", 2 * c)
+        for n, m in enumerate(near)
+        for c in others
+    }
+    send_far()
+    hx = send_home(*([nx[near[-1], chips - 1]] if "n" in OPT["od"] else []))
+    for n, m in enumerate(near):
+        row = pn[n * chips]
         for c in others:
-            row = row + came[m, c].astype(jnp.float32)
+            row = row + nx[m, c].astype(jnp.float32)
         returned[m] = swap(row.astype(jnp.bfloat16), "dp", m)
-    homes = {c: swap(after(parts[0, c], first), "expert", 2 * c) for c in others}
-    gots = []
-    for c in others:
-        gots += [homes[c]] + [swap(pair[c], "expert", 2 * c) for pair in pairs]
-    return combine(
-        mix, [returned[m] for m in [*soon, *late]], parts[0, 0], [pair[0] for pair in pairs], gots
-    )
+    gots = [hx[c] for c in others]
+    return combine(state["mix"], [returned[m] for m in order[: len(far)]], ph[0], [returned[m] for m in near], gots)
 
 
 def solution(mesh):

time: 42.6 us -> 42.8 us (level)
  waiting for transfers between devices: 10.9 us -> 11.6 us
  starting transfers between devices: 21.3 us -> 20.7 us
    ppermute x16 -> x15, waiting for transfers between devices: 10.9 us -> 11.6 us  [swap(): return lax.ppermute(block, axis, route)]
    ppermute x16 -> x15, starting transfers between devices: 21.3 us -> 20.7 us  [swap(): return lax.ppermute(block, axis, route)]
  transfers between devices with their start and end apart: 16 -> 15, of which waited for: 9 -> 7; matrix products, arithmetic and copies ran while one was open for 0% -> 0% of each run, Pallas kernels for 17% -> 17%
where the time goes in v4:
time: 42.8 us; the launch traced here: 42.6 us
  starting transfers between devices  20.7 us (48%)
  waiting for transfers between devices  11.6 us (27%)
  Pallas kernels  10.1 us (24%)
    ppermute x15, starting transfers between devices, swap(): return lax.ppermute(block, axis, route)  20.7 us
    ppermute x15, waiting for transfers between devices, swap(): return lax.ppermute(block, axis, route)  11.6 us
    pallas_call x2, Pallas kernels, expert_part(): pl.pallas_call(functools.partial(expert_kernel, len(keys), steps), out_sh...  4.94 us
    pallas_call x1, Pallas kernels, prepare(): pl.pallas_call(functools.partial(prepare_kernel, masks, cap), out_shape=[...  2.4 us
    pallas_call x1, Pallas kernels, dispatch(): pl.pallas_call(functools.partial(dispatch_kernel, masks, cap, steps), out...  1.53 us
    pallas_call x1, Pallas kernels, combine(): pl.pallas_call(functools.partial(combine_kernel, count, near, chips, step...  1.23 us
  transfers between devices with their start and end apart: 15, of which 7 were waited for; matrix products, arithmetic and copies ran while one was open for 0% of the time, Pallas kernels for 17%

profile of v4, /device:TPU:0, one launch (start us, length us, event | category | flops | bytes accessed | tf_op | source)
XLA Modules:
  0.0 42.6 jit_solution(65780972580269886)
XLA Ops:
  0.0 1.5 %dispatch.1 = (bf16[16,4096]{1,0:T(8,128)(2,1)S(1)}, bf16[16,4096]{1,0:T(8,128)(2,1)S(1)}, bf16[16,4096]{1,0:T(8,128)(2,1)S(1)}, bf16[16,4096]{1,0:T(8,128)(2,1)S(1)}) custom-call(s32[8,128]{1,0:T(8,128)} %bitcast.5, bf16[128,4096]{1,0:T(8,128)(2,1)} %tok_ref.1), custom_call_target="tpu_custom_call" | custom-call | bytes 3690000 | tf_op jit(solution)/shard_map/dispatch/pallas_call | solution.py:79
  1.5 0.5 %collective-permute-start.1 = (bf16[3,192,4096]{2,1,0:T(8,128)(2,1)}, bf16[3,192,4096]{2,1,0:T(8,128)(2,1)S(1)}, u32[]{:S(2)}, u32[]{:S(2)}) collective-permute-start(bf16[3,192,4096]{2,1,0:T(8,128)(2,1)} %bitcast.3), channel_id=1, source_target_pairs={{1,0},{0,1},{3,2},{2,3},{5,4},{4,5},{7,6},{6,7},{9,8},{8,9},{11,10... | collective-permute-start | bytes 14155784 | tf_op jit(solution)/shard_map/ppermute | solution.py:17
  2.1 4.7 %collective-permute-start.3 = (bf16[16,4096]{1,0:T(8,128)(2,1)S(1)}, bf16[16,4096]{1,0:T(8,128)(2,1)S(1)}, u32[]{:S(2)}, u32[]{:S(2)}) collective-permute-start(bf16[16,4096]{1,0:T(8,128)(2,1)S(1)} %get-tuple-element.29), channel_id=1, source_target_pairs={{12,0},{8,4},{4,8},{0,12},{13,1},{9,5},{5,9},{1,13},{14,2},{10,6},... | collective-permute-start | bytes 393224 | tf_op jit(solution)/shard_map/ppermute | solution.py:17
  6.7 0.0 collective-permute-start.6
  6.7 1.5 %collective-permute-start = (bf16[16,4096]{1,0:T(8,128)(2,1)S(1)}, bf16[16,4096]{1,0:T(8,128)(2,1)S(1)}, u32[]{:S(2)}, u32[]{:S(2)}) collective-permute-start(bf16[16,4096]{1,0:T(8,128)(2,1)S(1)} %get-tuple-element.24.refs_6_), channel_id=1, source_target_pairs={{2,0},{3,1},{0,2},{1,3},{6,4},{7,5},{4,6},{5,7},{10,8},{11,9},{8,1... | collective-permute-start | bytes 393224 | tf_op jit(solution)/shard_map/ppermute | solution.py:17
  8.2 0.8 %collective-permute-start.2 = (bf16[16,4096]{1,0:T(8,128)(2,1)S(1)}, bf16[16,4096]{1,0:T(8,128)(2,1)S(1)}, u32[]{:S(2)}, u32[]{:S(2)}) collective-permute-start(bf16[16,4096]{1,0:T(8,128)(2,1)S(1)} %get-tuple-element.28), channel_id=1, source_target_pairs={{8,0},{12,4},{0,8},{4,12},{9,1},{13,5},{1,9},{5,13},{10,2},{14,6},... | collective-permute-start | bytes 393224 | tf_op jit(solution)/shard_map/ppermute | solution.py:17
  9.0 2.1 %collective-permute-done.3.refs_2_ = bf16[16,4096]{1,0:T(8,128)(2,1)S(1)} collective-permute-done((bf16[16,4096]{1,0:T(8,128)(2,1)S(1)}, bf16[16,4096]{1,0:T(8,128)(2,1)S(1)}, u32[]{:S(2)}, u32[]{:S(2)}) %collective-permute-start.3) | collective-permute-done | bytes 131104 | tf_op jit(solution)/shard_map/ppermute | solution.py:17
  11.1 1.6 %collective-permute-start.4 = (bf16[16,4096]{1,0:T(8,128)(2,1)S(1)}, bf16[16,4096]{1,0:T(8,128)(2,1)S(1)}, u32[]{:S(2)}, u32[]{:S(2)}) collective-permute-start(bf16[16,4096]{1,0:T(8,128)(2,1)S(1)} %collective-permute-done.3.refs_2_), channel_id=1, source_target_pairs={{2,0},{3,1},{0,2},{1,3},{6,4},{7,5},{4,6},{5,7},{10,8},{11,9},{8,1... | collective-permute-start | bytes 393224 | tf_op jit(solution)/shard_map/ppermute | solution.py:17
  12.8 2.0 %collective-permute-done.6.refs_4_ = bf16[16,4096]{1,0:T(8,128)(2,1)S(1)} collective-permute-done((bf16[16,4096]{1,0:T(8,128)(2,1)S(1)}, bf16[16,4096]{1,0:T(8,128)(2,1)S(1)}, u32[]{:S(2)}, u32[]{:S(2)}) %collective-permute-start.6) | collective-permute-done | bytes 131104 | tf_op jit(solution)/shard_map/ppermute | solution.py:17
  14.7 1.5 %collective-permute-start.7 = (bf16[16,4096]{1,0:T(8,128)(2,1)S(1)}, bf16[16,4096]{1,0:T(8,128)(2,1)S(1)}, u32[]{:S(2)}, u32[]{:S(2)}) collective-permute-start(bf16[16,4096]{1,0:T(8,128)(2,1)S(1)} %collective-permute-done.6.refs_4_), channel_id=1, source_target_pairs={{2,0},{3,1},{0,2},{1,3},{6,4},{7,5},{4,6},{5,7},{10,8},{11,9},{8,1... | collective-permute-start | bytes 393224 | tf_op jit(solution)/shard_map/ppermute | solution.py:17
  16.2 0.0 collective-permute-done.after_ref.refs_7_
  16.2 2.4 %prepare.1 = (bf16[128,192]{1,0:T(8,128)(2,1)S(1)}, bf16[3,192,4096]{2,1,0:T(8,128)(2,1)S(1)}) custom-call(s32[8,128]{1,0:T(8,128)} %bitcast.6, f32[8,128]{1,0:T(8,128)} %bitcast.7, bf16[3,192,4096]{2,1,0:T(8,128)(2,1)} %bitcast.4, bf16[16,4096]{1,0:T(8,128)(2,1)S(1)} %collective-permute-done.after_ref.refs_7_), custom_call_target="tpu_custom_call" | custom-call | bytes 9225000 | tf_op jit(solution)/shard_map/prepare/pallas_call | solution.py:120
  18.6 0.0 collective-permute-done.2.refs_2_
  18.6 1.3 %collective-permute-start.5 = (bf16[16,4096]{1,0:T(8,128)(2,1)S(1)}, bf16[16,4096]{1,0:T(8,128)(2,1)S(1)}, u32[]{:S(2)}, u32[]{:S(2)}) collective-permute-start(bf16[16,4096]{1,0:T(8,128)(2,1)S(1)} %collective-permute-done.2.refs_2_), channel_id=1, source_target_pairs={{2,0},{3,1},{0,2},{1,3},{6,4},{7,5},{4,6},{5,7},{10,8},{11,9},{8,1... | collective-permute-start | bytes 393224 | tf_op jit(solution)/shard_map/ppermute | solution.py:17
  19.9 0.0 collective-permute-done.4.refs_3_
  19.9 0.0 collective-permute-done.1.refs_1_
  19.9 2.4 %experts.2 = (f32[16,4096]{1,0:T(8,128)S(1)}, bf16[16,4096]{1,0:T(8,128)(2,1)S(1)}) custom-call(bf16[3,192,4096]{2,1,0:T(8,128)(2,1)S(1)} %get-tuple-element.26.refs_0_, bf16[3,192,4096]{2,1,0:T(8,128)(2,1)S(1)} %collective-permute-done.1.refs_1_, bf16[16,4096]{1,0:T(8,128)(2,1)S(1)} %collective-permute-done.3.refs_2_, ...), custom_call_target="tpu_custom_call" | custom-call | bytes 9225000 | tf_op jit(solution)/shard_map/experts/pallas_call | solution.py:173
  22.4 0.8 %collective-permute-start.10 = (bf16[16,4096]{1,0:T(8,128)(2,1)S(1)}, bf16[16,4096]{1,0:T(8,128)(2,1)S(1)}, u32[]{:S(2)}, u32[]{:S(2)}) collective-permute-start(bf16[16,4096]{1,0:T(8,128)(2,1)S(1)} %get-tuple-element.36), channel_id=1, source_target_pairs={{2,0},{3,1},{0,2},{1,3},{6,4},{7,5},{4,6},{5,7},{10,8},{11,9},{8,1... | collective-permute-start | bytes 393224 | tf_op jit(solution)/shard_map/ppermute | solution.py:17
  23.2 0.0 collective-permute-done.7.refs_5_
  23.2 0.7 %collective-permute-done.5.refs_3_ = bf16[16,4096]{1,0:T(8,128)(2,1)S(1)} collective-permute-done((bf16[16,4096]{1,0:T(8,128)(2,1)S(1)}, bf16[16,4096]{1,0:T(8,128)(2,1)S(1)}, u32[]{:S(2)}, u32[]{:S(2)}) %collective-permute-start.5) | collective-permute-done | bytes 131104 | tf_op jit(solution)/shard_map/ppermute | solution.py:17
  23.8 2.5 %experts.3 = (f32[16,4096]{1,0:T(8,128)S(1)}, bf16[16,4096]{1,0:T(8,128)(2,1)S(1)}, f32[16,4096]{1,0:T(8,128)S(1)}, bf16[16,4096]{1,0:T(8,128)(2,1)S(1)}, f32[16...) custom-call(bf16[3,192,4096]{2,1,0:T(8,128)(2,1)S(1)} %get-tuple-element.26.refs_0_, ...), custom_call_target="tpu_custom_call" | custom-call | bytes 9225000 | tf_op jit(solution)/shard_map/experts/pallas_call | solution.py:173
  26.4 1.2 %collective-permute-start.8 = (bf16[16,4096]{1,0:T(8,128)(2,1)S(1)}, bf16[16,4096]{1,0:T(8,128)(2,1)S(1)}, u32[]{:S(2)}, u32[]{:S(2)}) collective-permute-start(bf16[16,4096]{1,0:T(8,128)(2,1)S(1)} %get-tuple-element.35), channel_id=1, source_target_pairs={{2,0},{3,1},{0,2},{1,3},{6,4},{7,5},{4,6},{5,7},{10,8},{11,9},{8,1... | collective-permute-start | bytes 393224 | tf_op jit(solution)/shard_map/ppermute | solution.py:17
  27.5 0.0 collective-permute-done.10
  27.6 2.6 %collective-permute-start.11 = (bf16[16,4096]{1,0:T(8,128)(2,1)S(1)}, bf16[16,4096]{1,0:T(8,128)(2,1)S(1)}, u32[]{:S(2)}, u32[]{:S(2)}) collective-permute-start(bf16[16,4096]{1,0:T(8,128)(2,1)S(1)} %add_convert_fusion.1), channel_id=1, source_target_pairs={{12,0},{8,4},{4,8},{0,12},{13,1},{9,5},{5,9},{1,13},{14,2},{10,6},... | collective-permute-start | bytes 393224 | tf_op jit(solution)/shard_map/ppermute | solution.py:17
  30.2 0.5 %collective-permute-start.12 = (bf16[16,4096]{1,0:T(8,128)(2,1)S(1)}, bf16[16,4096]{1,0:T(8,128)(2,1)S(1)}, u32[]{:S(2)}, u32[]{:S(2)}) collective-permute-start(bf16[16,4096]{1,0:T(8,128)(2,1)S(1)} %get-tuple-element.40), channel_id=1, source_target_pairs={{2,0},{3,1},{0,2},{1,3},{6,4},{7,5},{4,6},{5,7},{10,8},{11,9},{8,1... | collective-permute-start | bytes 393224 | tf_op jit(solution)/shard_map/ppermute | solution.py:17
  30.7 1.2 %collective-permute-done.8 = bf16[16,4096]{1,0:T(8,128)(2,1)S(1)} collective-permute-done((bf16[16,4096]{1,0:T(8,128)(2,1)S(1)}, bf16[16,4096]{1,0:T(8,128)(2,1)S(1)}, u32[]{:S(2)}, u32[]{:S(2)}) %collective-permute-start.8) | collective-permute-done | bytes 131104 | tf_op jit(solution)/shard_map/ppermute | solution.py:17
  31.9 2.1 %collective-permute-start.9 = (bf16[16,4096]{1,0:T(8,128)(2,1)S(1)}, bf16[16,4096]{1,0:T(8,128)(2,1)S(1)}, u32[]{:S(2)}, u32[]{:S(2)}) collective-permute-start(bf16[16,4096]{1,0:T(8,128)(2,1)S(1)} %add_convert_fusion.2), channel_id=1, source_target_pairs={{8,0},{12,4},{0,8},{4,12},{9,1},{13,5},{1,9},{5,13},{10,2},{14,6},... | collective-permute-start | bytes 393224 | tf_op jit(solution)/shard_map/ppermute | solution.py:17
  34.0 1.1 %collective-permute-done.12 = bf16[16,4096]{1,0:T(8,128)(2,1)S(1)} collective-permute-done((bf16[16,4096]{1,0:T(8,128)(2,1)S(1)}, bf16[16,4096]{1,0:T(8,128)(2,1)S(1)}, u32[]{:S(2)}, u32[]{:S(2)}) %collective-permute-start.12) | collective-permute-done | bytes 131104 | tf_op jit(solution)/shard_map/ppermute | solution.py:17
  35.2 0.4 collective-permute-start.13
  35.6 1.3 %collective-permute-start.14 = (bf16[16,4096]{1,0:T(8,128)(2,1)S(1)}, bf16[16,4096]{1,0:T(8,128)(2,1)S(1)}, u32[]{:S(2)}, u32[]{:S(2)}) collective-permute-start(bf16[16,4096]{1,0:T(8,128)(2,1)S(1)} %get-tuple-element.42), channel_id=1, source_target_pairs={{2,0},{3,1},{0,2},{1,3},{6,4},{7,5},{4,6},{5,7},{10,8},{11,9},{8,1... | collective-permute-start | bytes 393224 | tf_op jit(solution)/shard_map/ppermute | solution.py:17
  36.8 0.0 collective-permute-done.11.refs_1_
  36.8 3.8 %collective-permute-done.9.refs_0_ = bf16[16,4096]{1,0:T(8,128)(2,1)S(1)} collective-permute-done((bf16[16,4096]{1,0:T(8,128)(2,1)S(1)}, bf16[16,4096]{1,0:T(8,128)(2,1)S(1)}, u32[]{:S(2)}, u32[]{:S(2)}) %collective-permute-start.9) | collective-permute-done | bytes 131104 | tf_op jit(solution)/shard_map/ppermute | solution.py:17
  40.7 0.7 %collective-permute-done.13.refs_3_ = bf16[16,4096]{1,0:T(8,128)(2,1)S(1)} collective-permute-done((bf16[16,4096]{1,0:T(8,128)(2,1)S(1)}, bf16[16,4096]{1,0:T(8,128)(2,1)S(1)}, u32[]{:S(2)}, u32[]{:S(2)}) %collective-permute-start.13) | collective-permute-done | bytes 131104 | tf_op jit(solution)/shard_map/ppermute | solution.py:17
  41.3 0.0 collective-permute-done.14.refs_4_
  41.4 1.2 %combine.1 = bf16[128,4096]{1,0:T(8,128)(2,1)} custom-call(bf16[128,192]{1,0:T(8,128)(2,1)S(1)} %get-tuple-element.25.mix_ref, bf16[16,4096]{1,0:T(8,128)(2,1)S(1)} %collective-permute-done.9.refs_0_, bf16[16,4096]{1,0:T(8,128)(2,1)S(1)} %collective-permute-done.11.refs_1_, f32[16,4096]{1,0:T(8,128)S(1)} %get-tuple-element.37.refs_2_, ...), custom_call_target="tpu_custom_call" | custom-call | bytes 4428000 | tf_op jit(solution)/shard_map/combine/pallas_call | solution.py:220
  (3 shorter events, 0.1 us)
Async XLA Ops:
  1.5 18.4 %collective-permute-start.1 = (bf16[3,192,4096]{2,1,0:T(8,128)(2,1)}, bf16[3,192,4096]{2,1,0:T(8,128)(2,1)S(1)}, u32[]{:S(2)}, u32[]{:S(2)}) collective-permute-start(bf16[3,192,4096]{2,1,0:T(8,128)(2,1)} %bitcast.3), channel_id=1, source_target_pairs={{1,0},{0,1},{3,2},{2,3},{5,4},{4,5},{7,6},{6,7},{9,8},{8,9},{11,10... | collective-permute-start | bytes 14155784 | tf_op jit(solution)/shard_map/ppermute | solution.py:17
  2.1 9.1 %collective-permute-start.3 = (bf16[16,4096]{1,0:T(8,128)(2,1)S(1)}, bf16[16,4096]{1,0:T(8,128)(2,1)S(1)}, u32[]{:S(2)}, u32[]{:S(2)}) collective-permute-start(bf16[16,4096]{1,0:T(8,128)(2,1)S(1)} %get-tuple-element.29), channel_id=1, source_target_pairs={{12,0},{8,4},{4,8},{0,12},{13,1},{9,5},{5,9},{1,13},{14,2},{10,6},... | collective-permute-start | bytes 393224 | tf_op jit(solution)/shard_map/ppermute | solution.py:17
  6.7 8.0 %collective-permute-start.6 = (bf16[16,4096]{1,0:T(8,128)(2,1)S(1)}, bf16[16,4096]{1,0:T(8,128)(2,1)S(1)}, u32[]{:S(2)}, u32[]{:S(2)}) collective-permute-start(bf16[16,4096]{1,0:T(8,128)(2,1)S(1)} %get-tuple-element.33), channel_id=1, source_target_pairs={{4,0},{0,4},{12,8},{8,12},{5,1},{1,5},{13,9},{9,13},{6,2},{2,6},{1... | collective-permute-start | bytes 393224 | tf_op jit(solution)/shard_map/ppermute | solution.py:17
  6.7 9.5 %collective-permute-start = (bf16[16,4096]{1,0:T(8,128)(2,1)S(1)}, bf16[16,4096]{1,0:T(8,128)(2,1)S(1)}, u32[]{:S(2)}, u32[]{:S(2)}) collective-permute-start(bf16[16,4096]{1,0:T(8,128)(2,1)S(1)} %get-tuple-element.24.refs_6_), channel_id=1, source_target_pairs={{2,0},{3,1},{0,2},{1,3},{6,4},{7,5},{4,6},{5,7},{10,8},{11,9},{8,1... | collective-permute-start | bytes 393224 | tf_op jit(solution)/shard_map/ppermute | solution.py:17
  8.2 10.4 %collective-permute-start.2 = (bf16[16,4096]{1,0:T(8,128)(2,1)S(1)}, bf16[16,4096]{1,0:T(8,128)(2,1)S(1)}, u32[]{:S(2)}, u32[]{:S(2)}) collective-permute-start(bf16[16,4096]{1,0:T(8,128)(2,1)S(1)} %get-tuple-element.28), channel_id=1, source_target_pairs={{8,0},{12,4},{0,8},{4,12},{9,1},{13,5},{1,9},{5,13},{10,2},{14,6},... | collective-permute-start | bytes 393224 | tf_op jit(solution)/shard_map/ppermute | solution.py:17
  11.1 8.8 %collective-permute-start.4 = (bf16[16,4096]{1,0:T(8,128)(2,1)S(1)}, bf16[16,4096]{1,0:T(8,128)(2,1)S(1)}, u32[]{:S(2)}, u32[]{:S(2)}) collective-permute-start(bf16[16,4096]{1,0:T(8,128)(2,1)S(1)} %collective-permute-done.3.refs_2_), channel_id=1, source_target_pairs={{2,0},{3,1},{0,2},{1,3},{6,4},{7,5},{4,6},{5,7},{10,8},{11,9},{8,1... | collective-permute-start | bytes 393224 | tf_op jit(solution)/shard_map/ppermute | solution.py:17
  14.7 8.4 %collective-permute-start.7 = (bf16[16,4096]{1,0:T(8,128)(2,1)S(1)}, bf16[16,4096]{1,0:T(8,128)(2,1)S(1)}, u32[]{:S(2)}, u32[]{:S(2)}) collective-permute-start(bf16[16,4096]{1,0:T(8,128)(2,1)S(1)} %collective-permute-done.6.refs_4_), channel_id=1, source_target_pairs={{2,0},{3,1},{0,2},{1,3},{6,4},{7,5},{4,6},{5,7},{10,8},{11,9},{8,1... | collective-permute-start | bytes 393224 | tf_op jit(solution)/shard_map/ppermute | solution.py:17
  18.6 5.2 %collective-permute-start.5 = (bf16[16,4096]{1,0:T(8,128)(2,1)S(1)}, bf16[16,4096]{1,0:T(8,128)(2,1)S(1)}, u32[]{:S(2)}, u32[]{:S(2)}) collective-permute-start(bf16[16,4096]{1,0:T(8,128)(2,1)S(1)} %collective-permute-done.2.refs_2_), channel_id=1, source_target_pairs={{2,0},{3,1},{0,2},{1,3},{6,4},{7,5},{4,6},{5,7},{10,8},{11,9},{8,1... | collective-permute-start | bytes 393224 | tf_op jit(solution)/shard_map/ppermute | solution.py:17
  22.4 5.2 %collective-permute-start.10 = (bf16[16,4096]{1,0:T(8,128)(2,1)S(1)}, bf16[16,4096]{1,0:T(8,128)(2,1)S(1)}, u32[]{:S(2)}, u32[]{:S(2)}) collective-permute-start(bf16[16,4096]{1,0:T(8,128)(2,1)S(1)} %get-tuple-element.36), channel_id=1, source_target_pairs={{2,0},{3,1},{0,2},{1,3},{6,4},{7,5},{4,6},{5,7},{10,8},{11,9},{8,1... | collective-permute-start | bytes 393224 | tf_op jit(solution)/shard_map/ppermute | solution.py:17
  26.4 5.5 %collective-permute-start.8 = (bf16[16,4096]{1,0:T(8,128)(2,1)S(1)}, bf16[16,4096]{1,0:T(8,128)(2,1)S(1)}, u32[]{:S(2)}, u32[]{:S(2)}) collective-permute-start(bf16[16,4096]{1,0:T(8,128)(2,1)S(1)} %get-tuple-element.35), channel_id=1, source_target_pairs={{2,0},{3,1},{0,2},{1,3},{6,4},{7,5},{4,6},{5,7},{10,8},{11,9},{8,1... | collective-permute-start | bytes 393224 | tf_op jit(solution)/shard_map/ppermute | solution.py:17
  27.6 9.3 %collective-permute-start.11 = (bf16[16,4096]{1,0:T(8,128)(2,1)S(1)}, bf16[16,4096]{1,0:T(8,128)(2,1)S(1)}, u32[]{:S(2)}, u32[]{:S(2)}) collective-permute-start(bf16[16,4096]{1,0:T(8,128)(2,1)S(1)} %add_convert_fusion.1), channel_id=1, source_target_pairs={{12,0},{8,4},{4,8},{0,12},{13,1},{9,5},{5,9},{1,13},{14,2},{10,6},... | collective-permute-start | bytes 393224 | tf_op jit(solution)/shard_map/ppermute | solution.py:17
  30.2 5.0 %collective-permute-start.12 = (bf16[16,4096]{1,0:T(8,128)(2,1)S(1)}, bf16[16,4096]{1,0:T(8,128)(2,1)S(1)}, u32[]{:S(2)}, u32[]{:S(2)}) collective-permute-start(bf16[16,4096]{1,0:T(8,128)(2,1)S(1)} %get-tuple-element.40), channel_id=1, source_target_pairs={{2,0},{3,1},{0,2},{1,3},{6,4},{7,5},{4,6},{5,7},{10,8},{11,9},{8,1... | collective-permute-start | bytes 393224 | tf_op jit(solution)/shard_map/ppermute | solution.py:17
  31.9 8.8 %collective-permute-start.9 = (bf16[16,4096]{1,0:T(8,128)(2,1)S(1)}, bf16[16,4096]{1,0:T(8,128)(2,1)S(1)}, u32[]{:S(2)}, u32[]{:S(2)}) collective-permute-start(bf16[16,4096]{1,0:T(8,128)(2,1)S(1)} %add_convert_fusion.2), channel_id=1, source_target_pairs={{8,0},{12,4},{0,8},{4,12},{9,1},{13,5},{1,9},{5,13},{10,2},{14,6},... | collective-permute-start | bytes 393224 | tf_op jit(solution)/shard_map/ppermute | solution.py:17
  35.2 6.2 %collective-permute-start.13 = (bf16[16,4096]{1,0:T(8,128)(2,1)S(1)}, bf16[16,4096]{1,0:T(8,128)(2,1)S(1)}, u32[]{:S(2)}, u32[]{:S(2)}) collective-permute-start(bf16[16,4096]{1,0:T(8,128)(2,1)S(1)} %add_convert_fusion), channel_id=1, source_target_pairs={{4,0},{0,4},{12,8},{8,12},{5,1},{1,5},{13,9},{9,13},{6,2},{2,6},{1... | collective-permute-start | bytes 393224 | tf_op jit(solution)/shard_map/ppermute | solution.py:17
  35.6 5.8 %collective-permute-start.14 = (bf16[16,4096]{1,0:T(8,128)(2,1)S(1)}, bf16[16,4096]{1,0:T(8,128)(2,1)S(1)}, u32[]{:S(2)}, u32[]{:S(2)}) collective-permute-start(bf16[16,4096]{1,0:T(8,128)(2,1)S(1)} %get-tuple-element.42), channel_id=1, source_target_pairs={{2,0},{3,1},{0,2},{1,3},{6,4},{7,5},{4,6},{5,7},{10,8},{11,9},{8,1... | collective-permute-start | bytes 393224 | tf_op jit(solution)/shard_map/ppermute | solution.py:17

commit v5 on v3

--- a/solution.py
+++ b/solution.py
@@ -250,7 +250,7 @@
     across(0)
     for m in [*soon, *near, *late]:
         blocks[m, 0] = swap(outgoing[m], "dp", m)
-    sibling = swap(after(own, outgoing[0]), "expert", 1)
+    sibling = swap(own, "expert", 1)
     order = [*soon, *late, 0, *near]
     mix, own = prepare(assign, probs, own, order, cap, blocks[0, chips - 1])
     for m in soon:

time: 42.6 us -> 42.7 us (level)
  transfers between devices with their start and end apart: 16 -> 16, of which waited for: 9 -> 8; matrix products, arithmetic and copies ran while one was open for 0% -> 0% of each run, Pallas kernels for 17% -> 21%
where the time goes in v5:
time: 42.7 us; the launch traced here: 42.5 us
  starting transfers between devices  21.5 us (50%)
  waiting for transfers between devices  10.8 us (25%)
  Pallas kernels  10.1 us (24%)
    ppermute x16, starting transfers between devices, swap(): return lax.ppermute(block, axis, route)  21.5 us
    ppermute x16, waiting for transfers between devices, swap(): return lax.ppermute(block, axis, route)  10.8 us
    pallas_call x2, Pallas kernels, expert_part(): pl.pallas_call(functools.partial(expert_kernel, len(keys), steps), out_sh...  4.95 us
    pallas_call x1, Pallas kernels, prepare(): pl.pallas_call(functools.partial(prepare_kernel, masks, cap), out_shape=[...  2.4 us
    pallas_call x1, Pallas kernels, dispatch(): pl.pallas_call(functools.partial(dispatch_kernel, masks, cap, steps), out...  1.53 us
    pallas_call x1, Pallas kernels, combine(): pl.pallas_call(functools.partial(combine_kernel, count, near, chips, step...  1.23 us
  transfers between devices with their start and end apart: 16, of which 8 were waited for; matrix products, arithmetic and copies ran while one was open for 0% of the time, Pallas kernels for 21%

profile of v5, /device:TPU:0, one launch (start us, length us, event | category | flops | bytes accessed | tf_op | source)
XLA Modules:
  0.0 42.5 jit_solution(11259948567922717628)
XLA Ops:
  0.0 0.5 %collective-permute-start.1 = (bf16[3,192,4096]{2,1,0:T(8,128)(2,1)}, bf16[3,192,4096]{2,1,0:T(8,128)(2,1)S(1)}, u32[]{:S(2)}, u32[]{:S(2)}) collective-permute-start(bf16[3,192,4096]{2,1,0:T(8,128)(2,1)} %bitcast.3), channel_id=1, source_target_pairs={{1,0},{0,1},{3,2},{2,3},{5,4},{4,5},{7,6},{6,7},{9,8},{8,9},{11,10... | collective-permute-start | bytes 14155784 | tf_op jit(solution)/shard_map/ppermute | solution.py:17
  0.5 1.5 %dispatch.1 = (bf16[16,4096]{1,0:T(8,128)(2,1)S(1)}, bf16[16,4096]{1,0:T(8,128)(2,1)S(1)}, bf16[16,4096]{1,0:T(8,128)(2,1)S(1)}, bf16[16,4096]{1,0:T(8,128)(2,1)S(1)}) custom-call(s32[8,128]{1,0:T(8,128)} %bitcast.5, bf16[128,4096]{1,0:T(8,128)(2,1)} %tok_ref.1), custom_call_target="tpu_custom_call" | custom-call | bytes 3690000 | tf_op jit(solution)/shard_map/dispatch/pallas_call | solution.py:79
  2.0 4.7 %collective-permute-start.3 = (bf16[16,4096]{1,0:T(8,128)(2,1)S(1)}, bf16[16,4096]{1,0:T(8,128)(2,1)S(1)}, u32[]{:S(2)}, u32[]{:S(2)}) collective-permute-start(bf16[16,4096]{1,0:T(8,128)(2,1)S(1)} %get-tuple-element.29), channel_id=1, source_target_pairs={{12,0},{8,4},{4,8},{0,12},{13,1},{9,5},{5,9},{1,13},{14,2},{10,6},... | collective-permute-start | bytes 393224 | tf_op jit(solution)/shard_map/ppermute | solution.py:17
  6.7 0.0 collective-permute-start.6
  6.7 1.5 %collective-permute-start = (bf16[16,4096]{1,0:T(8,128)(2,1)S(1)}, bf16[16,4096]{1,0:T(8,128)(2,1)S(1)}, u32[]{:S(2)}, u32[]{:S(2)}) collective-permute-start(bf16[16,4096]{1,0:T(8,128)(2,1)S(1)} %get-tuple-element.25.refs_6_), channel_id=1, source_target_pairs={{2,0},{3,1},{0,2},{1,3},{6,4},{7,5},{4,6},{5,7},{10,8},{11,9},{8,1... | collective-permute-start | bytes 393224 | tf_op jit(solution)/shard_map/ppermute | solution.py:17
  8.2 0.8 %collective-permute-start.2 = (bf16[16,4096]{1,0:T(8,128)(2,1)S(1)}, bf16[16,4096]{1,0:T(8,128)(2,1)S(1)}, u32[]{:S(2)}, u32[]{:S(2)}) collective-permute-start(bf16[16,4096]{1,0:T(8,128)(2,1)S(1)} %get-tuple-element.28), channel_id=1, source_target_pairs={{8,0},{12,4},{0,8},{4,12},{9,1},{13,5},{1,9},{5,13},{10,2},{14,6},... | collective-permute-start | bytes 393224 | tf_op jit(solution)/shard_map/ppermute | solution.py:17
  9.0 2.1 %collective-permute-done.3.refs_2_ = bf16[16,4096]{1,0:T(8,128)(2,1)S(1)} collective-permute-done((bf16[16,4096]{1,0:T(8,128)(2,1)S(1)}, bf16[16,4096]{1,0:T(8,128)(2,1)S(1)}, u32[]{:S(2)}, u32[]{:S(2)}) %collective-permute-start.3) | collective-permute-done | bytes 131104 | tf_op jit(solution)/shard_map/ppermute | solution.py:17
  11.1 1.6 %collective-permute-start.4 = (bf16[16,4096]{1,0:T(8,128)(2,1)S(1)}, bf16[16,4096]{1,0:T(8,128)(2,1)S(1)}, u32[]{:S(2)}, u32[]{:S(2)}) collective-permute-start(bf16[16,4096]{1,0:T(8,128)(2,1)S(1)} %collective-permute-done.3.refs_2_), channel_id=1, source_target_pairs={{2,0},{3,1},{0,2},{1,3},{6,4},{7,5},{4,6},{5,7},{10,8},{11,9},{8,1... | collective-permute-start | bytes 393224 | tf_op jit(solution)/shard_map/ppermute | solution.py:17
  12.7 2.1 %collective-permute-done.6.refs_4_ = bf16[16,4096]{1,0:T(8,128)(2,1)S(1)} collective-permute-done((bf16[16,4096]{1,0:T(8,128)(2,1)S(1)}, bf16[16,4096]{1,0:T(8,128)(2,1)S(1)}, u32[]{:S(2)}, u32[]{:S(2)}) %collective-permute-start.6) | collective-permute-done | bytes 131104 | tf_op jit(solution)/shard_map/ppermute | solution.py:17
  14.7 1.5 %collective-permute-start.7 = (bf16[16,4096]{1,0:T(8,128)(2,1)S(1)}, bf16[16,4096]{1,0:T(8,128)(2,1)S(1)}, u32[]{:S(2)}, u32[]{:S(2)}) collective-permute-start(bf16[16,4096]{1,0:T(8,128)(2,1)S(1)} %collective-permute-done.6.refs_4_), channel_id=1, source_target_pairs={{2,0},{3,1},{0,2},{1,3},{6,4},{7,5},{4,6},{5,7},{10,8},{11,9},{8,1... | collective-permute-start | bytes 393224 | tf_op jit(solution)/shard_map/ppermute | solution.py:17
  16.2 0.0 collective-permute-done.after_ref.refs_7_
  16.2 2.4 %prepare.1 = (bf16[128,192]{1,0:T(8,128)(2,1)S(1)}, bf16[3,192,4096]{2,1,0:T(8,128)(2,1)S(1)}) custom-call(s32[8,128]{1,0:T(8,128)} %bitcast.6, f32[8,128]{1,0:T(8,128)} %bitcast.7, bf16[3,192,4096]{2,1,0:T(8,128)(2,1)} %bitcast.4, bf16[16,4096]{1,0:T(8,128)(2,1)S(1)} %collective-permute-done.after_ref.refs_7_), custom_call_target="tpu_custom_call" | custom-call | bytes 9225000 | tf_op jit(solution)/shard_map/prepare/pallas_call | solution.py:120
  18.6 0.0 collective-permute-done.2.refs_2_
  18.6 1.3 %collective-permute-start.5 = (bf16[16,4096]{1,0:T(8,128)(2,1)S(1)}, bf16[16,4096]{1,0:T(8,128)(2,1)S(1)}, u32[]{:S(2)}, u32[]{:S(2)}) collective-permute-start(bf16[16,4096]{1,0:T(8,128)(2,1)S(1)} %collective-permute-done.2.refs_2_), channel_id=1, source_target_pairs={{2,0},{3,1},{0,2},{1,3},{6,4},{7,5},{4,6},{5,7},{10,8},{11,9},{8,1... | collective-permute-start | bytes 393224 | tf_op jit(solution)/shard_map/ppermute | solution.py:17
  19.9 0.0 collective-permute-done.4.refs_3_
  19.9 0.0 collective-permute-done.1.refs_1_
  19.9 2.4 %experts.2 = (f32[16,4096]{1,0:T(8,128)S(1)}, bf16[16,4096]{1,0:T(8,128)(2,1)S(1)}) custom-call(bf16[3,192,4096]{2,1,0:T(8,128)(2,1)S(1)} %get-tuple-element.27.refs_0_, bf16[3,192,4096]{2,1,0:T(8,128)(2,1)S(1)} %collective-permute-done.1.refs_1_, bf16[16,4096]{1,0:T(8,128)(2,1)S(1)} %collective-permute-done.3.refs_2_, ...), custom_call_target="tpu_custom_call" | custom-call | bytes 9225000 | tf_op jit(solution)/shard_map/experts/pallas_call | solution.py:173
  22.3 0.8 %collective-permute-start.8 = (bf16[16,4096]{1,0:T(8,128)(2,1)S(1)}, bf16[16,4096]{1,0:T(8,128)(2,1)S(1)}, u32[]{:S(2)}, u32[]{:S(2)}) collective-permute-start(bf16[16,4096]{1,0:T(8,128)(2,1)S(1)} %get-tuple-element.36), channel_id=1, source_target_pairs={{2,0},{3,1},{0,2},{1,3},{6,4},{7,5},{4,6},{5,7},{10,8},{11,9},{8,1... | collective-permute-start | bytes 393224 | tf_op jit(solution)/shard_map/ppermute | solution.py:17
  23.2 0.0 collective-permute-done.7.refs_5_
  23.2 0.7 %collective-permute-done.5.refs_3_ = bf16[16,4096]{1,0:T(8,128)(2,1)S(1)} collective-permute-done((bf16[16,4096]{1,0:T(8,128)(2,1)S(1)}, bf16[16,4096]{1,0:T(8,128)(2,1)S(1)}, u32[]{:S(2)}, u32[]{:S(2)}) %collective-permute-start.5) | collective-permute-done | bytes 131104 | tf_op jit(solution)/shard_map/ppermute | solution.py:17
  23.9 2.5 %experts.3 = (f32[16,4096]{1,0:T(8,128)S(1)}, bf16[16,4096]{1,0:T(8,128)(2,1)S(1)}, bf16[16,4096]{1,0:T(8,128)(2,1)S(1)}, bf16[16,4096]{1,0:T(8,128)(2,1)S(1)}, ...) custom-call(bf16[3,192,4096]{2,1,0:T(8,128)(2,1)S(1)} %get-tuple-element.27.refs_0_, ...), custom_call_target="tpu_custom_call" | custom-call | bytes 9225000 | tf_op jit(solution)/shard_map/experts/pallas_call | solution.py:173
  26.4 0.9 %collective-permute-done.8 = bf16[16,4096]{1,0:T(8,128)(2,1)S(1)} collective-permute-done((bf16[16,4096]{1,0:T(8,128)(2,1)S(1)}, bf16[16,4096]{1,0:T(8,128)(2,1)S(1)}, u32[]{:S(2)}, u32[]{:S(2)}) %collective-permute-start.8) | collective-permute-done | bytes 131104 | tf_op jit(solution)/shard_map/ppermute | solution.py:17
  27.3 0.6 %collective-permute-start.14 = (bf16[16,4096]{1,0:T(8,128)(2,1)S(1)}, bf16[16,4096]{1,0:T(8,128)(2,1)S(1)}, u32[]{:S(2)}, u32[]{:S(2)}) collective-permute-start(bf16[16,4096]{1,0:T(8,128)(2,1)S(1)} %get-tuple-element.44), channel_id=1, source_target_pairs={{4,0},{0,4},{12,8},{8,12},{5,1},{1,5},{13,9},{9,13},{6,2},{2,6},{1... | collective-permute-start | bytes 393224 | tf_op jit(solution)/shard_map/ppermute | solution.py:17
  28.0 1.3 %collective-permute-start.9 = (bf16[16,4096]{1,0:T(8,128)(2,1)S(1)}, bf16[16,4096]{1,0:T(8,128)(2,1)S(1)}, u32[]{:S(2)}, u32[]{:S(2)}) collective-permute-start(bf16[16,4096]{1,0:T(8,128)(2,1)S(1)} %get-tuple-element.37), channel_id=1, source_target_pairs={{2,0},{3,1},{0,2},{1,3},{6,4},{7,5},{4,6},{5,7},{10,8},{11,9},{8,1... | collective-permute-start | bytes 393224 | tf_op jit(solution)/shard_map/ppermute | solution.py:17
  29.3 2.2 %collective-permute-start.11 = (bf16[16,4096]{1,0:T(8,128)(2,1)S(1)}, bf16[16,4096]{1,0:T(8,128)(2,1)S(1)}, u32[]{:S(2)}, u32[]{:S(2)}) collective-permute-start(bf16[16,4096]{1,0:T(8,128)(2,1)S(1)} %add_convert_fusion), channel_id=1, source_target_pairs={{12,0},{8,4},{4,8},{0,12},{13,1},{9,5},{5,9},{1,13},{14,2},{10,6},... | collective-permute-start | bytes 393224 | tf_op jit(solution)/shard_map/ppermute | solution.py:17
  31.5 0.4 %collective-permute-start.13 = (bf16[16,4096]{1,0:T(8,128)(2,1)S(1)}, bf16[16,4096]{1,0:T(8,128)(2,1)S(1)}, u32[]{:S(2)}, u32[]{:S(2)}) collective-permute-start(bf16[16,4096]{1,0:T(8,128)(2,1)S(1)} %get-tuple-element.42), channel_id=1, source_target_pairs={{2,0},{3,1},{0,2},{1,3},{6,4},{7,5},{4,6},{5,7},{10,8},{11,9},{8,1... | collective-permute-start | bytes 393224 | tf_op jit(solution)/shard_map/ppermute | solution.py:17
  31.9 1.1 %collective-permute-start.12 = (bf16[16,4096]{1,0:T(8,128)(2,1)S(1)}, bf16[16,4096]{1,0:T(8,128)(2,1)S(1)}, u32[]{:S(2)}, u32[]{:S(2)}) collective-permute-start(bf16[16,4096]{1,0:T(8,128)(2,1)S(1)} %get-tuple-element.40), channel_id=1, source_target_pairs={{4,0},{0,4},{12,8},{8,12},{5,1},{1,5},{13,9},{9,13},{6,2},{2,6},{1... | collective-permute-start | bytes 393224 | tf_op jit(solution)/shard_map/ppermute | solution.py:17
  33.0 1.0 %collective-permute-done.14 = bf16[16,4096]{1,0:T(8,128)(2,1)S(1)} collective-permute-done((bf16[16,4096]{1,0:T(8,128)(2,1)S(1)}, bf16[16,4096]{1,0:T(8,128)(2,1)S(1)}, u32[]{:S(2)}, u32[]{:S(2)}) %collective-permute-start.14) | collective-permute-done | bytes 131104 | tf_op jit(solution)/shard_map/ppermute | solution.py:17
  34.0 1.2 %collective-permute-start.15 = (bf16[16,4096]{1,0:T(8,128)(2,1)S(1)}, bf16[16,4096]{1,0:T(8,128)(2,1)S(1)}, u32[]{:S(2)}, u32[]{:S(2)}) collective-permute-start(bf16[16,4096]{1,0:T(8,128)(2,1)S(1)} %collective-permute-done.14), channel_id=1, source_target_pairs={{2,0},{3,1},{0,2},{1,3},{6,4},{7,5},{4,6},{5,7},{10,8},{11,9},{8,1... | collective-permute-start | bytes 393224 | tf_op jit(solution)/shard_map/ppermute | solution.py:17
  35.3 0.0 collective-permute-done.9
  35.3 1.9 %collective-permute-start.10 = (bf16[16,4096]{1,0:T(8,128)(2,1)S(1)}, bf16[16,4096]{1,0:T(8,128)(2,1)S(1)}, u32[]{:S(2)}, u32[]{:S(2)}) collective-permute-start(bf16[16,4096]{1,0:T(8,128)(2,1)S(1)} %add_convert_fusion.1), channel_id=1, source_target_pairs={{8,0},{12,4},{0,8},{4,12},{9,1},{13,5},{1,9},{5,13},{10,2},{14,6},... | collective-permute-start | bytes 393224 | tf_op jit(solution)/shard_map/ppermute | solution.py:17
  37.2 0.4 %collective-permute-done.11.refs_1_ = bf16[16,4096]{1,0:T(8,128)(2,1)S(1)} collective-permute-done((bf16[16,4096]{1,0:T(8,128)(2,1)S(1)}, bf16[16,4096]{1,0:T(8,128)(2,1)S(1)}, u32[]{:S(2)}, u32[]{:S(2)}) %collective-permute-start.11) | collective-permute-done | bytes 131104 | tf_op jit(solution)/shard_map/ppermute | solution.py:17
  37.7 0.0 collective-permute-done.13.refs_4_
  37.7 1.4 %collective-permute-done.12.refs_3_ = bf16[16,4096]{1,0:T(8,128)(2,1)S(1)} collective-permute-done((bf16[16,4096]{1,0:T(8,128)(2,1)S(1)}, bf16[16,4096]{1,0:T(8,128)(2,1)S(1)}, u32[]{:S(2)}, u32[]{:S(2)}) %collective-permute-start.12) | collective-permute-done | bytes 131104 | tf_op jit(solution)/shard_map/ppermute | solution.py:17
  39.0 0.0 collective-permute-done.15.refs_5_
  39.0 2.2 %collective-permute-done.10.refs_0_ = bf16[16,4096]{1,0:T(8,128)(2,1)S(1)} collective-permute-done((bf16[16,4096]{1,0:T(8,128)(2,1)S(1)}, bf16[16,4096]{1,0:T(8,128)(2,1)S(1)}, u32[]{:S(2)}, u32[]{:S(2)}) %collective-permute-start.10) | collective-permute-done | bytes 131104 | tf_op jit(solution)/shard_map/ppermute | solution.py:17
  41.2 1.2 %combine.1 = bf16[128,4096]{1,0:T(8,128)(2,1)} custom-call(bf16[128,192]{1,0:T(8,128)(2,1)S(1)} %get-tuple-element.26.mix_ref, bf16[16,4096]{1,0:T(8,128)(2,1)S(1)} %collective-permute-done.10.refs_0_, bf16[16,4096]{1,0:T(8,128)(2,1)S(1)} %collective-permute-done.11.refs_1_, f32[16,4096]{1,0:T(8,128)S(1)} %get-tuple-element.38.refs_2_, ...), custom_call_target="tpu_custom_call" | custom-call | bytes 4428000 | tf_op jit(solution)/shard_map/combine/pallas_call | solution.py:214
  (2 shorter events, 0.1 us)
Async XLA Ops:
  0.0 19.9 %collective-permute-start.1 = (bf16[3,192,4096]{2,1,0:T(8,128)(2,1)}, bf16[3,192,4096]{2,1,0:T(8,128)(2,1)S(1)}, u32[]{:S(2)}, u32[]{:S(2)}) collective-permute-start(bf16[3,192,4096]{2,1,0:T(8,128)(2,1)} %bitcast.3), channel_id=1, source_target_pairs={{1,0},{0,1},{3,2},{2,3},{5,4},{4,5},{7,6},{6,7},{9,8},{8,9},{11,10... | collective-permute-start | bytes 14155784 | tf_op jit(solution)/shard_map/ppermute | solution.py:17
  2.0 9.1 %collective-permute-start.3 = (bf16[16,4096]{1,0:T(8,128)(2,1)S(1)}, bf16[16,4096]{1,0:T(8,128)(2,1)S(1)}, u32[]{:S(2)}, u32[]{:S(2)}) collective-permute-start(bf16[16,4096]{1,0:T(8,128)(2,1)S(1)} %get-tuple-element.29), channel_id=1, source_target_pairs={{12,0},{8,4},{4,8},{0,12},{13,1},{9,5},{5,9},{1,13},{14,2},{10,6},... | collective-permute-start | bytes 393224 | tf_op jit(solution)/shard_map/ppermute | solution.py:17
  6.7 8.1 %collective-permute-start.6 = (bf16[16,4096]{1,0:T(8,128)(2,1)S(1)}, bf16[16,4096]{1,0:T(8,128)(2,1)S(1)}, u32[]{:S(2)}, u32[]{:S(2)}) collective-permute-start(bf16[16,4096]{1,0:T(8,128)(2,1)S(1)} %get-tuple-element.33), channel_id=1, source_target_pairs={{4,0},{0,4},{12,8},{8,12},{5,1},{1,5},{13,9},{9,13},{6,2},{2,6},{1... | collective-permute-start | bytes 393224 | tf_op jit(solution)/shard_map/ppermute | solution.py:17
  6.7 9.6 %collective-permute-start = (bf16[16,4096]{1,0:T(8,128)(2,1)S(1)}, bf16[16,4096]{1,0:T(8,128)(2,1)S(1)}, u32[]{:S(2)}, u32[]{:S(2)}) collective-permute-start(bf16[16,4096]{1,0:T(8,128)(2,1)S(1)} %get-tuple-element.25.refs_6_), channel_id=1, source_target_pairs={{2,0},{3,1},{0,2},{1,3},{6,4},{7,5},{4,6},{5,7},{10,8},{11,9},{8,1... | collective-permute-start | bytes 393224 | tf_op jit(solution)/shard_map/ppermute | solution.py:17
  8.2 10.5 %collective-permute-start.2 = (bf16[16,4096]{1,0:T(8,128)(2,1)S(1)}, bf16[16,4096]{1,0:T(8,128)(2,1)S(1)}, u32[]{:S(2)}, u32[]{:S(2)}) collective-permute-start(bf16[16,4096]{1,0:T(8,128)(2,1)S(1)} %get-tuple-element.28), channel_id=1, source_target_pairs={{8,0},{12,4},{0,8},{4,12},{9,1},{13,5},{1,9},{5,13},{10,2},{14,6},... | collective-permute-start | bytes 393224 | tf_op jit(solution)/shard_map/ppermute | solution.py:17
  11.1 8.8 %collective-permute-start.4 = (bf16[16,4096]{1,0:T(8,128)(2,1)S(1)}, bf16[16,4096]{1,0:T(8,128)(2,1)S(1)}, u32[]{:S(2)}, u32[]{:S(2)}) collective-permute-start(bf16[16,4096]{1,0:T(8,128)(2,1)S(1)} %collective-permute-done.3.refs_2_), channel_id=1, source_target_pairs={{2,0},{3,1},{0,2},{1,3},{6,4},{7,5},{4,6},{5,7},{10,8},{11,9},{8,1... | collective-permute-start | bytes 393224 | tf_op jit(solution)/shard_map/ppermute | solution.py:17
  14.7 8.5 %collective-permute-start.7 = (bf16[16,4096]{1,0:T(8,128)(2,1)S(1)}, bf16[16,4096]{1,0:T(8,128)(2,1)S(1)}, u32[]{:S(2)}, u32[]{:S(2)}) collective-permute-start(bf16[16,4096]{1,0:T(8,128)(2,1)S(1)} %collective-permute-done.6.refs_4_), channel_id=1, source_target_pairs={{2,0},{3,1},{0,2},{1,3},{6,4},{7,5},{4,6},{5,7},{10,8},{11,9},{8,1... | collective-permute-start | bytes 393224 | tf_op jit(solution)/shard_map/ppermute | solution.py:17
  18.6 5.2 %collective-permute-start.5 = (bf16[16,4096]{1,0:T(8,128)(2,1)S(1)}, bf16[16,4096]{1,0:T(8,128)(2,1)S(1)}, u32[]{:S(2)}, u32[]{:S(2)}) collective-permute-start(bf16[16,4096]{1,0:T(8,128)(2,1)S(1)} %collective-permute-done.2.refs_2_), channel_id=1, source_target_pairs={{2,0},{3,1},{0,2},{1,3},{6,4},{7,5},{4,6},{5,7},{10,8},{11,9},{8,1... | collective-permute-start | bytes 393224 | tf_op jit(solution)/shard_map/ppermute | solution.py:17
  22.3 5.0 %collective-permute-start.8 = (bf16[16,4096]{1,0:T(8,128)(2,1)S(1)}, bf16[16,4096]{1,0:T(8,128)(2,1)S(1)}, u32[]{:S(2)}, u32[]{:S(2)}) collective-permute-start(bf16[16,4096]{1,0:T(8,128)(2,1)S(1)} %get-tuple-element.36), channel_id=1, source_target_pairs={{2,0},{3,1},{0,2},{1,3},{6,4},{7,5},{4,6},{5,7},{10,8},{11,9},{8,1... | collective-permute-start | bytes 393224 | tf_op jit(solution)/shard_map/ppermute | solution.py:17
  27.3 6.7 %collective-permute-start.14 = (bf16[16,4096]{1,0:T(8,128)(2,1)S(1)}, bf16[16,4096]{1,0:T(8,128)(2,1)S(1)}, u32[]{:S(2)}, u32[]{:S(2)}) collective-permute-start(bf16[16,4096]{1,0:T(8,128)(2,1)S(1)} %get-tuple-element.44), channel_id=1, source_target_pairs={{4,0},{0,4},{12,8},{8,12},{5,1},{1,5},{13,9},{9,13},{6,2},{2,6},{1... | collective-permute-start | bytes 393224 | tf_op jit(solution)/shard_map/ppermute | solution.py:17
  28.0 7.3 %collective-permute-start.9 = (bf16[16,4096]{1,0:T(8,128)(2,1)S(1)}, bf16[16,4096]{1,0:T(8,128)(2,1)S(1)}, u32[]{:S(2)}, u32[]{:S(2)}) collective-permute-start(bf16[16,4096]{1,0:T(8,128)(2,1)S(1)} %get-tuple-element.37), channel_id=1, source_target_pairs={{2,0},{3,1},{0,2},{1,3},{6,4},{7,5},{4,6},{5,7},{10,8},{11,9},{8,1... | collective-permute-start | bytes 393224 | tf_op jit(solution)/shard_map/ppermute | solution.py:17
  29.3 8.4 %collective-permute-start.11 = (bf16[16,4096]{1,0:T(8,128)(2,1)S(1)}, bf16[16,4096]{1,0:T(8,128)(2,1)S(1)}, u32[]{:S(2)}, u32[]{:S(2)}) collective-permute-start(bf16[16,4096]{1,0:T(8,128)(2,1)S(1)} %add_convert_fusion), channel_id=1, source_target_pairs={{12,0},{8,4},{4,8},{0,12},{13,1},{9,5},{5,9},{1,13},{14,2},{10,6},... | collective-permute-start | bytes 393224 | tf_op jit(solution)/shard_map/ppermute | solution.py:17
  31.5 6.2 %collective-permute-start.13 = (bf16[16,4096]{1,0:T(8,128)(2,1)S(1)}, bf16[16,4096]{1,0:T(8,128)(2,1)S(1)}, u32[]{:S(2)}, u32[]{:S(2)}) collective-permute-start(bf16[16,4096]{1,0:T(8,128)(2,1)S(1)} %get-tuple-element.42), channel_id=1, source_target_pairs={{2,0},{3,1},{0,2},{1,3},{6,4},{7,5},{4,6},{5,7},{10,8},{11,9},{8,1... | collective-permute-start | bytes 393224 | tf_op jit(solution)/shard_map/ppermute | solution.py:17
  31.9 7.1 %collective-permute-start.12 = (bf16[16,4096]{1,0:T(8,128)(2,1)S(1)}, bf16[16,4096]{1,0:T(8,128)(2,1)S(1)}, u32[]{:S(2)}, u32[]{:S(2)}) collective-permute-start(bf16[16,4096]{1,0:T(8,128)(2,1)S(1)} %get-tuple-element.40), channel_id=1, source_target_pairs={{4,0},{0,4},{12,8},{8,12},{5,1},{1,5},{13,9},{9,13},{6,2},{2,6},{1... | collective-permute-start | bytes 393224 | tf_op jit(solution)/shard_map/ppermute | solution.py:17
  34.0 5.0 %collective-permute-start.15 = (bf16[16,4096]{1,0:T(8,128)(2,1)S(1)}, bf16[16,4096]{1,0:T(8,128)(2,1)S(1)}, u32[]{:S(2)}, u32[]{:S(2)}) collective-permute-start(bf16[16,4096]{1,0:T(8,128)(2,1)S(1)} %collective-permute-done.14), channel_id=1, source_target_pairs={{2,0},{3,1},{0,2},{1,3},{6,4},{7,5},{4,6},{5,7},{10,8},{11,9},{8,1... | collective-permute-start | bytes 393224 | tf_op jit(solution)/shard_map/ppermute | solution.py:17
  35.3 5.9 %collective-permute-start.10 = (bf16[16,4096]{1,0:T(8,128)(2,1)S(1)}, bf16[16,4096]{1,0:T(8,128)(2,1)S(1)}, u32[]{:S(2)}, u32[]{:S(2)}) collective-permute-start(bf16[16,4096]{1,0:T(8,128)(2,1)S(1)} %add_convert_fusion.1), channel_id=1, source_target_pairs={{8,0},{12,4},{0,8},{4,12},{9,1},{13,5},{1,9},{5,13},{10,2},{14,6},... | collective-permute-start | bytes 393224 | tf_op jit(solution)/shard_map/ppermute | solution.py:17
